TPU v7x, 32 devices: a whole 2x2x4 slice. The times are simulated.
32 devices in a mesh: seq: 32 (over z, y, x, core).
Axes of the slice: x: 2, y: 2, z: 4, core: 2. Of those that a mesh axis runs over, the one named last changes fastest.
Arguments:
- block_input: float32 [4096, 2048], P('seq'), may hold values from -6 to 6
- start_flags: int32 [4096], P('seq'), may hold values from 0 to 1, as said below
- norm_gain: bfloat16 [2048], replicated, may hold values from 0.5 to 1.5
- gate_weight: bfloat16 [2048, 2730], P('seq'), may hold values from -0.125 to 0.125
- linear_weight: bfloat16 [2048, 2730], P('seq'), may hold values from -0.125 to 0.125
- conv_taps: bfloat16 [4, 2730], replicated, may hold values from -3 to 3
- conv_bias: bfloat16 [2730], replicated, may hold values from -2 to 2
- reset_weight: bfloat16 [10, 273, 273], replicated, may hold values from -0.375 to 0.375
- reset_bias: bfloat16 [2730], replicated, may hold values from -3 to 3
- input_weight: bfloat16 [10, 273, 273], replicated, may hold values from -0.375 to 0.375
- input_bias: bfloat16 [2730], replicated, may hold values from -3 to 3
- decay_param: bfloat16 [2730], replicated, may hold values from 6 to 14
- out_weight: bfloat16 [2048, 2730], P('seq'), may hold values from -0.109375 to 0.109375
- feed_norm_gain: bfloat16 [2048], replicated, may hold values from 0.5 to 1.5
- feed_gate_weight: bfloat16 [2048, 6144], P('seq'), may hold values from -0.125 to 0.125
- feed_value_weight: bfloat16 [2048, 6144], P('seq'), may hold values from -0.125 to 0.125
- feed_down_weight: bfloat16 [2048, 6144], P('seq'), may hold values from -0.078125 to 0.078125
- output_grad: float32 [4096, 2048], P('seq'), may hold values from -6 to 6
Outputs:
- block_output: float32 [4096, 2048], P('seq')
- input_grad: float32 [4096, 2048], P('seq')
- grad_norm_gain: float32 [2048], replicated
- grad_gate_weight: float32 [2048, 2730], P('seq')
- grad_linear_weight: float32 [2048, 2730], P('seq')
- grad_conv_taps: float32 [4, 2730], replicated
- grad_conv_bias: float32 [2730], replicated
- grad_reset_weight: float32 [10, 273, 273], replicated
- grad_reset_bias: float32 [2730], replicated
- grad_input_weight: float32 [10, 273, 273], replicated
- grad_input_bias: float32 [2730], replicated
- grad_decay_param: float32 [2730], replicated
- grad_out_weight: float32 [2048, 2730], P('seq')
- grad_feed_norm_gain: float32 [2048], replicated
- grad_feed_gate_weight: float32 [2048, 6144], P('seq')
- grad_feed_value_weight: float32 [2048, 6144], P('seq')
- grad_feed_down_weight: float32 [2048, 6144], P('seq')
Inputs may be any that keep to these rules, and one draw needn't show every extreme that they name: start_flags is 1 at token 0. The stream is a packing of 2 rows of 2048 tokens each. Each row begins with a 1 and holds at most three documents.
All inputs are finite; a program needn't handle non-finite values.
Results may differ from a plain program's by a relative error of at most 0.008.
The roundings to bfloat16 on the way count: a program that leaves them out, or rounds other values in their place, can miss the bound.
Values may be sent and summed in bfloat16 or wider, within the bound.
No kernel may reach another device: no remote copies, remote signals or barrier semaphores. Data moves between devices by JAX's collectives and lax.ppermute only.
A program may use at most 832 MiB of HBM per device.

v0:
```python
import jax
import jax.numpy as jnp
from jax import lax
from jax.sharding import PartitionSpec as P

ROOT_GUARD = 0.001
CONTRACT_LAST = (((1,), (1,)), ((), ()))
CONTRACT_FIRST = (((0,), (0,)), ((), ()))


def shifted(block, axis, distance):
    devices = range(lax.axis_size(axis))
    route = [(i - distance, i) for i in devices if i - distance in devices]
    return lax.ppermute(block, axis, route)


def carried_in(part, axis, combine, identity, reverse):
    count = lax.axis_size(axis)
    place = lax.axis_index(axis)
    ahead = count - 1 - place if reverse else place
    gathered = jax.tree.map(lambda a: lax.all_gather(a, axis), part)
    state = jax.tree.map(lambda a, e: jnp.zeros_like(a) + jnp.asarray(e, a.dtype), part, identity)

    def one(hop, state):
        source = count - 1 - hop if reverse else hop
        return combine(
            state, jax.tree.map(lambda a: lax.dynamic_index_in_dim(a, source, 0, False), gathered)
        )

    return lax.fori_loop(0, ahead, one, state)


def rms_scale(values):
    return lax.rsqrt(jnp.mean(values * values, axis=-1, keepdims=True) + 1e-06)


def matmul(left_side, right_side):
    return jnp.dot(left_side, right_side, preferred_element_type=jnp.float32)


def matmul_last(left_side, right_side):
    return lax.dot_general(left_side, right_side, CONTRACT_LAST, preferred_element_type=jnp.float32)


def matmul_first(left_side, right_side):
    return lax.dot_general(
        left_side, right_side, CONTRACT_FIRST, preferred_element_type=jnp.float32
    )


def chain_link(earlier_part, later_part):
    return (earlier_part[0] * later_part[0], later_part[0] * earlier_part[1] + later_part[1])


def norm_back(grad_normed, values, scale, gain):
    scaled = grad_normed * gain
    return scale * scaled - values * (scale * scale * scale) * jnp.mean(
        scaled * values, axis=-1, keepdims=True
    )


def body(
    block_input,
    start_flags,
    norm_gain,
    gate_weight,
    linear_weight,
    conv_taps,
    conv_bias,
    reset_weight,
    reset_bias,
    input_weight,
    input_bias,
    decay_param,
    out_weight,
    feed_norm_gain,
    feed_gate_weight,
    feed_value_weight,
    feed_down_weight,
    output_grad,
):
    tokens_here = block_input.shape[0]
    heads_count = reset_weight.shape[0]
    block_size = reset_weight.shape[1]
    rec_width = gate_weight.shape[1]
    feed_width = feed_gate_weight.shape[1]
    gain_one = norm_gain.astype(jnp.float32)
    gain_two = feed_norm_gain.astype(jnp.float32)
    taps_float = conv_taps.astype(jnp.float32)
    decay_float = decay_param.astype(jnp.float32)
    mixer_full = (
        lax.all_gather(gate_weight, "seq", axis=0, tiled=True),
        lax.all_gather(linear_weight, "seq", axis=0, tiled=True),
        lax.all_gather(out_weight, "seq", axis=0, tiled=True),
    )
    feed_full = (
        lax.all_gather(feed_gate_weight, "seq", axis=0, tiled=True),
        lax.all_gather(feed_value_weight, "seq", axis=0, tiled=True),
        lax.all_gather(feed_down_weight, "seq", axis=0, tiled=True),
    )
    scale_one = rms_scale(block_input)
    normed = (block_input * scale_one * gain_one).astype(jnp.bfloat16)
    gate_pre = matmul(normed, mixer_full[0])
    linear = matmul(normed, mixer_full[1])
    starts = start_flags.astype(jnp.float32)[:, None]
    keep_mask = 1.0 - starts
    counted = jnp.cumsum(start_flags)
    after_end = counted[-1] - counted[-3:]
    tail_rows = linear[-3:] * (after_end == 0).astype(jnp.float32)[:, None]
    halo_rows = shifted(tail_rows, "seq", 1)
    extended = jnp.concatenate([halo_rows, linear], axis=0)
    counted_ext = jnp.concatenate([jnp.zeros((3,), counted.dtype), counted])
    conv_sum = linear * taps_float[0] + conv_bias.astype(jnp.float32)
    same_masks = []
    for shift_by in range(1, 4):
        same_doc = (
            counted_ext[3:] - counted_ext[3 - shift_by : 3 - shift_by + tokens_here] == 0
        ).astype(jnp.float32)[:, None]
        same_masks.append(same_doc)
        conv_sum = (
            conv_sum
            + extended[3 - shift_by : 3 - shift_by + tokens_here] * taps_float[shift_by] * same_doc
        )
    conv_low = conv_sum.astype(jnp.bfloat16)
    conv_value = conv_low.astype(jnp.float32)
    conv_blocks = conv_low.reshape(tokens_here, heads_count, block_size)
    reset_pre = jnp.einsum(
        "thi,hij->thj", conv_blocks, reset_weight, preferred_element_type=jnp.float32
    ).reshape(tokens_here, rec_width) + reset_bias.astype(jnp.float32)
    input_pre = jnp.einsum(
        "thi,hij->thj", conv_blocks, input_weight, preferred_element_type=jnp.float32
    ).reshape(tokens_here, rec_width) + input_bias.astype(jnp.float32)
    reset_gate = jax.nn.sigmoid(reset_pre)
    input_gate = jax.nn.sigmoid(input_pre)
    soft_rate = jax.nn.softplus(-decay_float)
    decay_rate = jnp.exp(-8.0 * reset_gate * soft_rate) * keep_mask
    root_term = jnp.sqrt(1.0 - decay_rate * decay_rate + ROOT_GUARD)
    multiplier = keep_mask * root_term + starts
    driven = multiplier * input_gate * conv_value
    decay_acc, local_states = lax.associative_scan(chain_link, (decay_rate, driven), axis=0)
    decay_total = decay_acc[-1]
    identity = (jnp.ones_like(decay_total), jnp.zeros_like(decay_total))
    incoming = carried_in((decay_total, local_states[-1]), "seq", chain_link, identity, False)[1]
    states = local_states + decay_acc * incoming
    gate_act, gate_pull = jax.vjp(jax.nn.gelu, gate_pre)
    mixed = (states * gate_act).astype(jnp.bfloat16)
    middle = block_input + matmul_last(mixed, mixer_full[2])
    scale_two = rms_scale(middle)
    normed_two = (middle * scale_two * gain_two).astype(jnp.bfloat16)
    inner_gate = matmul(normed_two, feed_full[0])
    inner_value = matmul(normed_two, feed_full[1])
    gelu_gate, feed_pull = jax.vjp(jax.nn.gelu, inner_gate)
    hidden = (gelu_gate * inner_value).astype(jnp.bfloat16)
    block_output = middle + matmul_last(hidden, feed_full[2])
    feed_back = (
        lax.all_gather(feed_gate_weight, "seq", axis=0, tiled=True),
        lax.all_gather(feed_value_weight, "seq", axis=0, tiled=True),
        lax.all_gather(feed_down_weight, "seq", axis=0, tiled=True),
    )
    grad_top = output_grad.astype(jnp.bfloat16)
    grad_hidden = matmul(grad_top, feed_back[2])
    grad_inner_gate = feed_pull(grad_hidden * inner_value)[0].astype(jnp.bfloat16)
    grad_inner_value = (grad_hidden * gelu_gate).astype(jnp.bfloat16)
    grad_normed_two = matmul_last(grad_inner_gate, feed_back[0]) + matmul_last(
        grad_inner_value, feed_back[1]
    )
    grad_gain_two = jnp.sum(grad_normed_two * middle * scale_two, axis=0)
    grad_middle = output_grad + norm_back(grad_normed_two, middle, scale_two, gain_two)
    grad_branch = grad_middle.astype(jnp.bfloat16)
    normed_part = normed_two
    feed_grads = lax.psum_scatter(
        jnp.concatenate(
            [
                matmul_first(normed_part, grad_inner_gate),
                matmul_first(normed_part, grad_inner_value),
                matmul_first(grad_top, hidden),
            ],
            axis=1,
        ),
        "seq",
        scatter_dimension=0,
        tiled=True,
    )
    mixer_back = (
        lax.all_gather(gate_weight, "seq", axis=0, tiled=True),
        lax.all_gather(linear_weight, "seq", axis=0, tiled=True),
        lax.all_gather(out_weight, "seq", axis=0, tiled=True),
    )
    grad_mixed = matmul(grad_branch, mixer_back[2])
    grad_state_in = grad_mixed * gate_act
    grad_gate_pre = gate_pull(grad_mixed * states)[0].astype(jnp.bfloat16)
    next_decay = jnp.concatenate([decay_rate[1:], jnp.ones((1, rec_width), jnp.float32)], axis=0)
    suffix_decay, local_grads = lax.associative_scan(
        chain_link, (next_decay, grad_state_in), reverse=True, axis=0
    )
    head_term = decay_rate[0] * local_grads[0]
    from_right = carried_in((decay_total, head_term), "seq", chain_link, identity, True)[1]
    grad_states = local_grads + suffix_decay * from_right
    prior_states = jnp.concatenate([incoming[None], states[:-1]], axis=0)
    grad_log = decay_rate * (
        grad_states * prior_states - grad_states * input_gate * conv_value * decay_rate / root_term
    )
    grad_decay = jnp.sum(8.0 * reset_gate * grad_log, axis=0) * jax.nn.sigmoid(-decay_float)
    grad_reset_pre = (-8.0 * soft_rate * grad_log * reset_gate * (1.0 - reset_gate)).astype(
        jnp.bfloat16
    )
    grad_input_pre = (
        grad_states * multiplier * conv_value * input_gate * (1.0 - input_gate)
    ).astype(jnp.bfloat16)
    reset_blocks = grad_reset_pre.reshape(tokens_here, heads_count, block_size)
    input_blocks = grad_input_pre.reshape(tokens_here, heads_count, block_size)
    grad_reset_w = jnp.einsum(
        "thi,thj->hij", conv_blocks, reset_blocks, preferred_element_type=jnp.float32
    )
    grad_input_w = jnp.einsum(
        "thi,thj->hij", conv_blocks, input_blocks, preferred_element_type=jnp.float32
    )
    grad_reset_b = jnp.sum(grad_reset_pre.astype(jnp.float32), axis=0)
    grad_input_b = jnp.sum(grad_input_pre.astype(jnp.float32), axis=0)
    grad_conv = grad_states * multiplier * input_gate
    grad_conv = grad_conv + jnp.einsum(
        "thj,hij->thi", reset_blocks, reset_weight, preferred_element_type=jnp.float32
    ).reshape(tokens_here, rec_width)
    grad_conv = grad_conv + jnp.einsum(
        "thj,hij->thi", input_blocks, input_weight, preferred_element_type=jnp.float32
    ).reshape(tokens_here, rec_width)
    grad_bias_conv = jnp.sum(grad_conv, axis=0)
    tap_terms = [jnp.sum(grad_conv * linear, axis=0)]
    for shift_by in range(1, 4):
        tap_terms.append(
            jnp.sum(
                grad_conv
                * extended[3 - shift_by : 3 - shift_by + tokens_here]
                * same_masks[shift_by - 1],
                axis=0,
            )
        )
    grad_taps = jnp.stack(tap_terms, axis=0)
    head_rows = grad_conv[:3] * (counted[:3] == 0).astype(jnp.float32)[:, None]
    rows_from_right = shifted(head_rows, "seq", -1)
    grad_ext = jnp.concatenate([grad_conv, rows_from_right], axis=0)
    counted_tail = jnp.concatenate([counted, jnp.broadcast_to(counted[-1], (3,))])
    grad_linear = grad_conv * taps_float[0]
    for shift_by in range(1, 4):
        same_after = (counted_tail[shift_by : shift_by + tokens_here] - counted == 0).astype(
            jnp.float32
        )[:, None]
        grad_linear = (
            grad_linear
            + grad_ext[shift_by : shift_by + tokens_here] * taps_float[shift_by] * same_after
        )
    grad_linear_low = grad_linear.astype(jnp.bfloat16)
    grad_normed = matmul_last(grad_gate_pre, mixer_back[0]) + matmul_last(
        grad_linear_low, mixer_back[1]
    )
    grad_gain_one = jnp.sum(grad_normed * block_input * scale_one, axis=0)
    input_grad = grad_middle + norm_back(grad_normed, block_input, scale_one, gain_one)
    normed_part = normed
    mixer_grads = lax.psum_scatter(
        jnp.concatenate(
            [
                matmul_first(normed_part, grad_gate_pre),
                matmul_first(normed_part, grad_linear_low),
                matmul_first(grad_branch, mixed),
            ],
            axis=1,
        ),
        "seq",
        scatter_dimension=0,
        tiled=True,
    )
    small_sums = lax.psum(
        (
            grad_gain_one,
            grad_taps,
            grad_bias_conv,
            grad_reset_w,
            grad_reset_b,
            grad_input_w,
            grad_input_b,
            grad_decay,
            grad_gain_two,
        ),
        "seq",
    )
    return (
        block_output,
        input_grad,
        small_sums[0],
        mixer_grads[:, :rec_width],
        mixer_grads[:, rec_width : 2 * rec_width],
        small_sums[1],
        small_sums[2],
        small_sums[3],
        small_sums[4],
        small_sums[5],
        small_sums[6],
        small_sums[7],
        mixer_grads[:, 2 * rec_width :],
        small_sums[8],
        feed_grads[:, :feed_width],
        feed_grads[:, feed_width : 2 * feed_width],
        feed_grads[:, 2 * feed_width :],
    )


def solution(mesh):
    in_specs = (
        P("seq", None),
        P("seq"),
        P(),
        P("seq", None),
        P("seq", None),
        P(),
        P(),
        P(),
        P(),
        P(),
        P(),
        P(),
        P("seq", None),
        P(),
        P("seq", None),
        P("seq", None),
        P("seq", None),
        P("seq", None),
    )
    out_specs = (
        P("seq", None),
        P("seq", None),
        P(),
        P("seq", None),
        P("seq", None),
        P(),
        P(),
        P(),
        P(),
        P(),
        P(),
        P(),
        P("seq", None),
        P(),
        P("seq", None),
        P("seq", None),
        P("seq", None),
    )
    return jax.shard_map(body, mesh=mesh, in_specs=in_specs, out_specs=out_specs, check_vma=False)
```

profile of v0, /device:TPU:0, one launch (start us, length us, event | category | flops | bytes accessed | tf_op | source)
XLA Modules:
  0.0 3627.2 jit_solution(9994218633629376511)
XLA Ops:
  16.6 88.2 %all-gather.10.cloned.1.call-done = bf16[2048,2730]{1,0:T(8,128)(2,1)} async-done(((bf16[64,2730]{1,0:T(8,128)(2,1)}), bf16[2048,2730]{1,0:T(8,128)(2,1)}) %all-gather.10.cloned.1.call-update) | async-done | bytes 11182096 | tf_op jit(solution)/shard_map/all_gather | solution.py:93
  104.8 6.1 fusion.94
  115.2 4.0 add_convert_fusion
  130.0 3.7 convolution_bitcast_fusion.4
  139.1 4.3 convert_multiply_fusion.2
  144.6 3.5 slice.590
  148.1 3.4 slice.544
  151.5 3.4 slice.543
  156.3 3.5 slice.546
  159.8 3.4 slice.542
  179.9 3.5 slice.541
  186.1 3.4 slice.617
  189.5 3.4 slice.610
  192.9 3.4 slice.608
  217.9 5.0 pad.203
  229.0 5.0 pad.202
  234.9 44.7 %all-gather = f32[32,1,2730]{2,1,0:T(1,128)S(1)} all-gather(f32[1,1,2730]{2,1,0:T(1,128)S(1)} %add_bitcast_fusion.1), channel_id=1, replica_groups=mesh['seq'=32] {'seq'}, dimensions={0}, use_global_device_ids=true | all-gather | bytes 360360 | tf_op jit(solution)/shard_map/all_gather | solution.py:21
  287.7 38.8 %all-gather.1 = f32[32,1,2730]{2,1,0:T(1,128)S(1)} all-gather(f32[1,1,2730]{2,1,0:T(1,128)S(1)} %add_bitcast_fusion), channel_id=1, replica_groups=mesh['seq'=32] {'seq'}, dimensions={0}, use_global_device_ids=true | all-gather | bytes 360360 | tf_op jit(solution)/shard_map/all_gather | solution.py:21
  327.4 11.1 slice.618
  338.5 11.1 slice.609
  349.6 6.9 slice.611
  356.5 10.0 multiply_convert_fusion.3
  366.5 8.6 multiply_reduce_fusion.9
  376.2 72.8 %all-gather.18.cloned.1.call-done = bf16[2048,6144]{1,0:T(8,128)(2,1)} async-done(((bf16[64,6144]{1,0:T(8,128)(2,1)}), bf16[2048,6144]{1,0:T(8,128)(2,1)}) %all-gather.18.cloned.1.call-update) | async-done | bytes 25165840 | tf_op jit(solution)/shard_map/all_gather | solution.py:98
  449.0 13.4 fusion.96
  462.4 142.1 %all-gather.16.cloned.1.call-done = bf16[2048,6144]{1,0:T(8,128)(2,1)} async-done(((bf16[64,6144]{1,0:T(8,128)(2,1)}), bf16[2048,6144]{1,0:T(8,128)(2,1)}) %all-gather.16.cloned.1.call-update) | async-done | bytes 25165840 | tf_op jit(solution)/shard_map/all_gather | solution.py:97
  604.5 13.4 fusion.95
  618.0 142.1 %all-gather.20.cloned.1.call-done = bf16[2048,6144]{1,0:T(8,128)(2,1)} async-done(((bf16[64,6144]{1,0:T(8,128)(2,1)}), bf16[2048,6144]{1,0:T(8,128)(2,1)}) %all-gather.20.cloned.1.call-update) | async-done | bytes 25165840 | tf_op jit(solution)/shard_map/all_gather | solution.py:99
  760.1 15.0 multiply_convert_fusion
  775.1 14.3 fusion.97
  789.4 15.3 multiply_reduce_fusion.5
  807.2 7.6 fusion.38
  816.5 3.4 slice.662
  822.1 3.4 slice.612
  825.5 11.0 slice.613
  836.5 7.0 slice.615
  866.9 6.9 slice.663
  899.3 5.0 pad.216
  911.4 9.1 fusion.41
  921.4 11.8 rev.8
  933.2 39.5 %all-gather.2 = f32[32,1,2730]{2,1,0:T(1,128)S(1)} all-gather(f32[1,1,2730]{2,1,0:T(1,128)S(1)} %fusion.72), channel_id=1, replica_groups=mesh['seq'=32] {'seq'}, dimensions={0}, use_global_device_ids=true | all-gather | bytes 360360 | tf_op jit(solution)/shard_map/all_gather | solution.py:21
  972.8 31.0 while.27
  1003.9 5.4 pad.230
  1015.3 12.0 rev.9
  1027.3 6.3 multiply_reduce_fusion
  1056.1 5.7 multiply_reduce_fusion.3
  1063.2 9.2 fusion.99
  1073.4 9.1 fusion.100
  1082.5 161.7 %concatenate.126 = f32[2048,8190]{0,1:T(8,128)} concatenate(f32[2048,2730]{0,1:T(8,128)} %fusion.99, f32[2048,2730]{0,1:T(8,128)} %fusion.100, f32[2048,2730]{0,1:T(8,128)} %fusion.41), dimensions={1} | concatenate | bytes 134184960 | tf_op jit(solution)/shard_map/concatenate | solution.py:260
  1244.1 61.2 %copy.231 = f32[2048,8190]{1,0:T(8,128)} copy(f32[2048,8190]{0,1:T(8,128)} %concatenate.126) | data formatting | bytes 134184960
  1307.0 20.2 fusion.104
  1327.2 21.4 fusion.103
  1348.6 19.9 convolution_bitcast_fusion
  1368.5 98.8 %pad_maximum_fusion = f32[2048,18432]{1,0:T(8,128)} fusion(f32[2048,6144]{1,0:T(8,128)} %convolution_bitcast_fusion, f32[2048,6144]{1,0:T(8,128)} %fusion.104, f32[2048,6144]{1,0:T(8,128)} %fusion.103), kind=kLoop, calls=%fused_computation.6 | loop fusion | flops 75497472 | bytes 301989888 | tf_op jit(solution)/shard_map/concatenate | solution.py:172
  1472.3 9.3 fusion.98
  1481.7 6.8 multiply_reduce_fusion.6
  1492.8 14.5 convolution_add_fusion.1
  1509.9 495.6 %reduce-scatter.7.cloned.1.call-done = f32[64,8190]{1,0:T(8,128)} async-done(((f32[2048,8190]{1,0:T(8,128)}), f32[64,8190]{1,0:T(8,128)}) %reduce-scatter.7.cloned.1.call-update) | async-done | bytes 2096656
  2005.5 3.3 fusion.84
  2008.8 1275.9 %reduce-scatter.5.cloned.1.call-done = f32[64,18432]{1,0:T(8,128)} async-done(((f32[2048,18432]{1,0:T(8,128)}), f32[64,18432]{1,0:T(8,128)}) %reduce-scatter.5.cloned.1.call-update) | async-done | bytes 4718608 | tf_op jit(solution)/shard_map/reduce_scatter | solution.py:171
  3284.7 4.6 fusion.83
  3289.3 126.9 %all-reduce.65.cloned.1.call-done = (f32[2048]{0:T(1024)}, f32[4,2730]{1,0:T(4,128)}, f32[2730]{0:T(1024)}, f32[2730]{0:T(1024)}, f32[2730]{0:T(1024)}, /*index=5*/f32[2730]{0:T(1024)}, f32[2048]{0:T(1024)}) async-done(((f32[2048]{0:T(1024)}, f32[4,2730]{1,0:T(4,128)}, f32[2730]{0:T(1024)}, f32[2730]{0:T(1024)}, f32[2730]{0:T(1024)}, /*index=5*/f32[2730]{0:T(1024)}, f32[2048]{0:T(1024)}), (f32[2048]{0:T(1024)}, ...) | async-done | bytes 103760 | tf_op jit(solution)/shard_map/psum | solution.py:272
  3416.3 190.5 %all-reduce.67.cloned.1.call-done = (f32[10,273,273]{2,1,0:T(8,128)}, f32[10,273,273]{2,1,0:T(8,128)}) async-done(((f32[10,273,273]{2,1,0:T(8,128)}, f32[10,273,273]{2,1,0:T(8,128)}), (f32[10,273,273]{2,1,0:T(8,128)}, f32[10,273,273]{2,1,0:T(8,128)})) %all-reduce.67.cloned.1.call-update) | async-done | bytes 5962336 | tf_op jit(solution)/shard_map/psum | solution.py:272
  3610.9 4.6 copy.317
  (609 shorter events, 235.4 us)
Async XLA Ops:
  7.2 115.3 %copy-start = (bf16[10,273,273]{2,1,0:T(8,128)(2,1)S(1)}, bf16[10,273,273]{2,1,0:T(8,128)(2,1)}, u32[]{:S(2)}) copy-start(bf16[10,273,273]{2,1,0:T(8,128)(2,1)} %param.31) | copy-start | bytes 4471744
  7.2 97.6 %all-gather.10.cloned.1.call-start = ((), (), s32[]{:S(2)}) async-start(), calls=%async_computation.2 | async-start | bytes 11894784 | tf_op jit(solution)/shard_map/all_gather | solution.py:93
  7.9 348.6 %all-gather.12.cloned.1.call-start = ((), (), s32[]{:S(2)}) async-start(), calls=%async_computation.3 | async-start | bytes 11894784 | tf_op jit(solution)/shard_map/all_gather | solution.py:92
  8.7 357.8 %all-gather.14.cloned.1.call-start = ((), (), s32[]{:S(2)}) async-start(), calls=%async_computation.4 | async-start | bytes 11894784 | tf_op jit(solution)/shard_map/all_gather | solution.py:94
  9.5 439.5 %all-gather.18.cloned.1.call-start = ((), (), s32[]{:S(2)}) async-start(), calls=%async_computation.6 | async-start | bytes 25952256 | tf_op jit(solution)/shard_map/all_gather | solution.py:98
  10.1 594.5 %all-gather.16.cloned.1.call-start = ((), (), s32[]{:S(2)}) async-start(), calls=%async_computation.5 | async-start | bytes 25952256 | tf_op jit(solution)/shard_map/all_gather | solution.py:97
  10.6 749.5 %all-gather.20.cloned.1.call-start = ((), (), s32[]{:S(2)}) async-start(), calls=%async_computation.7 | async-start | bytes 25952256 | tf_op jit(solution)/shard_map/all_gather | solution.py:99
  11.2 1994.3 %reduce-scatter.7.cloned.1.call-start = ((), (), s32[]{:S(2)}) async-start(), calls=%async_computation.9 | async-start | bytes 69206016
  14.3 96.7 %copy-start.106 = (f32[128]{0:T(128)}, f32[128]{0:T(128)S(1)}, u32[]{:S(2)}) copy-start(f32[128]{0:T(128)S(1)} %get-tuple-element.384) | copy-start | bytes 1540
  15.6 99.6 %copy-start.108 = (f32[128]{0:T(128)}, f32[128]{0:T(128)S(1)}, u32[]{:S(2)}) copy-start(f32[128]{0:T(128)S(1)} %get-tuple-element.387) | copy-start | bytes 1540
  15.6 99.6 %copy-start.110 = (f32[128]{0:T(128)}, f32[128]{0:T(128)S(1)}, u32[]{:S(2)}) copy-start(f32[128]{0:T(128)S(1)} %get-tuple-element.388) | copy-start | bytes 1540
  15.6 99.6 %copy-start.112 = (f32[128]{0:T(128)}, f32[128]{0:T(128)S(1)}, u32[]{:S(2)}) copy-start(f32[128]{0:T(128)S(1)} %get-tuple-element.389) | copy-start | bytes 1540
  16.6 98.1 %copy-start.115 = (bf16[2048]{0:T(1024)(128)(2,1)S(1)}, bf16[2048]{0:T(1024)(128)(2,1)}, u32[]{:S(2)}) copy-start(bf16[2048]{0:T(1024)(128)(2,1)} %param.35) | copy-start | bytes 12292
  16.6 98.1 %copy-start.103 = (bf16[2730]{0:T(1024)(128)(2,1)S(1)}, bf16[2730]{0:T(1024)(128)(2,1)}, u32[]{:S(2)}) copy-start(bf16[2730]{0:T(1024)(128)(2,1)} %param.30) | copy-start | bytes 16384
  16.6 98.1 %copy-start.104 = (bf16[2730]{0:T(1024)(128)(2,1)S(1)}, bf16[2730]{0:T(1024)(128)(2,1)}, u32[]{:S(2)}) copy-start(bf16[2730]{0:T(1024)(128)(2,1)} %param.32) | copy-start | bytes 16384
  16.6 98.2 %copy-start.105 = (bf16[2730]{0:T(1024)(128)(2,1)S(1)}, bf16[2730]{0:T(1024)(128)(2,1)}, u32[]{:S(2)}) copy-start(bf16[2730]{0:T(1024)(128)(2,1)} %param.28) | copy-start | bytes 16384
  112.1 3.0 collective-permute-start
  114.6 6.6 copy-start.71
  114.6 6.6 copy-start.73
  114.6 6.6 copy-start.75
  114.6 6.6 copy-start.77
  114.7 24.5 copy-start.116
  114.8 912.5 %copy-start.65 = (f32[2730]{0:T(1024)}, f32[2730]{0:T(1024)S(1)}, u32[]{:S(2)}) copy-start(f32[2730]{0:T(1024)S(1)} %convert_element_type.105) | copy-start | bytes 32764
  115.2 6.0 copy-start.67
  122.5 7.5 copy-start.11
  206.6 7.4 copy-start.59
  229.0 50.6 %copy-start.45 = (f32[64,2730]{1,0:T(8,128)S(1)}, f32[64,2730]{1,0:T(8,128)}, u32[]{:S(2)}) copy-start(f32[64,2730]{1,0:T(8,128)} %add.511) | copy-start | bytes 2096644
  327.4 22.2 copy-start.47
  338.5 18.0 copy-start.9
  375.1 429.6 %copy-start.3 = (f32[128,2048]{1,0:T(8,128)}, f32[128,2048]{1,0:T(8,128)S(1)}, u32[]{:S(2)}) copy-start(f32[128,2048]{1,0:T(8,128)S(1)} %get-tuple-element.395) | copy-start | bytes 3145732
  806.8 8.0 copy-start.19
  866.6 7.5 copy-start.90
  866.7 7.5 copy-start.91
  884.6 6.7 copy-start.60
  911.4 9.1 copy-start.52
  972.8 36.4 %copy-start.44 = (f32[64,2730]{1,0:T(8,128)S(1)}, f32[64,2730]{1,0:T(8,128)}, u32[]{:S(2)}) copy-start(f32[64,2730]{1,0:T(8,128)} %add.556) | copy-start | bytes 2096644
  1015.3 12.0 copy-start.18
  1015.3 12.0 copy-start.117
  1027.3 6.3 copy-start.7
  1056.1 7.1 copy-start.10
  1056.1 7.1 copy-start.53
  1061.9 10.6 collective-permute-start.1
  1063.2 9.3 copy-start.72
  1063.2 9.3 copy-start.74
  1063.2 9.2 copy-start.76
  1063.2 9.2 copy-start.78
  1063.2 9.2 copy-start.118
  1063.2 9.2 copy-start.119
  1063.2 9.2 copy-start.120
  1073.3 9.1 copy-start.32
  1305.4 1979.3 %reduce-scatter.5.cloned.1.call-start = ((), (), s32[]{:S(2)}) async-start(), calls=%async_computation.8 | async-start | bytes 155713536 | tf_op jit(solution)/shard_map/reduce_scatter | solution.py:171
  1327.2 21.4 copy-start.15
  1327.2 21.4 copy-start.40
  1467.3 1948.9 %all-reduce.65.cloned.1.call-start = ((), (), s32[]{:S(2)}) async-start(), calls=%async_computation.10 | async-start | bytes 221184 | tf_op jit(solution)/shard_map/psum | solution.py:272
  1469.4 12.3 copy-start.70
  1469.4 12.3 copy-start.107
  1472.3 9.4 copy-start.2
  1472.3 9.4 copy-start.6
  1472.3 9.4 copy-start.33
  1481.7 6.9 copy-start.35
  1488.5 2118.2 %all-reduce.67.cloned.1.call-start = ((), (), s32[]{:S(2)}) async-start(), calls=%async_computation.11 | async-start | bytes 17203200 | tf_op jit(solution)/shard_map/psum | solution.py:272
  1492.8 14.5 copy-start.21
  1492.8 14.5 copy-start.123
  3608.1 8.1 slice-start
  (74 other events, 170.0 us)
Sparse Core Ops, SparseCore 0:
  10.9 93.8 all-gather.9
  107.7 89.5 all-gather.11
  200.1 92.2 all-gather.13
  295.1 153.8 all-gather.17
  451.7 152.7 all-gather.15
  607.3 152.7 all-gather.19
  1305.5 699.9 reduce-scatter.6
  2011.9 1272.7 reduce-scatter.4
  3293.4 122.8 all-reduce.64
  3423.3 183.3 all-reduce.66
where the time goes:
time: 3640 us; the launch traced here: 3630 us
  waiting for transfers between devices  2540 us (70%)
  local copies, waits for them, and re-layouts  521 us (14%)
  matrix products  240 us (7%)
  other arithmetic  183 us (5%)
  blocking collectives  123 us (3%)
    reduce_scatter x1, waiting for transfers between devices, body(): lax.psum_scatter(jnp.concatenate([matmul_first(normed_part, grad_inner_ga...  1280 us
    unnamed x11, waiting for transfers between devices  499 us
    psum x2, waiting for transfers between devices, body(): lax.psum((grad_gain_one, grad_taps, grad_bias_conv, grad_reset_w, grad_re...  317 us
    concatenate x1, local copies, waits for them, and re-layouts, body(): jnp.concatenate([matmul_first(normed_part, grad_gate_pre), matmul_first(n...  162 us
    all_gather x1, waiting for transfers between devices, body(): lax.all_gather(feed_down_weight, 'seq', axis=0, tiled=True)  142 us
    all_gather x1, waiting for transfers between devices, body(): lax.all_gather(feed_gate_weight, 'seq', axis=0, tiled=True)  142 us
    all_gather x3, blocking collectives, carried_in(): gathered = jax.tree.map(lambda a: lax.all_gather(a, axis), part)  123 us
    concatenate x1, other arithmetic, body(): jnp.concatenate([matmul_first(normed_part, grad_inner_gate), matmul_first...  98.8 us
  transfers between devices with their start and end apart: 12, of which 9 were waited for; matrix products, arithmetic and copies ran while one was open for 12% of the time, Pallas kernels for 0%

commit v1 on v0

v1 whole, which is shorter than its diff:
```python
import functools

import jax
import jax.numpy as jnp
from jax import lax
from jax.experimental import pallas as pl
from jax.experimental.pallas import tpu as pltpu
from jax.sharding import PartitionSpec as P

AXIS = "seq"
ROOT_GUARD = 0.001
SIDE = 8
CORE, XBIT, YBIT, LBIT, HBIT = 1, 2, 4, 8, 16
EXTRA = {0: 8, 6: 9}
F32, BF16 = jnp.float32, jnp.bfloat16


def place_in_side(i):
    return ((i >> 3) & 1) * 4 + (i & 3)


def mask_of(j):
    return (j & 3) | ((j >> 2) & 1) * LBIT


def swap(v, mask, only=None):
    n = lax.axis_size(AXIS)
    pairs = [(i, i ^ mask) for i in range(n) if only is None or place_in_side(i) in only]
    return lax.ppermute(v, AXIS, pairs)


def far_masks():
    n, masks, m = lax.axis_size(AXIS), [], HBIT
    while m < n:
        masks.append(m)
        m *= 2
    return masks + [YBIT]


def side_groups():
    n = lax.axis_size(AXIS)
    return [
        [b | mask_of(j) for j in range(SIDE)] for b in range(n) if b & (CORE | XBIT | LBIT) == 0
    ]


def dot(a, b):
    return lax.dot_general(a, b, (((1,), (0,)), ((), ())), preferred_element_type=F32)


def dot_last(a, b):
    return lax.dot_general(a, b, (((1,), (1,)), ((), ())), preferred_element_type=F32)


def dot_first(a, b):
    return lax.dot_general(a, b, (((0,), (0,)), ((), ())), preferred_element_type=F32)


def gather_side(x):
    half = x.shape[0] // 2
    by_l, by_x = swap(x, LBIT), swap(x, XBIT)
    both = jnp.concatenate([swap(by_l[:half], XBIT), swap(by_x[half:], LBIT)])
    found = []
    for own in (x, by_x, by_l, both):
        found += [own, swap(own, CORE)]
    return found


def scatter_side(blocks):
    rows, width = blocks[0].shape
    sent = swap(jnp.concatenate([b.astype(BF16) for b in blocks[1::2]]), CORE).reshape(
        4, rows, width
    )
    kept = [blocks[2 * i] + sent[i].astype(F32) for i in range(4)]
    half = width // 2
    ka, kb = [k[:, :half] for k in kept], [k[:, half:] for k in kept]

    def pair(first, second, mask):
        got = swap(jnp.concatenate([first, second]).astype(BF16), mask).astype(F32)
        return got[:rows], got[rows:]

    a0, a1 = pair(ka[2], ka[3], LBIT)
    b0, b1 = pair(kb[1], kb[3], XBIT)
    a_last = swap((ka[1] + a1).astype(BF16), XBIT).astype(F32)
    b_last = swap((kb[2] + b1).astype(BF16), LBIT).astype(F32)
    return jnp.concatenate([ka[0] + a0 + a_last, kb[0] + b0 + b_last], axis=1)


def gather_far(x, only=None):
    chunks = [x]
    for m in far_masks():
        chunks += [swap(c, m, only) for c in chunks]
    return chunks


def scatter_far(x, axis, only=None):
    for m in reversed(far_masks()):
        half = x.shape[axis] // 2
        kept = lax.slice_in_dim(x, 0, half, axis=axis)
        sent = lax.slice_in_dim(x, half, 2 * half, axis=axis)
        x = kept + swap(sent.astype(BF16), m, only).astype(F32)
    return x


def flips(v, me, y_axis, h_axis):
    v = jnp.where((me & YBIT) != 0, jnp.flip(v, y_axis), v)
    size, m = v.shape[h_axis], HBIT
    step = 1
    while step < size:
        shape = v.shape
        split = shape[:h_axis] + (size // (2 * step), 2, step) + shape[h_axis + 1 :]
        w = v.reshape(split)
        w = jnp.where((me & m) != 0, jnp.flip(w, h_axis + 1), w)
        v = w.reshape(shape)
        m *= 2
        step *= 2
    return v


def to_near(v, me):
    lead, k = v.shape[:-1], v.ndim - 1
    n, width = lax.axis_size(AXIS), v.shape[-1]
    high = n // 16
    w = v.reshape(lead + (high, 2, 2, width // (high * 4)))
    w = flips(w, me, k + 2, k)
    order = tuple(range(k)) + (k + 2, k, k + 1, k + 3)
    return w.transpose(order).reshape(v.shape)


def from_near(v, me):
    lead, k = v.shape[:-1], v.ndim - 1
    n, width = lax.axis_size(AXIS), v.shape[-1]
    high = n // 16
    w = v.reshape(lead + (2, high, 2, width // (high * 4)))
    w = flips(w, me, k, k + 1)
    order = tuple(range(k)) + (k + 1, k + 2, k, k + 3)
    return w.transpose(order).reshape(v.shape)


def rms_scale(values):
    return lax.rsqrt(jnp.mean(values * values, axis=-1, keepdims=True) + 1e-06)


def norm_back(grad_normed, values, scale, gain):
    scaled = grad_normed * gain
    return scale * scaled - values * (scale * scale * scale) * jnp.mean(
        scaled * values, axis=-1, keepdims=True
    )


def gelu_pair(v):
    k = 0.7978845608028654
    sq = v * v
    th = jnp.tanh(k * v * (1.0 + 0.044715 * sq))
    half = 0.5 * (1.0 + th)
    act = v * half
    slope = half + 0.5 * v * (1.0 - th * th) * (k * (1.0 + 3.0 * 0.044715 * sq))
    return act, slope


NB = 8
UNROLL = 8


def scan_kernel(a_ref, b_ref, p_ref, s_ref):
    bl = a_ref.shape[0] // NB

    def rows(i):
        return pl.ds(i, NB, stride=bl)

    def step(i, c):
        p, s = c
        a, b = a_ref[rows(i), :], b_ref[rows(i), :]
        p, s = p * a, a * s + b
        p_ref[rows(i), :] = p
        s_ref[rows(i), :] = s
        return p, s

    def steps(o, c):
        for k in range(UNROLL):
            c = step(o * UNROLL + k, c)
        return c

    shape = (NB, a_ref.shape[1])
    p, s = lax.fori_loop(0, bl // UNROLL, steps, (jnp.ones(shape, F32), jnp.zeros(shape, F32)))
    half = NB // 2
    for seg in range(2):
        j = seg * half
        cp, cs = p[j : j + 1], s[j : j + 1]
        for j in range(seg * half + 1, seg * half + half):
            sl = pl.ds(j * bl, bl)
            pv = p_ref[sl, :]
            s_ref[sl, :] = s_ref[sl, :] + pv * cs
            p_ref[sl, :] = pv * cp
            cs = s[j : j + 1] + p[j : j + 1] * cs
            cp = p[j : j + 1] * cp


def back_scan_kernel(a_ref, b_ref, q_ref, g_ref):
    bl = a_ref.shape[0] // NB

    def rows(i):
        return pl.ds(i, NB, stride=bl)

    def step(i, c):
        ag, aq = c
        b = b_ref[rows(i), :]
        g, q = b + ag, aq
        g_ref[rows(i), :] = g
        q_ref[rows(i), :] = q
        a = a_ref[rows(i), :]
        return a * g, a * q

    def steps(o, c):
        for k in range(UNROLL):
            c = step(bl - 1 - (o * UNROLL + k), c)
        return c

    shape = (NB, a_ref.shape[1])
    hg, hq = lax.fori_loop(0, bl // UNROLL, steps, (jnp.zeros(shape, F32), jnp.ones(shape, F32)))
    half = NB // 2
    for seg in range(2):
        j = seg * half + half - 1
        u, v = hg[j : j + 1], hq[j : j + 1]
        for j in range(seg * half + half - 2, seg * half - 1, -1):
            sl = pl.ds(j * bl, bl)
            qv = q_ref[sl, :]
            g_ref[sl, :] = g_ref[sl, :] + qv * u
            q_ref[sl, :] = qv * v
            u = hg[j : j + 1] + hq[j : j + 1] * u
            v = hq[j : j + 1] * v


def run_scan(kernel, a, b):
    rows, width = a.shape
    spec = pl.BlockSpec((rows, 128), lambda j: (0, j))
    return pl.pallas_call(
        kernel,
        grid=(pl.cdiv(width, 128),),
        in_specs=[spec, spec],
        out_specs=[spec, spec],
        out_shape=[jax.ShapeDtypeStruct((rows, width), F32)] * 2,
        compiler_params=pltpu.CompilerParams(vmem_limit_bytes=32 * 1024 * 1024),
    )(a, b)


def body(
    block_input,
    start_flags,
    norm_gain,
    gate_weight,
    linear_weight,
    conv_taps,
    conv_bias,
    reset_weight,
    reset_bias,
    input_weight,
    input_bias,
    decay_param,
    out_weight,
    feed_norm_gain,
    feed_gate_weight,
    feed_value_weight,
    feed_down_weight,
    output_grad,
):
    n = lax.axis_size(AXIS)
    me = lax.axis_index(AXIS)
    here = ((me >> 3) & 1) * 4 + (me & 3)
    tok, width = block_input.shape
    heads, blk = reset_weight.shape[:2]
    rows_w = gate_weight.shape[0]
    feed = feed_gate_weight.shape[1]
    fs = feed // SIDE
    high = n // 16
    groups = side_groups()
    only = tuple(EXTRA)
    extra_here = jnp.where(here == only[1], EXTRA[only[1]], EXTRA[only[0]])
    has_extra = (here == only[0]) | (here == only[1])

    def exchange(v):
        return lax.all_to_all(v, AXIS, 0, 0, axis_index_groups=groups, tiled=True)

    def head_parts(w):
        w = w.reshape(rows_w, heads, blk)
        zero = jnp.zeros((rows_w, blk), w.dtype)
        return jnp.stack(
            [
                jnp.concatenate([w[:, s], w[:, EXTRA[s]] if s in EXTRA else zero], axis=1)
                for s in range(SIDE)
            ]
        )

    def feed_parts(w):
        return w.reshape(rows_w, SIDE, fs).transpose(1, 0, 2)

    def mixer_full(parts):
        shard = parts.reshape(SIDE * rows_w, 2 * blk).T
        first = gather_far(shard[:blk])
        second = gather_far(shard[blk:], only)
        return jnp.concatenate(
            [jnp.concatenate(first, axis=1), jnp.concatenate(second, axis=1)], axis=0
        )

    def feed_full(parts):
        return jnp.concatenate(gather_far(parts.reshape(SIDE * rows_w, fs)), axis=0)

    mix_parts = exchange(
        jnp.stack([head_parts(gate_weight), head_parts(linear_weight)], axis=1)
    )
    out_parts = exchange(head_parts(out_weight))
    feed_parts_all = exchange(
        jnp.stack(
            [feed_parts(w) for w in (feed_gate_weight, feed_value_weight, feed_down_weight)], axis=1
        )
    )
    gate_t, linear_t = mixer_full(mix_parts[:, 0]), mixer_full(mix_parts[:, 1])
    out_t = mixer_full(out_parts)
    w_gate, w_value, w_down = (feed_full(feed_parts_all[:, i]) for i in range(3))

    def pick(p):
        first = lax.dynamic_index_in_dim(p, here, 0, False)
        second = lax.dynamic_index_in_dim(p, extra_here, 0, False)
        return first, jnp.where(has_extra, second, jnp.zeros_like(second))

    def pick_vector(p):
        return jnp.concatenate(pick(p.astype(F32).reshape(heads, blk)))

    def pick_square(p):
        first, second = pick(p)
        return jnp.pad(first, ((0, blk), (0, blk))) + jnp.pad(second, ((blk, 0), (blk, 0)))

    taps = [pick_vector(conv_taps[k]) for k in range(4)]
    c_bias, r_bias, i_bias = (pick_vector(p) for p in (conv_bias, reset_bias, input_bias))
    decay_float = pick_vector(decay_param)
    r_square, i_square = pick_square(reset_weight), pick_square(input_weight)

    flags = lax.all_gather(
        start_flags.astype(F32), AXIS, axis_index_groups=groups, tiled=True
    )
    side_tok = SIDE * tok
    seg_tok = side_tok // 2
    starts = flags.reshape(side_tok, 1)
    keep = 1.0 - starts
    keep_seg = keep.reshape(2, seg_tok, 1)

    gain_one = to_near(norm_gain.astype(F32), me)
    gain_two = to_near(feed_norm_gain.astype(F32), me)
    x = to_near(block_input, me)
    top = to_near(output_grad, me)

    def canonical(blocks):
        buf = jnp.zeros((SIDE * blocks[0].shape[0], blocks[0].shape[1]), blocks[0].dtype)
        for j, b in enumerate(blocks):
            buf = lax.dynamic_update_slice(buf, b, ((here ^ j) * b.shape[0], 0))
        return buf

    def uncanonical(v):
        return [lax.dynamic_slice_in_dim(v, (here ^ j) * tok, tok, 0) for j in range(SIDE)]

    def blocks_of(v):
        return [v[j * tok : (j + 1) * tok] for j in range(SIDE)]

    scale_one = rms_scale(x)
    normed = (x * scale_one * gain_one).astype(BF16)
    normed_all = canonical(gather_side(normed))
    top_low = top.astype(BF16)
    top_all = jnp.concatenate(gather_side(top_low))

    linear = dot_last(normed_all, linear_t)
    gate_pre = dot_last(normed_all, gate_t)
    cw = linear.shape[1]
    lin_seg = linear.reshape(2, seg_tok, cw)
    k_last = keep_seg[:, seg_tok - 1 :]
    k_mid = k_last * keep_seg[:, seg_tok - 2 : seg_tok - 1]
    tail_keep = jnp.concatenate([k_mid, k_last, jnp.ones_like(k_last)], axis=1)
    tails = lin_seg[:, -3:] * tail_keep
    in_y = (me & YBIT) != 0
    tails_y = swap(tails, YBIT)
    fore = [(i - HBIT + YBIT, i) for i in range(HBIT, n) if i & YBIT == 0]
    back = [(b, a) for a, b in fore]
    tails_h = lax.ppermute(tails[1], AXIS, fore)
    halo = jnp.stack(
        [jnp.where(in_y, tails_y[0], tails_h), jnp.where(in_y, tails_y[1], tails_y[0])]
    )
    ext = jnp.concatenate([halo, lin_seg], axis=1)
    one_col = jnp.ones((2, 3, 1), F32)
    keep_ext = jnp.concatenate([one_col, keep_seg], axis=1)

    def behind(v, k):
        return v[:, 3 - k : 3 - k + seg_tok]

    same, running = [], None
    for k in range(3):
        running = behind(keep_ext, k) if running is None else running * behind(keep_ext, k)
        same.append(running)
    conv = lin_seg * taps[0] + c_bias
    for k in range(1, 4):
        conv = conv + behind(ext, k) * taps[k] * same[k - 1]
    conv_low = conv.astype(BF16).reshape(side_tok, cw)
    conv_value = conv_low.astype(F32)
    reset_gate = jax.nn.sigmoid(dot(conv_low, r_square) + r_bias)
    input_gate = jax.nn.sigmoid(dot(conv_low, i_square) + i_bias)
    soft_rate = jax.nn.softplus(-decay_float)
    decay = jnp.exp(-8.0 * reset_gate * soft_rate) * keep
    root = jnp.sqrt(1.0 - decay * decay + ROOT_GUARD)
    multiplier = keep * root + starts
    driven = multiplier * input_gate * conv_value
    decay_acc, local_states = run_scan(scan_kernel, decay, driven)

    here_far = [(me >> 2) & 1, me >> 4]

    def chain(scale_part, value_part, reverse):
        pair = jnp.stack([scale_part, value_part])
        found = jnp.stack(gather_far(pair))
        found = found.reshape(2, high, 2, 2, cw)
        found = flips(found, me, 0, 1)
        found = found.transpose(2, 1, 3, 0, 4).reshape(2, 4 * high, cw)
        order = range(4 * high - 1, -1, -1) if reverse else range(4 * high)
        state, incoming = jnp.zeros((cw,), F32), [None] * (4 * high)
        for g in order:
            incoming[g] = state
            state = found[0, g] * state + found[1, g]
        incoming = jnp.stack(incoming).reshape(high, 2, 2, cw)
        return incoming[here_far[1], :, here_far[0]]

    acc_seg = decay_acc.reshape(2, seg_tok, cw)
    loc_seg = local_states.reshape(2, seg_tok, cw)
    incoming = chain(acc_seg[:, -1], loc_seg[:, -1], False)
    states_seg = loc_seg + acc_seg * incoming[:, None]
    states = states_seg.reshape(side_tok, cw)
    gate_act, gate_slope = gelu_pair(gate_pre)
    mixed = (states * gate_act).astype(BF16)
    middle = x + scatter_side(uncanonical(dot(mixed, out_t)))

    scale_two = rms_scale(middle)
    normed_two = (middle * scale_two * gain_two).astype(BF16)
    two_all = jnp.concatenate(gather_side(normed_two))
    inner_gate = dot(two_all, w_gate)
    inner_value = dot(two_all, w_value)
    grad_hidden = dot(top_all, w_down)
    feed_act, feed_slope = gelu_pair(inner_gate)
    hidden = (feed_act * inner_value).astype(BF16)
    grad_ig = (grad_hidden * inner_value * feed_slope).astype(BF16)
    grad_iv = (grad_hidden * feed_act).astype(BF16)
    grad_normed_two = scatter_side(
        blocks_of(dot_last(grad_ig, w_gate) + dot_last(grad_iv, w_value))
    )
    block_output = middle + scatter_side(blocks_of(dot_last(hidden, w_down)))
    grad_gain_two = jnp.sum(grad_normed_two * middle * scale_two, axis=0)
    grad_middle = top + norm_back(grad_normed_two, middle, scale_two, gain_two)
    grad_branch = grad_middle.astype(BF16)
    branch_all = canonical(gather_side(grad_branch))

    def feed_grad(g):
        shard = scatter_far(g, 0).astype(BF16).reshape(SIDE, rows_w, fs)
        return exchange(shard).transpose(1, 0, 2).reshape(rows_w, feed).astype(F32)

    grad_w_gate = feed_grad(dot_first(two_all, grad_ig))
    grad_w_value = feed_grad(dot_first(two_all, grad_iv))
    grad_w_down = feed_grad(dot_first(top_all, hidden))

    grad_mixed = dot_last(branch_all, out_t)
    grad_gate_pre = (grad_mixed * states * gate_slope).astype(BF16)
    suffix, local_grads = run_scan(back_scan_kernel, decay, grad_mixed * gate_act)
    suf_seg = suffix.reshape(2, seg_tok, cw)
    lg_seg = local_grads.reshape(2, seg_tok, cw)
    first_decay = decay.reshape(2, seg_tok, cw)[:, 0]
    from_right = chain(first_decay * suf_seg[:, 0], first_decay * lg_seg[:, 0], True)
    grad_states = (lg_seg + suf_seg * from_right[:, None]).reshape(side_tok, cw)
    prior = jnp.concatenate([incoming[:, None], states_seg[:, :-1]], axis=1).reshape(side_tok, cw)
    grad_log = decay * (
        grad_states * prior - grad_states * input_gate * conv_value * decay / root
    )
    grad_decay = jnp.sum(8.0 * reset_gate * grad_log, axis=0) * jax.nn.sigmoid(-decay_float)
    grad_reset_pre = (-8.0 * soft_rate * grad_log * reset_gate * (1.0 - reset_gate)).astype(BF16)
    grad_input_pre = (
        grad_states * multiplier * conv_value * input_gate * (1.0 - input_gate)
    ).astype(BF16)
    grad_conv = (
        grad_states * multiplier * input_gate
        + dot_last(grad_reset_pre, r_square)
        + dot_last(grad_input_pre, i_square)
    )
    grad_r_bias = jnp.sum(grad_reset_pre.astype(F32), axis=0)
    grad_i_bias = jnp.sum(grad_input_pre.astype(F32), axis=0)
    gc_seg = grad_conv.reshape(2, seg_tok, cw)
    grad_c_bias = jnp.sum(grad_conv, axis=0)
    grad_taps = [jnp.sum(gc_seg * lin_seg, axis=(0, 1))]
    for k in range(1, 4):
        grad_taps.append(jnp.sum(gc_seg * behind(ext, k) * same[k - 1], axis=(0, 1)))
    h0 = keep_seg[:, 0:1]
    h1 = h0 * keep_seg[:, 1:2]
    h2 = h1 * keep_seg[:, 2:3]
    head_rows = gc_seg[:, :3] * jnp.concatenate([h0, h1, h2], axis=1)
    heads_y = swap(head_rows, YBIT)
    heads_h = lax.ppermute(head_rows[0], AXIS, back)
    after = jnp.stack(
        [jnp.where(in_y, heads_y[1], heads_y[0]), jnp.where(in_y, heads_h, heads_y[1])]
    )
    gc_ext = jnp.concatenate([gc_seg, after], axis=1)
    keep_after = jnp.concatenate([keep_seg, one_col], axis=1)
    grad_linear = gc_seg * taps[0]
    running = None
    for k in range(1, 4):
        ahead = keep_after[:, k : k + seg_tok]
        running = ahead if running is None else running * ahead
        grad_linear = grad_linear + gc_ext[:, k : k + seg_tok] * taps[k] * running
    grad_linear_low = grad_linear.astype(BF16).reshape(side_tok, cw)
    grad_normed = scatter_side(
        uncanonical(dot(grad_gate_pre, gate_t) + dot(grad_linear_low, linear_t))
    )
    grad_gain_one = jnp.sum(grad_normed * x * scale_one, axis=0)
    input_grad = grad_middle + norm_back(grad_normed, x, scale_one, gain_one)

    def mixer_shard(g):
        first = scatter_far(g[:blk], 1)
        second = scatter_far(g[blk:], 1, only)
        both = jnp.concatenate([first, second], axis=0).astype(BF16)
        return both.T.reshape(SIDE, rows_w, 2 * blk)

    def mixer_out(v):
        first = v[:, :, :blk].transpose(1, 0, 2).reshape(rows_w, SIDE * blk)
        return jnp.concatenate([first] + [v[s, :, blk:] for s in EXTRA], axis=1).astype(F32)

    grad_w_out = mixer_out(exchange(mixer_shard(dot_first(mixed, branch_all))))
    grad_w_mix = exchange(
        jnp.stack(
            [
                mixer_shard(dot_first(grad_gate_pre, normed_all)),
                mixer_shard(dot_first(grad_linear_low, normed_all)),
            ],
            axis=1,
        )
    )

    def head_squares(slot):
        sl = slice(slot * blk, (slot + 1) * blk)
        squares = jnp.concatenate(
            [
                dot_first(conv_low[:, sl], grad_reset_pre[:, sl]),
                dot_first(conv_low[:, sl], grad_input_pre[:, sl]),
            ],
            axis=1,
        )
        vectors = [grad_r_bias, grad_i_bias, grad_decay, grad_c_bias] + grad_taps
        vectors = jnp.stack([v[sl] for v in vectors]).reshape(4, 2 * blk)
        return jnp.concatenate([squares, vectors])

    def total_far(v, only=None):
        for m in far_masks():
            low = v.astype(BF16)
            v = low.astype(F32) + swap(low, m, only).astype(F32)
        return v.astype(BF16)

    first = canonical(gather_side_rows(total_far(head_squares(0))))
    second = total_far(head_squares(1), only)
    second = canonical(gather_side_rows(second))
    pack = blk + 4
    first = first.reshape(SIDE, -1, 2 * blk)
    second = second.reshape(SIDE, -1, 2 * blk)[jnp.array(only)]
    packs = jnp.concatenate([first, second])[:, :pack].astype(F32)
    grad_r_weight, grad_i_weight = packs[:, :blk, :blk], packs[:, :blk, blk:]
    vec = packs[:, blk:].reshape(heads, 8, blk).transpose(1, 0, 2).reshape(8, heads * blk)

    gains = jnp.stack([from_near(grad_gain_one, me), from_near(grad_gain_two, me)])
    gains = gains.reshape(-1, 256)
    for m in [CORE, XBIT, LBIT] + far_masks():
        gains = gains + swap(gains, m)
    gains = gains.reshape(2, width)

    return (
        from_near(block_output, me),
        from_near(input_grad, me),
        gains[0],
        mixer_out(grad_w_mix[:, 0]),
        mixer_out(grad_w_mix[:, 1]),
        vec[4:],
        vec[3],
        grad_r_weight,
        vec[0],
        grad_i_weight,
        vec[1],
        vec[2],
        grad_w_out,
        gains[1],
        grad_w_gate,
        grad_w_value,
        grad_w_down,
    )


def gather_side_rows(v):
    rows = v.shape[0]
    full = -(-rows // 32) * 32
    return gather_side(jnp.pad(v, ((0, full - rows), (0, 0))))


def solution(mesh):
    split, whole = P(AXIS, None), P()
    in_specs = (split, P(AXIS), whole, split, split) + (whole,) * 7
    in_specs += (split, whole, split, split, split, split)
    out_specs = (split, split, whole, split, split) + (whole,) * 7
    out_specs += (split, whole, split, split, split)
    return jax.shard_map(body, mesh=mesh, in_specs=in_specs, out_specs=out_specs, check_vma=False)
```

time: 3640 us -> 1110 us (0.30)
  waiting for transfers between devices: 2540 us -> 342 us
  local copies, waits for them, and re-layouts: 521 us -> 201 us
  starting transfers between devices: 4.21 us -> 239 us
  blocking collectives: 123 us -> 17.6 us
  matrix products: 240 us -> 143 us
  other arithmetic: 183 us -> 137 us
    reduce_scatter x1 -> x0, waiting for transfers between devices: 1280 us -> none  [body(): lax.psum_scatter(jnp.concatenate([matmul_first(normed_part, grad_inner_ga...]
    unnamed x11 -> x0, waiting for transfers between devices: 499 us -> none
    all_gather x6 -> x0, waiting for transfers between devices: 445 us -> none  [the longest x1 142 us: body(): lax.all_gather(feed_down_weight, 'seq', axis=0, tiled=True)]
    ppermute x2 -> x132, waiting for transfers between devices: 0.38 us -> 342 us  [the longest x130 342 us: swap(): return lax.ppermute(v, AXIS, pairs)]
    psum x2 -> x0, waiting for transfers between devices: 317 us -> none  [body(): lax.psum((grad_gain_one, grad_taps, grad_bias_conv, grad_reset_w, grad_re...]
    ppermute x2 -> x132, starting transfers between devices: 3.61 us -> 206 us  [the longest x130 205 us: swap(): return lax.ppermute(v, AXIS, pairs)]
    concatenate x3 -> x18, local copies, waits for them, and re-layouts: 164 us -> 20.5 us  [the longest x8 16.3 us: scatter_side(): return jnp.concatenate([ka[0] + a0 + a_last, kb[0] + b0 + b_last], axis=1)]
    all_gather x3 -> x1, blocking collectives: 123 us -> 17.6 us  [body(): lax.all_gather(start_flags.astype(F32), AXIS, axis_index_groups=groups, t...]
  transfers between devices with their start and end apart: 12 -> 140, of which waited for: 9 -> 37; matrix products, arithmetic and copies ran while one was open for 12% -> 37% of each run, Pallas kernels for 0% -> 1%
where the time goes in v1:
time: 1110 us; the launch traced here: 1100 us
  waiting for transfers between devices  342 us (31%)
  starting transfers between devices  239 us (22%)
  local copies, waits for them, and re-layouts  201 us (18%)
  matrix products  143 us (13%)
  other arithmetic  137 us (12%)
  blocking collectives  17.6 us (2%)
  Pallas kernels  16.4 us (1%)
    ppermute x130, waiting for transfers between devices, swap(): return lax.ppermute(v, AXIS, pairs)  342 us
    ppermute x130, starting transfers between devices, swap(): return lax.ppermute(v, AXIS, pairs)  205 us
    dot_general x8, matrix products, dot(): lax.dot_general(a, b, (((1,), (0,)), ((), ())), preferred_element_type=F32)  67.4 us
    dot_general x7, matrix products, dot_last(): lax.dot_general(a, b, (((1,), (1,)), ((), ())), preferred_element_type=F32)  44.5 us
    unnamed x461, local copies, waits for them, and re-layouts  43.1 us
    all_to_all x8, starting transfers between devices, exchange(): return lax.all_to_all(v, AXIS, 0, 0, axis_index_groups=groups, tiled=True)  33.3 us
    dynamic_update_slice x28, local copies, waits for them, and re-layouts, canonical(): buf = lax.dynamic_update_slice(buf, b, ((here ^ j) * b.shape[0], 0))  28.5 us
    dot_general x10, matrix products, dot_first(): lax.dot_general(a, b, (((0,), (0,)), ((), ())), preferred_element_type=F32)  27.2 us
  transfers between devices with their start and end apart: 140, of which 37 were waited for; matrix products, arithmetic and copies ran while one was open for 37% of the time, Pallas kernels for 1%

profile of v1, /device:TPU:0, one launch (start us, length us, event | category | flops | bytes accessed | tf_op | source)
XLA Modules:
  0.0 1102.3 jit_solution(8999632809959615503)
XLA Ops:
  36.2 17.6 %all-gather = f32[8,1,128]{2,1,0:T(1,128)S(1)} all-gather(f32[1,1,128]{2,1,0:T(1,128)S(1)} %convert_bitcast_fusion.3), channel_id=1, replica_groups={{0,1,2,3,8,9,10,11},{4,5,6,7,12,13,14,15},{16,17,18,19,24,25,26,27},{20..., dimensions={0}, use_global_device_ids=true | all-gather | bytes 4608 | tf_op jit(solution)/shard_map/all_gather | solution.py:338
  86.9 13.3 %collective-permute-done.5 = bf16[64,2048]{1,0:T(8,128)(2,1)S(1)} collective-permute-done((bf16[64,2048]{1,0:T(8,128)(2,1)S(1)}, bf16[64,2048]{1,0:T(8,128)(2,1)S(1)}, u32[]{:S(2)}, u32[]{:S(2)}) %collective-permute-start.5) | collective-permute-done | bytes 262176 | tf_op jit(solution)/shard_map/ppermute | solution.py:29
  103.1 4.4 all-to-all-start.2
  118.2 24.1 %collective-permute-done.8 = bf16[273,512]{0,1:T(8,128)(2,1)S(1)} collective-permute-done((bf16[273,512]{0,1:T(8,128)(2,1)S(1)}, bf16[273,512]{0,1:T(8,128)(2,1)S(1)}, u32[]{:S(2)}, u32[]{:S(2)}) %collective-permute-start.8) | collective-permute-done | bytes 279584 | tf_op jit(solution)/shard_map/ppermute | solution.py:29
  168.8 4.1 convert_multiply_fusion.2
  172.9 7.7 shard_map.314
  182.9 16.7 %collective-permute-start.16 = (f32[2,2,546]{2,1,0:T(2,128)S(1)}, f32[2,2,546]{2,1,0:T(2,128)S(1)}, u32[]{:S(2)}, u32[]{:S(2)}) collective-permute-start(f32[2,2,546]{2,1,0:T(2,128)S(1)} %get-tuple-element.226), channel_id=1, source_target_pairs={{0,16},{1,17},{2,18},{3,19},{4,20},{5,21},{6,22},{7,23},{8,24},{9,... | collective-permute-start | bytes 26216 | tf_op jit(solution)/shard_map/ppermute | solution.py:29
  206.3 3.8 collective-permute-start.28
  226.9 3.8 collective-permute-done.23
  230.7 3.9 collective-permute-start.30
  240.9 16.6 %collective-permute-done.24 = bf16[273,512]{0,1:T(8,128)(2,1)} collective-permute-done((bf16[273,512]{0,1:T(8,128)(2,1)}, bf16[273,512]{0,1:T(8,128)(2,1)}, u32[]{:S(2)}, u32[]{:S(2)}) %collective-permute-start.24) | collective-permute-done | bytes 279584 | tf_op jit(solution)/shard_map/ppermute | solution.py:29
  257.5 9.9 multiply_convert_fusion.5
  267.6 8.3 collective-permute-start.64
  276.4 8.8 fusion.142
  304.3 4.6 collective-permute-done.34
  310.3 12.3 %collective-permute-done.32 = bf16[256,1024]{1,0:T(8,128)(2,1)S(1)} collective-permute-done((bf16[256,1024]{1,0:T(8,128)(2,1)}, bf16[256,1024]{1,0:T(8,128)(2,1)S(1)}, u32[]{:S(2)}, u32[]{:S(2)}) %collective-permute-start.32) | collective-permute-done | bytes 524320 | tf_op jit(solution)/shard_map/ppermute | solution.py:29
  326.3 31.6 %collective-permute-done.50 = bf16[512,768]{1,0:T(8,128)(2,1)} collective-permute-done((bf16[512,768]{1,0:T(8,128)(2,1)}, bf16[512,768]{1,0:T(8,128)(2,1)}, u32[]{:S(2)}, u32[]{:S(2)}) %collective-permute-start.50) | collective-permute-done | bytes 786464 | tf_op jit(solution)/shard_map/ppermute | solution.py:29
  367.2 19.5 %collective-permute-start.39 = (bf16[128,2048]{1,0:T(8,128)(2,1)S(1)}, bf16[128,2048]{1,0:T(8,128)(2,1)S(1)}, u32[]{:S(2)}, u32[]{:S(2)}) collective-permute-start(bf16[128,2048]{1,0:T(8,128)(2,1)S(1)} %get-tuple-element.79), channel_id=1, source_target_pairs={{0,8},{1,9},{2,10},{3,11},{4,12},{5,13},{6,14},{7,15},{8,0},{9,1},... | collective-permute-start | bytes 1572872 | tf_op jit(solution)/shard_map/ppermute | solution.py:29
  386.9 5.3 fusion.48
  392.1 23.8 %collective-permute-done.39 = bf16[128,2048]{1,0:T(8,128)(2,1)S(1)} collective-permute-done((bf16[128,2048]{1,0:T(8,128)(2,1)S(1)}, bf16[128,2048]{1,0:T(8,128)(2,1)S(1)}, u32[]{:S(2)}, u32[]{:S(2)}) %collective-permute-start.39) | collective-permute-done | bytes 524320 | tf_op jit(solution)/shard_map/ppermute | solution.py:29
  416.5 5.9 collective-permute-done.41
  428.7 14.4 %collective-permute-done.48 = bf16[512,768]{1,0:T(8,128)(2,1)S(1)} collective-permute-done((bf16[512,768]{1,0:T(8,128)(2,1)}, bf16[512,768]{1,0:T(8,128)(2,1)S(1)}, u32[]{:S(2)}, u32[]{:S(2)}) %collective-permute-start.48) | collective-permute-done | bytes 786464 | tf_op jit(solution)/shard_map/ppermute | solution.py:29
  443.1 33.7 %collective-permute-done.49 = bf16[512,768]{1,0:T(8,128)(2,1)S(1)} collective-permute-done((bf16[512,768]{1,0:T(8,128)(2,1)}, bf16[512,768]{1,0:T(8,128)(2,1)S(1)}, u32[]{:S(2)}, u32[]{:S(2)}) %collective-permute-start.49) | collective-permute-done | bytes 786464 | tf_op jit(solution)/shard_map/ppermute | solution.py:29
  476.8 5.2 fusion.51
  482.0 5.3 collective-permute-done.46
  487.3 7.7 multiply_convert_fusion.1
  495.1 3.7 fusion.199
  501.9 3.7 fusion.198
  508.7 3.7 fusion.197
  517.2 8.4 fusion.50
  525.5 7.4 fusion.192
  535.4 9.4 fusion.193
  548.9 4.1 collective-permute-start.131
  553.0 18.6 %collective-permute-done.128 = bf16[1024,768]{1,0:T(8,128)(2,1)} collective-permute-done((bf16[1024,768]{1,0:T(8,128)(2,1)}, bf16[1024,768]{1,0:T(8,128)(2,1)}, u32[]{:S(2)}, u32[]{:S(2)}) %collective-permute-start.128) | collective-permute-done | bytes 1572896 | tf_op jit(solution)/shard_map/ppermute | solution.py:29
  577.8 20.3 %collective-permute-done.126 = bf16[1024,768]{1,0:T(8,128)(2,1)} collective-permute-done((bf16[1024,768]{1,0:T(8,128)(2,1)}, bf16[1024,768]{1,0:T(8,128)(2,1)}, u32[]{:S(2)}, u32[]{:S(2)}) %collective-permute-start.126) | collective-permute-done | bytes 1572896 | tf_op jit(solution)/shard_map/ppermute | solution.py:29
  600.8 5.6 collective-permute-start.127
  621.9 4.7 all-to-all-start.7
  626.6 11.8 %collective-permute-done.129 = bf16[512,768]{1,0:T(8,128)(2,1)} collective-permute-done((bf16[512,768]{1,0:T(8,128)(2,1)}, bf16[512,768]{1,0:T(8,128)(2,1)}, u32[]{:S(2)}, u32[]{:S(2)}) %collective-permute-start.129) | collective-permute-done | bytes 786464 | tf_op jit(solution)/shard_map/ppermute | solution.py:29
  644.6 18.8 %collective-permute-done.67 = bf16[256,1024]{1,0:T(8,128)(2,1)} collective-permute-done((bf16[256,1024]{1,0:T(8,128)(2,1)}, bf16[256,1024]{1,0:T(8,128)(2,1)}, u32[]{:S(2)}, u32[]{:S(2)}) %collective-permute-start.67) | collective-permute-done | bytes 524320 | tf_op jit(solution)/shard_map/ppermute | solution.py:29
  667.8 15.2 %collective-permute-done.54 = bf16[256,1024]{1,0:T(8,128)(2,1)S(1)} collective-permute-done((bf16[256,1024]{1,0:T(8,128)(2,1)}, bf16[256,1024]{1,0:T(8,128)(2,1)S(1)}, u32[]{:S(2)}, u32[]{:S(2)}) %collective-permute-start.54) | collective-permute-done | bytes 524320 | tf_op jit(solution)/shard_map/ppermute | solution.py:29
  694.2 4.2 all-to-all-start.6
  698.4 3.7 multiply_reduce_fusion.5
  716.6 4.7 collective-permute-done.74
  727.1 4.0 all-to-all-start.5
  755.0 4.6 fusion.196
  759.6 6.6 multiply_convert_fusion.4
  766.3 8.7 shard_map.315
  781.7 4.7 fusion.195
  789.7 15.7 %collective-permute-done.81 = f32[2,2,546]{2,1,0:T(2,128)S(1)} collective-permute-done((f32[2,2,546]{2,1,0:T(2,128)S(1)}, f32[2,2,546]{2,1,0:T(2,128)S(1)}, u32[]{:S(2)}, u32[]{:S(2)}) %collective-permute-start.81) | collective-permute-done | bytes 8768 | tf_op jit(solution)/shard_map/ppermute | solution.py:29
  805.7 6.8 fusion.146
  813.8 5.5 multiply_reduce_fusion.4
  857.9 8.2 collective-permute-start.112
  869.1 4.1 fusion.194
  873.3 20.2 %fusion.143 = f32[1024,2048]{1,0:T(8,128)} fusion(bf16[1024,546]{1,0:T(8,128)(2,1)S(1)} %bitcast.628, bf16[273,512]{0,1:T(8,128)(2,1)S(1)} %copy-done.177, bf16[273,512]{0,1:T(8,128)(2,1)S(1)} %copy-done.171, bf16[273,512]{0,1:T(8,128)(2,1)S(1)} %copy-done.169, bf16[273,512]{0,1:T(8,128)(2,1)S(1)} %copy-done.101, bf16[273,512]{0,1:T(8,128)(2,1)S(1)} %copy-done.175, ...), kind=kOutput, calls=%fused_computation.585 | convolution fusion | flops 2307981312 | bytes 11743232 | tf_op jit(solution)/shard_map/dot_general | solution.py:48
  893.5 14.8 %convolution_add_fusion = f32[1024,2048]{1,0:T(8,128)S(1)} fusion(f32[1024,2048]{1,0:T(8,128)} %fusion.143, bf16[1024,546]{1,0:T(8,128)(2,1)S(1)} %copy-done.88, bf16[273,512]{0,1:T(8,128)(2,1)} %collective-permute-done.24, bf16[273,512]{0,1:T(8,128)(2,1)S(1)} %copy-done.105, bf16[273,512]{0,1:T(8,128)(2,1)} %collective-permute-done.22, ...), kind=kOutput, calls=%fused_computation.4 | convolution fusion | flops 2310078464 | bytes 20131840 | tf_op jit(solution)/shard_map/dot_general | solution.py:48
  913.8 3.9 collective-permute-start.96
  956.9 4.9 all-to-all-start.4
  976.9 4.5 collective-permute-done.105
  983.3 5.9 collective-permute-done.115
  1016.5 4.8 fusion.164
  1021.3 4.0 all-to-all-start.3
  1025.3 4.5 convert_add_fusion.1
  1042.2 11.7 %collective-permute-done.87 = bf16[256,1024]{1,0:T(8,128)(2,1)} collective-permute-done((bf16[256,1024]{1,0:T(8,128)(2,1)}, bf16[256,1024]{1,0:T(8,128)(2,1)}, u32[]{:S(2)}, u32[]{:S(2)}) %collective-permute-start.87) | collective-permute-done | bytes 524320 | tf_op jit(solution)/shard_map/ppermute | solution.py:29
  1080.1 4.9 subtract_add_fusion
  (1093 shorter events, 483.7 us)
Async XLA Ops:
  10.7 71.9 %collective-permute-start = (bf16[128,2048]{1,0:T(8,128)(2,1)}, bf16[128,2048]{1,0:T(8,128)(2,1)}, u32[]{:S(2)}, u32[]{:S(2)}) collective-permute-start(bf16[128,2048]{1,0:T(8,128)(2,1)} %get-tuple-element.92), channel_id=1, source_target_pairs={{0,1},{1,0},{2,3},{3,2},{4,5},{5,4},{6,7},{7,6},{8,9},{9,8},{10,11... | collective-permute-start | bytes 1572872 | tf_op jit(solution)/shard_map/ppermute | solution.py:29
  11.2 69.0 %collective-permute-start.1 = (bf16[128,2048]{1,0:T(8,128)(2,1)}, bf16[128,2048]{1,0:T(8,128)(2,1)}, u32[]{:S(2)}, u32[]{:S(2)}) collective-permute-start(bf16[128,2048]{1,0:T(8,128)(2,1)} %get-tuple-element.92), channel_id=1, source_target_pairs={{0,2},{1,3},{2,0},{3,1},{4,6},{5,7},{6,4},{7,5},{8,10},{9,11},{10,... | collective-permute-start | bytes 1572872 | tf_op jit(solution)/shard_map/ppermute | solution.py:29
  13.7 64.5 %collective-permute-start.3 = (bf16[128,2048]{1,0:T(8,128)(2,1)}, bf16[128,2048]{1,0:T(8,128)(2,1)S(1)}, u32[]{:S(2)}, u32[]{:S(2)}) collective-permute-start(bf16[128,2048]{1,0:T(8,128)(2,1)} %get-tuple-element.92), channel_id=1, source_target_pairs={{0,8},{1,9},{2,10},{3,11},{4,12},{5,13},{6,14},{7,15},{8,0},{9,1},... | collective-permute-start | bytes 1572872 | tf_op jit(solution)/shard_map/ppermute | solution.py:29
  22.2 51.6 %all-to-all-start.1 = ((bf16[8,64,546]{2,1,0:T(8,128)(2,1)}), bf16[8,64,546]{2,1,0:T(8,128)(2,1)S(1)}, u32[]{:S(2)}, u32[]{:S(2)}) async-start(bf16[8,64,546]{2,1,0:T(8,128)(2,1)} %constant_dynamic-update-slice_fusion.18), calls=%async_computation.1 | async-start | bytes 1310720 | tf_op jit(solution)/shard_map/all_to_all | solution.py:282
  34.3 170.3 %collective-permute-start.59 = (bf16[128,2048]{1,0:T(8,128)(2,1)}, bf16[128,2048]{1,0:T(8,128)(2,1)}, u32[]{:S(2)}, u32[]{:S(2)}) collective-permute-start(bf16[128,2048]{1,0:T(8,128)(2,1)} %get-tuple-element.77), channel_id=1, source_target_pairs={{0,2},{1,3},{2,0},{3,1},{4,6},{5,7},{6,4},{7,5},{8,10},{9,11},{10,... | collective-permute-start | bytes 1572872 | tf_op jit(solution)/shard_map/ppermute | solution.py:29
  73.8 29.3 %all-to-all-start = ((bf16[8,2,64,546]{3,2,1,0:T(8,128)(2,1)}), bf16[8,2,64,546]{3,2,1,0:T(8,128)(2,1)S(1)}, u32[]{:S(2)}, u32[]{:S(2)}) async-start(bf16[8,2,64,546]{3,2,1,0:T(8,128)(2,1)} %copy.911), calls=%async_computation | async-start | bytes 2621440 | tf_op jit(solution)/shard_map/all_to_all | solution.py:282
  82.7 30.3 %collective-permute-start.4 = (bf16[128,2048]{1,0:T(8,128)(2,1)S(1)}, bf16[128,2048]{1,0:T(8,128)(2,1)}, u32[]{:S(2)}, u32[]{:S(2)}) collective-permute-start(bf16[128,2048]{1,0:T(8,128)(2,1)S(1)} %collective-permute-done.3), channel_id=1, source_target_pairs={{0,1},{1,0},{2,3},{3,2},{4,5},{5,4},{6,7},{7,6},{8,9},{9,8},{10,11... | collective-permute-start | bytes 1572872 | tf_op jit(solution)/shard_map/ppermute | solution.py:29
  103.1 196.3 %all-to-all-start.2 = ((bf16[8,3,64,768]{3,2,1,0:T(8,128)(2,1)}), bf16[8,3,64,768]{3,2,1,0:T(8,128)(2,1)}, u32[]{:S(2)}, u32[]{:S(2)}) async-start(bf16[8,3,64,768]{3,2,1,0:T(8,128)(2,1)} %copy.927), calls=%async_computation.2 | async-start | bytes 4718592 | tf_op jit(solution)/shard_map/all_to_all | solution.py:282
  107.8 34.4 %collective-permute-start.8 = (bf16[273,512]{0,1:T(8,128)(2,1)S(1)}, bf16[273,512]{0,1:T(8,128)(2,1)S(1)}, u32[]{:S(2)}, u32[]{:S(2)}) collective-permute-start(bf16[273,512]{0,1:T(8,128)(2,1)S(1)} %get-tuple-element.205), channel_id=1, source_target_pairs={{0,16},{1,17},{2,18},{3,19},{4,20},{5,21},{6,22},{7,23},{8,24},{9,... | collective-permute-start | bytes 838664 | tf_op jit(solution)/shard_map/ppermute | solution.py:29
  110.5 36.0 %collective-permute-start.11 = (bf16[273,512]{0,1:T(8,128)(2,1)S(1)}, bf16[273,512]{0,1:T(8,128)(2,1)S(1)}, u32[]{:S(2)}, u32[]{:S(2)}) collective-permute-start(bf16[273,512]{0,1:T(8,128)(2,1)S(1)} %get-tuple-element.206), channel_id=1, source_target_pairs={{0,16},{4,20},{10,26},{14,30},{16,0},{20,4},{26,10},{30,14}} | collective-permute-start | bytes 838664 | tf_op jit(solution)/shard_map/ppermute | solution.py:29
  114.1 37.2 %collective-permute-start.12 = (bf16[273,512]{0,1:T(8,128)(2,1)S(1)}, bf16[273,512]{0,1:T(8,128)(2,1)S(1)}, u32[]{:S(2)}, u32[]{:S(2)}) collective-permute-start(bf16[273,512]{0,1:T(8,128)(2,1)S(1)} %get-tuple-element.206), channel_id=1, source_target_pairs={{0,4},{4,0},{10,14},{14,10},{16,20},{20,16},{26,30},{30,26}} | collective-permute-start | bytes 838664 | tf_op jit(solution)/shard_map/ppermute | solution.py:29
  117.6 33.9 %collective-permute-start.9 = (bf16[273,512]{0,1:T(8,128)(2,1)S(1)}, bf16[273,512]{0,1:T(8,128)(2,1)S(1)}, u32[]{:S(2)}, u32[]{:S(2)}) collective-permute-start(bf16[273,512]{0,1:T(8,128)(2,1)S(1)} %get-tuple-element.205), channel_id=1, source_target_pairs={{0,4},{1,5},{2,6},{3,7},{4,0},{5,1},{6,2},{7,3},{8,12},{9,13},{10,... | collective-permute-start | bytes 838664 | tf_op jit(solution)/shard_map/ppermute | solution.py:29
  151.4 48.8 %collective-permute-start.61 = (bf16[128,2048]{1,0:T(8,128)(2,1)}, bf16[128,2048]{1,0:T(8,128)(2,1)}, u32[]{:S(2)}, u32[]{:S(2)}) collective-permute-start(bf16[128,2048]{1,0:T(8,128)(2,1)} %get-tuple-element.77), channel_id=1, source_target_pairs={{0,8},{1,9},{2,10},{3,11},{4,12},{5,13},{6,14},{7,15},{8,0},{9,1},... | collective-permute-start | bytes 1572872 | tf_op jit(solution)/shard_map/ppermute | solution.py:29
  151.5 62.7 %collective-permute-start.25 = (bf16[273,512]{0,1:T(8,128)(2,1)}, bf16[273,512]{0,1:T(8,128)(2,1)}, u32[]{:S(2)}, u32[]{:S(2)}) collective-permute-start(bf16[273,512]{0,1:T(8,128)(2,1)} %get-tuple-element.203), channel_id=1, source_target_pairs={{0,16},{1,17},{2,18},{3,19},{4,20},{5,21},{6,22},{7,23},{8,24},{9,... | collective-permute-start | bytes 838664 | tf_op jit(solution)/shard_map/ppermute | solution.py:29
  155.0 62.1 %collective-permute-start.19 = (bf16[273,512]{0,1:T(8,128)(2,1)S(1)}, bf16[273,512]{0,1:T(8,128)(2,1)}, u32[]{:S(2)}, u32[]{:S(2)}) collective-permute-start(bf16[273,512]{0,1:T(8,128)(2,1)S(1)} %get-tuple-element.207), channel_id=1, source_target_pairs={{0,16},{1,17},{2,18},{3,19},{4,20},{5,21},{6,22},{7,23},{8,24},{9,... | collective-permute-start | bytes 838664 | tf_op jit(solution)/shard_map/ppermute | solution.py:29
  218.3 49.2 %collective-permute-start.26 = (bf16[273,512]{0,1:T(8,128)(2,1)}, bf16[273,512]{0,1:T(8,128)(2,1)}, u32[]{:S(2)}, u32[]{:S(2)}) collective-permute-start(bf16[273,512]{0,1:T(8,128)(2,1)} %get-tuple-element.203), channel_id=1, source_target_pairs={{0,4},{1,5},{2,6},{3,7},{4,0},{5,1},{6,2},{7,3},{8,12},{9,13},{10,... | collective-permute-start | bytes 838664 | tf_op jit(solution)/shard_map/ppermute | solution.py:29
  222.9 44.7 %collective-permute-start.29 = (bf16[273,512]{0,1:T(8,128)(2,1)}, bf16[273,512]{0,1:T(8,128)(2,1)}, u32[]{:S(2)}, u32[]{:S(2)}) collective-permute-start(bf16[273,512]{0,1:T(8,128)(2,1)} %get-tuple-element.204), channel_id=1, source_target_pairs={{0,4},{4,0},{10,14},{14,10},{16,20},{20,16},{26,30},{30,26}} | collective-permute-start | bytes 838664 | tf_op jit(solution)/shard_map/ppermute | solution.py:29
  224.9 51.0 %collective-permute-start.27 = (bf16[273,512]{0,1:T(8,128)(2,1)}, bf16[273,512]{0,1:T(8,128)(2,1)}, u32[]{:S(2)}, u32[]{:S(2)}) collective-permute-start(bf16[273,512]{0,1:T(8,128)(2,1)} %collective-permute-done.25), channel_id=1, source_target_pairs={{0,4},{1,5},{2,6},{3,7},{4,0},{5,1},{6,2},{7,3},{8,12},{9,13},{10,... | collective-permute-start | bytes 838664 | tf_op jit(solution)/shard_map/ppermute | solution.py:29
  230.7 45.2 %collective-permute-start.30 = (bf16[273,512]{0,1:T(8,128)(2,1)}, bf16[273,512]{0,1:T(8,128)(2,1)}, u32[]{:S(2)}, u32[]{:S(2)}) collective-permute-start(bf16[273,512]{0,1:T(8,128)(2,1)} %collective-permute-done.28), channel_id=1, source_target_pairs={{0,4},{4,0},{10,14},{14,10},{16,20},{20,16},{26,30},{30,26}} | collective-permute-start | bytes 838664 | tf_op jit(solution)/shard_map/ppermute | solution.py:29
  257.5 28.4 %collective-permute-start.58 = (bf16[128,2048]{1,0:T(8,128)(2,1)}, bf16[128,2048]{1,0:T(8,128)(2,1)S(1)}, u32[]{:S(2)}, u32[]{:S(2)}) collective-permute-start(bf16[128,2048]{1,0:T(8,128)(2,1)} %get-tuple-element.77), channel_id=1, source_target_pairs={{0,1},{1,0},{2,3},{3,2},{4,5},{5,4},{6,7},{7,6},{8,9},{9,8},{10,11... | collective-permute-start | bytes 1572872 | tf_op jit(solution)/shard_map/ppermute | solution.py:29
  302.5 55.4 %collective-permute-start.50 = (bf16[512,768]{1,0:T(8,128)(2,1)}, bf16[512,768]{1,0:T(8,128)(2,1)}, u32[]{:S(2)}, u32[]{:S(2)}) collective-permute-start(bf16[512,768]{1,0:T(8,128)(2,1)} %bitcast.95), channel_id=1, source_target_pairs={{0,16},{1,17},{2,18},{3,19},{4,20},{5,21},{6,22},{7,23},{8,24},{9,... | collective-permute-start | bytes 2359304 | tf_op jit(solution)/shard_map/ppermute | solution.py:29
  310.1 47.8 %collective-permute-start.35 = (bf16[128,1024]{1,0:T(8,128)(2,1)S(1)}, bf16[128,1024]{1,0:T(8,128)(2,1)S(1)}, u32[]{:S(2)}, u32[]{:S(2)}) collective-permute-start(bf16[128,1024]{1,0:T(8,128)(2,1)S(1)} %fusion.65), channel_id=1, source_target_pairs={{0,8},{1,9},{2,10},{3,11},{4,12},{5,13},{6,14},{7,15},{8,0},{9,1},... | collective-permute-start | bytes 786440 | tf_op jit(solution)/shard_map/ppermute | solution.py:29
  322.8 36.0 %collective-permute-start.33 = (bf16[128,1024]{1,0:T(8,128)(2,1)S(1)}, bf16[128,1024]{1,0:T(8,128)(2,1)S(1)}, u32[]{:S(2)}, u32[]{:S(2)}) collective-permute-start(bf16[128,1024]{1,0:T(8,128)(2,1)S(1)} %fusion.67), channel_id=1, source_target_pairs={{0,2},{1,3},{2,0},{3,1},{4,6},{5,7},{6,4},{7,5},{8,10},{9,11},{10,... | collective-permute-start | bytes 786440 | tf_op jit(solution)/shard_map/ppermute | solution.py:29
  324.6 62.1 %collective-permute-start.51 = (bf16[512,768]{1,0:T(8,128)(2,1)}, bf16[512,768]{1,0:T(8,128)(2,1)}, u32[]{:S(2)}, u32[]{:S(2)}) collective-permute-start(bf16[512,768]{1,0:T(8,128)(2,1)} %bitcast.95), channel_id=1, source_target_pairs={{0,4},{1,5},{2,6},{3,7},{4,0},{5,1},{6,2},{7,3},{8,12},{9,13},{10,... | collective-permute-start | bytes 2359304 | tf_op jit(solution)/shard_map/ppermute | solution.py:29
  326.3 97.0 %collective-permute-start.47 = (bf16[512,768]{1,0:T(8,128)(2,1)}, bf16[512,768]{1,0:T(8,128)(2,1)}, u32[]{:S(2)}, u32[]{:S(2)}) collective-permute-start(bf16[512,768]{1,0:T(8,128)(2,1)} %bitcast.94), channel_id=1, source_target_pairs={{0,16},{1,17},{2,18},{3,19},{4,20},{5,21},{6,22},{7,23},{8,24},{9,... | collective-permute-start | bytes 2359304 | tf_op jit(solution)/shard_map/ppermute | solution.py:29
  357.9 66.6 %collective-permute-start.44 = (bf16[512,768]{1,0:T(8,128)(2,1)}, bf16[512,768]{1,0:T(8,128)(2,1)}, u32[]{:S(2)}, u32[]{:S(2)}) collective-permute-start(bf16[512,768]{1,0:T(8,128)(2,1)} %bitcast.93), channel_id=1, source_target_pairs={{0,16},{1,17},{2,18},{3,19},{4,20},{5,21},{6,22},{7,23},{8,24},{9,... | collective-permute-start | bytes 2359304 | tf_op jit(solution)/shard_map/ppermute | solution.py:29
  357.9 28.9 %collective-permute-start.52 = (bf16[512,768]{1,0:T(8,128)(2,1)}, bf16[512,768]{1,0:T(8,128)(2,1)}, u32[]{:S(2)}, u32[]{:S(2)}) collective-permute-start(bf16[512,768]{1,0:T(8,128)(2,1)} %collective-permute-done.50), channel_id=1, source_target_pairs={{0,4},{1,5},{2,6},{3,7},{4,0},{5,1},{6,2},{7,3},{8,12},{9,13},{10,... | collective-permute-start | bytes 2359304 | tf_op jit(solution)/shard_map/ppermute | solution.py:29
  367.2 48.7 %collective-permute-start.39 = (bf16[128,2048]{1,0:T(8,128)(2,1)S(1)}, bf16[128,2048]{1,0:T(8,128)(2,1)S(1)}, u32[]{:S(2)}, u32[]{:S(2)}) collective-permute-start(bf16[128,2048]{1,0:T(8,128)(2,1)S(1)} %get-tuple-element.79), channel_id=1, source_target_pairs={{0,8},{1,9},{2,10},{3,11},{4,12},{5,13},{6,14},{7,15},{8,0},{9,1},... | collective-permute-start | bytes 1572872 | tf_op jit(solution)/shard_map/ppermute | solution.py:29
  386.8 29.5 %collective-permute-start.37 = (bf16[128,2048]{1,0:T(8,128)(2,1)S(1)}, bf16[128,2048]{1,0:T(8,128)(2,1)S(1)}, u32[]{:S(2)}, u32[]{:S(2)}) collective-permute-start(bf16[128,2048]{1,0:T(8,128)(2,1)S(1)} %get-tuple-element.79), channel_id=1, source_target_pairs={{0,2},{1,3},{2,0},{3,1},{4,6},{5,7},{6,4},{7,5},{8,10},{9,11},{10,... | collective-permute-start | bytes 1572872 | tf_op jit(solution)/shard_map/ppermute | solution.py:29
  386.8 29.6 %collective-permute-start.36 = (bf16[128,2048]{1,0:T(8,128)(2,1)S(1)}, bf16[128,2048]{1,0:T(8,128)(2,1)S(1)}, u32[]{:S(2)}, u32[]{:S(2)}) collective-permute-start(bf16[128,2048]{1,0:T(8,128)(2,1)S(1)} %get-tuple-element.79), channel_id=1, source_target_pairs={{0,1},{1,0},{2,3},{3,2},{4,5},{5,4},{6,7},{7,6},{8,9},{9,8},{10,11... | collective-permute-start | bytes 1572872 | tf_op jit(solution)/shard_map/ppermute | solution.py:29
  423.3 58.6 %collective-permute-start.45 = (bf16[512,768]{1,0:T(8,128)(2,1)}, bf16[512,768]{1,0:T(8,128)(2,1)S(1)}, u32[]{:S(2)}, u32[]{:S(2)}) collective-permute-start(bf16[512,768]{1,0:T(8,128)(2,1)} %bitcast.93), channel_id=1, source_target_pairs={{0,4},{1,5},{2,6},{3,7},{4,0},{5,1},{6,2},{7,3},{8,12},{9,13},{10,... | collective-permute-start | bytes 2359304 | tf_op jit(solution)/shard_map/ppermute | solution.py:29
  424.5 52.2 %collective-permute-start.49 = (bf16[512,768]{1,0:T(8,128)(2,1)}, bf16[512,768]{1,0:T(8,128)(2,1)S(1)}, u32[]{:S(2)}, u32[]{:S(2)}) collective-permute-start(bf16[512,768]{1,0:T(8,128)(2,1)} %collective-permute-done.47), channel_id=1, source_target_pairs={{0,4},{1,5},{2,6},{3,7},{4,0},{5,1},{6,2},{7,3},{8,12},{9,13},{10,... | collective-permute-start | bytes 2359304 | tf_op jit(solution)/shard_map/ppermute | solution.py:29
  425.4 61.9 %collective-permute-start.46 = (bf16[512,768]{1,0:T(8,128)(2,1)}, bf16[512,768]{1,0:T(8,128)(2,1)S(1)}, u32[]{:S(2)}, u32[]{:S(2)}) collective-permute-start(bf16[512,768]{1,0:T(8,128)(2,1)} %collective-permute-done.44), channel_id=1, source_target_pairs={{0,4},{1,5},{2,6},{3,7},{4,0},{5,1},{6,2},{7,3},{8,12},{9,13},{10,... | collective-permute-start | bytes 2359304 | tf_op jit(solution)/shard_map/ppermute | solution.py:29
  500.2 46.3 %collective-permute-start.130 = (bf16[1024,768]{1,0:T(8,128)(2,1)}, bf16[1024,768]{1,0:T(8,128)(2,1)}, u32[]{:S(2)}, u32[]{:S(2)}) collective-permute-start(bf16[1024,768]{1,0:T(8,128)(2,1)} %slice.1826), channel_id=1, source_target_pairs={{0,4},{1,5},{2,6},{3,7},{4,0},{5,1},{6,2},{7,3},{8,12},{9,13},{10,... | collective-permute-start | bytes 4718600 | tf_op jit(solution)/shard_map/ppermute | solution.py:29
  507.1 64.5 %collective-permute-start.128 = (bf16[1024,768]{1,0:T(8,128)(2,1)}, bf16[1024,768]{1,0:T(8,128)(2,1)}, u32[]{:S(2)}, u32[]{:S(2)}) collective-permute-start(bf16[1024,768]{1,0:T(8,128)(2,1)} %slice.1827), channel_id=1, source_target_pairs={{0,4},{1,5},{2,6},{3,7},{4,0},{5,1},{6,2},{7,3},{8,12},{9,13},{10,... | collective-permute-start | bytes 4718600 | tf_op jit(solution)/shard_map/ppermute | solution.py:29
  516.3 81.8 %collective-permute-start.126 = (bf16[1024,768]{1,0:T(8,128)(2,1)}, bf16[1024,768]{1,0:T(8,128)(2,1)}, u32[]{:S(2)}, u32[]{:S(2)}) collective-permute-start(bf16[1024,768]{1,0:T(8,128)(2,1)} %slice.1828), channel_id=1, source_target_pairs={{0,4},{1,5},{2,6},{3,7},{4,0},{5,1},{6,2},{7,3},{8,12},{9,13},{10,... | collective-permute-start | bytes 4718600 | tf_op jit(solution)/shard_map/ppermute | solution.py:29
  534.7 71.7 %collective-permute-start.66 = (bf16[512,2048]{1,0:T(8,128)(2,1)}, bf16[512,2048]{1,0:T(8,128)(2,1)}, u32[]{:S(2)}, u32[]{:S(2)}) collective-permute-start(bf16[512,2048]{1,0:T(8,128)(2,1)} %pad_maximum_fusion.9), channel_id=1, source_target_pairs={{0,1},{1,0},{2,3},{3,2},{4,5},{5,4},{6,7},{7,6},{8,9},{9,8},{10,11... | collective-permute-start | bytes 6291464 | tf_op jit(solution)/shard_map/ppermute | solution.py:29
  546.5 68.8 %collective-permute-start.53 = (bf16[512,2048]{1,0:T(8,128)(2,1)}, bf16[512,2048]{1,0:T(8,128)(2,1)}, u32[]{:S(2)}, u32[]{:S(2)}) collective-permute-start(bf16[512,2048]{1,0:T(8,128)(2,1)} %pad_maximum_fusion.8), channel_id=1, source_target_pairs={{0,1},{1,0},{2,3},{3,2},{4,5},{5,4},{6,7},{7,6},{8,9},{9,8},{10,11... | collective-permute-start | bytes 6291464 | tf_op jit(solution)/shard_map/ppermute | solution.py:29
  548.9 71.9 %collective-permute-start.131 = (bf16[512,768]{1,0:T(8,128)(2,1)S(1)}, bf16[512,768]{1,0:T(8,128)(2,1)S(1)}, u32[]{:S(2)}, u32[]{:S(2)}) collective-permute-start(bf16[512,768]{1,0:T(8,128)(2,1)S(1)} %slice.1829), channel_id=1, source_target_pairs={{0,16},{1,17},{2,18},{3,19},{4,20},{5,21},{6,22},{7,23},{8,24},{9,... | collective-permute-start | bytes 2359304 | tf_op jit(solution)/shard_map/ppermute | solution.py:29
  574.5 64.0 %collective-permute-start.129 = (bf16[512,768]{1,0:T(8,128)(2,1)}, bf16[512,768]{1,0:T(8,128)(2,1)}, u32[]{:S(2)}, u32[]{:S(2)}) collective-permute-start(bf16[512,768]{1,0:T(8,128)(2,1)} %slice.1830), channel_id=1, source_target_pairs={{0,16},{1,17},{2,18},{3,19},{4,20},{5,21},{6,22},{7,23},{8,24},{9,... | collective-permute-start | bytes 2359304 | tf_op jit(solution)/shard_map/ppermute | solution.py:29
  600.8 107.9 %collective-permute-start.127 = (bf16[512,768]{1,0:T(8,128)(2,1)}, bf16[512,768]{1,0:T(8,128)(2,1)}, u32[]{:S(2)}, u32[]{:S(2)}) collective-permute-start(bf16[512,768]{1,0:T(8,128)(2,1)} %slice.1831), channel_id=1, source_target_pairs={{0,16},{1,17},{2,18},{3,19},{4,20},{5,21},{6,22},{7,23},{8,24},{9,... | collective-permute-start | bytes 2359304 | tf_op jit(solution)/shard_map/ppermute | solution.py:29
  610.9 30.3 %collective-permute-start.69 = (bf16[256,1024]{1,0:T(8,128)(2,1)}, bf16[256,1024]{1,0:T(8,128)(2,1)}, u32[]{:S(2)}, u32[]{:S(2)}) collective-permute-start(bf16[256,1024]{1,0:T(8,128)(2,1)} %pad_maximum_fusion.28), channel_id=1, source_target_pairs={{0,2},{1,3},{2,0},{3,1},{4,6},{5,7},{6,4},{7,5},{8,10},{9,11},{10,... | collective-permute-start | bytes 1572872 | tf_op jit(solution)/shard_map/ppermute | solution.py:29
  615.4 48.0 %collective-permute-start.67 = (bf16[256,1024]{1,0:T(8,128)(2,1)}, bf16[256,1024]{1,0:T(8,128)(2,1)}, u32[]{:S(2)}, u32[]{:S(2)}) collective-permute-start(bf16[256,1024]{1,0:T(8,128)(2,1)} %pad_maximum_fusion.27), channel_id=1, source_target_pairs={{0,8},{1,9},{2,10},{3,11},{4,12},{5,13},{6,14},{7,15},{8,0},{9,1},... | collective-permute-start | bytes 1572872 | tf_op jit(solution)/shard_map/ppermute | solution.py:29
  620.7 44.0 %collective-permute-start.56 = (bf16[256,1024]{1,0:T(8,128)(2,1)}, bf16[256,1024]{1,0:T(8,128)(2,1)}, u32[]{:S(2)}, u32[]{:S(2)}) collective-permute-start(bf16[256,1024]{1,0:T(8,128)(2,1)} %pad_maximum_fusion.25), channel_id=1, source_target_pairs={{0,2},{1,3},{2,0},{3,1},{4,6},{5,7},{6,4},{7,5},{8,10},{9,11},{10,... | collective-permute-start | bytes 1572872 | tf_op jit(solution)/shard_map/ppermute | solution.py:29
  621.9 72.3 %all-to-all-start.7 = ((bf16[8,64,768]{2,1,0:T(8,128)(2,1)}), bf16[8,64,768]{2,1,0:T(8,128)(2,1)}, u32[]{:S(2)}, u32[]{:S(2)}) async-start(bf16[8,64,768]{2,1,0:T(8,128)(2,1)} %bitcast.614), calls=%async_computation.7 | async-start | bytes 1572864 | tf_op jit(solution)/shard_map/all_to_all | solution.py:282
  638.5 44.5 %collective-permute-start.54 = (bf16[256,1024]{1,0:T(8,128)(2,1)}, bf16[256,1024]{1,0:T(8,128)(2,1)S(1)}, u32[]{:S(2)}, u32[]{:S(2)}) collective-permute-start(bf16[256,1024]{1,0:T(8,128)(2,1)} %pad_maximum_fusion.24), channel_id=1, source_target_pairs={{0,8},{1,9},{2,10},{3,11},{4,12},{5,13},{6,14},{7,15},{8,0},{9,1},... | collective-permute-start | bytes 1572872 | tf_op jit(solution)/shard_map/ppermute | solution.py:29
  642.6 45.8 %collective-permute-start.70 = (bf16[128,1024]{1,0:T(8,128)(2,1)S(1)}, bf16[128,1024]{1,0:T(8,128)(2,1)S(1)}, u32[]{:S(2)}, u32[]{:S(2)}) collective-permute-start(bf16[128,1024]{1,0:T(8,128)(2,1)S(1)} %fusion.57), channel_id=1, source_target_pairs={{0,8},{1,9},{2,10},{3,11},{4,12},{5,13},{6,14},{7,15},{8,0},{9,1},... | collective-permute-start | bytes 786440 | tf_op jit(solution)/shard_map/ppermute | solution.py:29
  664.6 23.7 %collective-permute-start.68 = (bf16[128,1024]{1,0:T(8,128)(2,1)S(1)}, bf16[128,1024]{1,0:T(8,128)(2,1)S(1)}, u32[]{:S(2)}, u32[]{:S(2)}) collective-permute-start(bf16[128,1024]{1,0:T(8,128)(2,1)S(1)} %fusion.59), channel_id=1, source_target_pairs={{0,2},{1,3},{2,0},{3,1},{4,6},{5,7},{6,4},{7,5},{8,10},{9,11},{10,... | collective-permute-start | bytes 786440 | tf_op jit(solution)/shard_map/ppermute | solution.py:29
  667.8 43.2 %collective-permute-start.57 = (bf16[128,1024]{1,0:T(8,128)(2,1)}, bf16[128,1024]{1,0:T(8,128)(2,1)S(1)}, u32[]{:S(2)}, u32[]{:S(2)}) collective-permute-start(bf16[128,1024]{1,0:T(8,128)(2,1)} %fusion.61), channel_id=1, source_target_pairs={{0,8},{1,9},{2,10},{3,11},{4,12},{5,13},{6,14},{7,15},{8,0},{9,1},... | collective-permute-start | bytes 786440 | tf_op jit(solution)/shard_map/ppermute | solution.py:29
  684.8 26.2 %collective-permute-start.55 = (bf16[128,1024]{1,0:T(8,128)(2,1)}, bf16[128,1024]{1,0:T(8,128)(2,1)}, u32[]{:S(2)}, u32[]{:S(2)}) collective-permute-start(bf16[128,1024]{1,0:T(8,128)(2,1)} %fusion.63), channel_id=1, source_target_pairs={{0,2},{1,3},{2,0},{3,1},{4,6},{5,7},{6,4},{7,5},{8,10},{9,11},{10,... | collective-permute-start | bytes 786440 | tf_op jit(solution)/shard_map/ppermute | solution.py:29
  694.2 33.0 %all-to-all-start.6 = ((bf16[8,64,768]{2,1,0:T(8,128)(2,1)}), bf16[8,64,768]{2,1,0:T(8,128)(2,1)}, u32[]{:S(2)}, u32[]{:S(2)}) async-start(bf16[8,64,768]{2,1,0:T(8,128)(2,1)} %bitcast.613), calls=%async_computation.6 | async-start | bytes 1572864 | tf_op jit(solution)/shard_map/all_to_all | solution.py:282
  726.6 25.1 %collective-permute-start.75 = (bf16[128,2048]{1,0:T(8,128)(2,1)}, bf16[128,2048]{1,0:T(8,128)(2,1)}, u32[]{:S(2)}, u32[]{:S(2)}) collective-permute-start(bf16[128,2048]{1,0:T(8,128)(2,1)} %collective-permute-done.74), channel_id=1, source_target_pairs={{0,1},{1,0},{2,3},{3,2},{4,5},{5,4},{6,7},{7,6},{8,9},{9,8},{10,11... | collective-permute-start | bytes 1572872 | tf_op jit(solution)/shard_map/ppermute | solution.py:29
  777.7 144.7 %collective-permute-start.122 = (bf16[273,1024]{1,0:T(8,128)(2,1)}, bf16[273,1024]{1,0:T(8,128)(2,1)}, u32[]{:S(2)}, u32[]{:S(2)}) collective-permute-start(bf16[273,1024]{1,0:T(8,128)(2,1)} %get-tuple-element.143), channel_id=1, source_target_pairs={{0,4},{1,5},{2,6},{3,7},{4,0},{5,1},{6,2},{7,3},{8,12},{9,13},{10,... | collective-permute-start | bytes 1677320 | tf_op jit(solution)/shard_map/ppermute | solution.py:29
  778.9 145.3 %collective-permute-start.124 = (bf16[273,1024]{1,0:T(8,128)(2,1)}, bf16[273,1024]{1,0:T(8,128)(2,1)}, u32[]{:S(2)}, u32[]{:S(2)}) collective-permute-start(bf16[273,1024]{1,0:T(8,128)(2,1)} %get-tuple-element.144), channel_id=1, source_target_pairs={{0,4},{4,0},{10,14},{14,10},{16,20},{20,16},{26,30},{30,26}} | collective-permute-start | bytes 1677320 | tf_op jit(solution)/shard_map/ppermute | solution.py:29
  788.9 137.3 %collective-permute-start.94 = (bf16[273,1024]{1,0:T(8,128)(2,1)}, bf16[273,1024]{1,0:T(8,128)(2,1)}, u32[]{:S(2)}, u32[]{:S(2)}) collective-permute-start(bf16[273,1024]{1,0:T(8,128)(2,1)} %get-tuple-element.145), channel_id=1, source_target_pairs={{0,4},{1,5},{2,6},{3,7},{4,0},{5,1},{6,2},{7,3},{8,12},{9,13},{10,... | collective-permute-start | bytes 1677320 | tf_op jit(solution)/shard_map/ppermute | solution.py:29
  830.1 27.1 %collective-permute-start.82 = (f32[2,3,546]{2,1,0:T(4,128)S(1)}, f32[2,3,546]{2,1,0:T(4,128)S(1)}, u32[]{:S(2)}, u32[]{:S(2)}) collective-permute-start(f32[2,3,546]{2,1,0:T(4,128)S(1)} %slice_multiply_fusion.4), channel_id=1, source_target_pairs={{0,4},{1,5},{2,6},{3,7},{4,0},{5,1},{6,2},{7,3},{8,12},{9,13},{10,... | collective-permute-start | bytes 39320 | tf_op jit(solution)/shard_map/ppermute | solution.py:29
  841.6 72.2 %collective-permute-start.102 = (bf16[277,546]{1,0:T(8,128)(2,1)}, bf16[277,546]{1,0:T(8,128)(2,1)}, u32[]{:S(2)}, u32[]{:S(2)}) collective-permute-start(bf16[277,546]{1,0:T(8,128)(2,1)} %pad_maximum_fusion.31), channel_id=1, source_target_pairs={{0,16},{1,17},{2,18},{3,19},{4,20},{5,21},{6,22},{7,23},{8,24},{9,... | collective-permute-start | bytes 907460 | tf_op jit(solution)/shard_map/ppermute | solution.py:29
  857.9 61.0 %collective-permute-start.112 = (bf16[277,546]{1,0:T(8,128)(2,1)}, bf16[277,546]{1,0:T(8,128)(2,1)}, u32[]{:S(2)}, u32[]{:S(2)}) collective-permute-start(bf16[277,546]{1,0:T(8,128)(2,1)} %pad_maximum_fusion.32), channel_id=1, source_target_pairs={{0,16},{4,20},{10,26},{14,30},{16,0},{20,4},{26,10},{30,14}} | collective-permute-start | bytes 907460 | tf_op jit(solution)/shard_map/ppermute | solution.py:29
  938.0 23.9 %collective-permute-start.95 = (bf16[273,512]{1,0:T(8,128)(2,1)}, bf16[273,512]{1,0:T(8,128)(2,1)}, u32[]{:S(2)}, u32[]{:S(2)}) collective-permute-start(bf16[273,512]{1,0:T(8,128)(2,1)} %slice.1837), channel_id=1, source_target_pairs={{0,16},{1,17},{2,18},{3,19},{4,20},{5,21},{6,22},{7,23},{8,24},{9,... | collective-permute-start | bytes 838664 | tf_op jit(solution)/shard_map/ppermute | solution.py:29
  956.9 64.4 %all-to-all-start.4 = ((bf16[8,64,546]{2,1,0:T(8,128)(2,1)}), bf16[8,64,546]{2,1,0:T(8,128)(2,1)}, u32[]{:S(2)}, u32[]{:S(2)}) async-start(bf16[8,64,546]{2,1,0:T(8,128)(2,1)} %bitcast.617), calls=%async_computation.4 | async-start | bytes 1310720 | tf_op jit(solution)/shard_map/all_to_all | solution.py:282
  965.9 24.8 %collective-permute-start.104 = (bf16[288,546]{1,0:T(8,128)(2,1)}, bf16[288,546]{1,0:T(8,128)(2,1)}, u32[]{:S(2)}, u32[]{:S(2)}) collective-permute-start(bf16[288,546]{1,0:T(8,128)(2,1)} %get-tuple-element.217), channel_id=1, source_target_pairs={{0,1},{1,0},{2,3},{3,2},{4,5},{5,4},{6,7},{7,6},{8,9},{9,8},{10,11... | collective-permute-start | bytes 943496 | tf_op jit(solution)/shard_map/ppermute | solution.py:29
  981.4 43.9 %collective-permute-start.84 = (bf16[512,2048]{1,0:T(8,128)(2,1)}, bf16[512,2048]{1,0:T(8,128)(2,1)}, u32[]{:S(2)}, u32[]{:S(2)}) collective-permute-start(bf16[512,2048]{1,0:T(8,128)(2,1)} %pad_maximum_fusion.10), channel_id=1, source_target_pairs={{0,1},{1,0},{2,3},{3,2},{4,5},{5,4},{6,7},{7,6},{8,9},{9,8},{10,11... | collective-permute-start | bytes 6291464 | tf_op jit(solution)/shard_map/ppermute | solution.py:29
  1021.3 38.5 %all-to-all-start.3 = ((bf16[8,2,64,546]{3,2,1,0:T(8,128)(2,1)}), bf16[8,2,64,546]{3,2,1,0:T(8,128)(2,1)S(1)}, u32[]{:S(2)}, u32[]{:S(2)}) async-start(bf16[8,2,64,546]{3,2,1,0:T(8,128)(2,1)} %copy.956), calls=%async_computation.3 | async-start | bytes 2621440 | tf_op jit(solution)/shard_map/all_to_all | solution.py:282
  1033.7 23.6 %collective-permute-start.85 = (bf16[256,1024]{1,0:T(8,128)(2,1)}, bf16[256,1024]{1,0:T(8,128)(2,1)}, u32[]{:S(2)}, u32[]{:S(2)}) collective-permute-start(bf16[256,1024]{1,0:T(8,128)(2,1)} %pad_maximum_fusion.29), channel_id=1, source_target_pairs={{0,8},{1,9},{2,10},{3,11},{4,12},{5,13},{6,14},{7,15},{8,0},{9,1},... | collective-permute-start | bytes 1572872 | tf_op jit(solution)/shard_map/ppermute | solution.py:29
  (269 other events, 4058.4 us)

commit v2 on v0

v2 whole, which is shorter than its diff:
```python
import functools

import jax
import jax.numpy as jnp
from jax import lax
from jax.experimental import pallas as pl
from jax.experimental.pallas import tpu as pltpu
from jax.sharding import PartitionSpec as P

AXIS = "seq"
ROOT_GUARD = 0.001
F32, BF16 = jnp.float32, jnp.bfloat16
SIDE = 8
XBIT, CBIT = 2, 1
EXTRA = {0: 8, 6: 9}
SLOT = 288
CW = 640
HALO = 16
SHORT_ROW = 2048
UNROLL = 4


def lbit(n):
    return 8 if n == 32 else 4


def far_masks(n):
    masks, m = [], n // 2
    while m >= 4:
        if m != lbit(n):
            masks.append(m)
        m //= 2
    return masks


def row_span(n, tok):
    return SHORT_ROW // tok if n * tok == 2 * SHORT_ROW else n


def side_mask(q, n):
    return (q & 1) * XBIT | ((q >> 1) & 1) * lbit(n) | ((q >> 2) & 1) * CBIT


def side_place(d, n):
    x = (d >> (XBIT.bit_length() - 1)) & 1
    l = (d >> (lbit(n).bit_length() - 1)) & 1
    return x + l * 2 + ((d >> (CBIT.bit_length() - 1)) & 1) * 4


def side_code(i, n):
    return (i & 3) | (((i & lbit(n)) != 0) * 4)


def side_groups(n):
    low = XBIT | CBIT | lbit(n)
    return [
        sorted(b | side_mask(q, n) for q in range(SIDE)) for b in range(n) if b & low == 0
    ]


def far_groups(n):
    low = XBIT | CBIT | lbit(n)
    return [[i for i in range(n) if i & low == side_mask(q, n)] for q in range(SIDE)]


def far_mask_of(r, n):
    return sum(m for k, m in enumerate(far_masks(n)) if (r >> k) & 1)


def near_units(n, me):
    low = 2 if lbit(n) == 8 else 3
    units = []
    for r in range(n // SIDE):
        for l in range(SIDE >> low):
            u = 0
            for k, m in enumerate(far_masks(n)):
                bit = lax.shift_right_logical(me, m.bit_length() - 1) & 1
                u = u + ((bit ^ ((r >> k) & 1)) << (m.bit_length() - 1 - low))
            units.append(u + (l << (lbit(n).bit_length() - 1 - low) if low == 2 else 0))
    return units


def fixed_units(n):
    low = 2 if lbit(n) == 8 else 3
    base = [g[0] for g in side_groups(n)]
    return [
        (b | (l * lbit(n) if low == 2 else 0)) >> low for b in base for l in range(SIDE >> low)
    ]


def swap(v, mask, only=None):
    n = lax.axis_size(AXIS)
    pairs = [(i, i ^ mask) for i in range(n) if only is None or side_code(i, n) in only]
    return lax.ppermute(v, AXIS, pairs)


def dot(a, b):
    return lax.dot_general(a, b, (((1,), (0,)), ((), ())), preferred_element_type=F32)


def dot_last(a, b):
    return lax.dot_general(a, b, (((1,), (1,)), ((), ())), preferred_element_type=F32)


def dot_first(a, b):
    return lax.dot_general(a, b, (((0,), (0,)), ((), ())), preferred_element_type=F32)


def after(v, *deps):
    return lax.optimization_barrier((v, *deps))[0]


def kernel_call(kernel, ins, outs, scratch=(), smem=1, us=3):
    specs = [pl.BlockSpec(memory_space=pltpu.SMEM)] * smem
    specs += [pl.BlockSpec(memory_space=pltpu.VMEM)] * (len(ins) - smem)
    return pl.pallas_call(
        kernel,
        in_specs=specs,
        out_specs=[pl.BlockSpec(memory_space=pltpu.VMEM)] * len(outs),
        out_shape=[jax.ShapeDtypeStruct(s, d) for s, d in outs],
        scratch_shapes=list(scratch),
        compiler_params=pltpu.CompilerParams(vmem_limit_bytes=60 * 1024 * 1024),
        cost_estimate=pl.CostEstimate(
            flops=us * 10**9, bytes_accessed=us * 3 * 10**6, transcendentals=0
        ),
    )(*ins)


def gather_side(x, main=None, marks=(None, None)):
    n = lax.axis_size(AXIS)
    half = x.shape[0] // 32 * 16
    by_l, by_x = swap(x, lbit(n)), swap(x, XBIT)
    if marks[0] is not None:
        by_l, by_x = after((by_l, by_x), marks[0])
    low, high = swap(by_l[:half], XBIT), swap(by_x[half:], lbit(n))
    if marks[1] is not None:
        low, high = after((low, high), marks[1])
    if main is None:
        mine = jnp.concatenate([x, by_x, by_l, low, high])
        return mine, swap(mine, CBIT)
    cut = main - half
    mine = jnp.concatenate([x[:main], by_x[:main], by_l[:main], low, high[:cut]])
    rest = jnp.concatenate([x[main:], by_x[main:], by_l[main:], high[cut:]])
    return mine, swap(mine, CBIT), rest, swap(rest, CBIT)


def first_sum_kernel(mine, recv, send_a, send_b, keep_a, keep_b):
    tok, half = mine.shape[0] // 4, mine.shape[1] // 2
    step = 16

    def tile(i, _):
        for b in range(4):
            rows = pl.ds(pl.multiple_of(b * tok + i * step, step), step)
            at = lambda k: pl.ds(pl.multiple_of(k * tok + i * step, step), step)
            va = mine[rows, :half] + recv[rows, :half].astype(F32)
            vb = mine[rows, half:] + recv[rows, half:].astype(F32)
            if b < 2:
                keep_a[at(b), :] = va
            else:
                send_a[at(b - 2), :] = va.astype(BF16)
            if b % 2 == 0:
                keep_b[at(b // 2), :] = vb
            else:
                send_b[at(b // 2), :] = vb.astype(BF16)
        return 0

    lax.fori_loop(0, tok // step, tile, 0)


def second_sum_kernel(keep_a, recv_a, keep_b, recv_b, send_a, send_b, last):
    tok, half = send_a.shape
    step = 16

    def tile(i, _):
        own = pl.ds(pl.multiple_of(i * step, step), step)
        far = pl.ds(pl.multiple_of(tok + i * step, step), step)
        last[own, :half] = keep_a[own, :] + recv_a[own, :].astype(F32)
        last[own, half:] = keep_b[own, :] + recv_b[own, :].astype(F32)
        send_a[own, :] = (keep_a[far, :] + recv_a[far, :].astype(F32)).astype(BF16)
        send_b[own, :] = (keep_b[far, :] + recv_b[far, :].astype(F32)).astype(BF16)
        return 0

    lax.fori_loop(0, tok // step, tile, 0)


def scatter_side(mine, theirs, mark=None, mark_last=None):
    n = lax.axis_size(AXIS)
    rows, width = mine.shape
    tok, half = rows // 4, width // 2
    recv = swap(theirs, CBIT)
    send_a, send_b, keep_a, keep_b = kernel_call(
        first_sum_kernel,
        (mine, recv),
        [((2 * tok, half), BF16)] * 2 + [((2 * tok, half), F32)] * 2,
        smem=0,
    )
    recv_a, recv_b = swap(send_a, lbit(n)), swap(send_b, XBIT)
    if mark is not None:
        keep_a = after(keep_a, mark)
    send_a, send_b, last = kernel_call(
        second_sum_kernel,
        (keep_a, recv_a, keep_b, recv_b),
        [((tok, half), BF16)] * 2 + [((tok, width), F32)],
        smem=0,
    )
    parts = (last, swap(send_a, XBIT), swap(send_b, lbit(n)))
    if mark_last is not None:
        parts = after(parts, mark_last)
    return parts, keep_a, last


def rms_scale(values):
    return lax.rsqrt(jnp.mean(values * values, axis=-1, keepdims=True) + 1e-06)


def unit_slice(u, size):
    return pl.ds(pl.multiple_of(u * size, 128), size)


def put_units(out, rows, value_ref, value_rows, units, size):
    for p, u in enumerate(units):
        out[rows, p * size : (p + 1) * size] = value_ref[value_rows, unit_slice(u, size)]


def tail_kernel(x, gain, flags, out):
    v = x[...]
    out[...] = (v * rms_scale(v) * gain[...]).astype(BF16)
    row = lax.broadcasted_iota(jnp.int32, (HALO, 128), 0) == 0
    out[:, :128] = jnp.where(row, flags[...], out[:, :128].astype(F32)).astype(BF16)


ROWS = 32


def norm_one_kernel(n, me, x, gain, flags, tail, out, held):
    units = near_units(n, me[0])
    size = x.shape[1] // len(units)
    tok = x.shape[0]
    for i in range(tok // ROWS):
        rows = slice(i * ROWS, (i + 1) * ROWS)
        v = x[rows, :]
        held[...] = v * rms_scale(v) * gain[...]
        for p, u in enumerate(units):
            out[rows, p * size : (p + 1) * size] = held[:, unit_slice(u, size)].astype(BF16)
    halo = slice(tok, tok + HALO)
    put_units(out, halo, tail, slice(0, HALO), units, size)
    row = lax.broadcasted_iota(jnp.int32, (HALO, 128), 0)
    first = out[halo, :128].astype(F32)
    both = jnp.where(row == 0, flags[...], first)
    both = jnp.where(row == 1, tail[:, :128].astype(F32)[0:1], both)
    out[halo, :128] = both.astype(BF16)


def top_kernel(n, g, out):
    units = fixed_units(n)
    size = g.shape[1] // len(units)
    for p, u in enumerate(units):
        out[:, p * size : (p + 1) * size] = g[:, u * size : (u + 1) * size].astype(BF16)


def summed(last, ra, rb, rows, p, size):
    half = ra.shape[1]
    a, b = p * size, (p + 1) * size
    if b <= half:
        extra = ra[rows, a:b]
    else:
        extra = rb[rows, a - half : b - half]
    return last[rows, a:b] + extra.astype(F32)


def norm_two_kernel(n, me, x, gain, last, ra, rb, middle, out, held):
    units = near_units(n, me[0])
    size = x.shape[1] // len(units)
    for i in range(x.shape[0] // ROWS):
        rows = slice(i * ROWS, (i + 1) * ROWS)
        for p, u in enumerate(units):
            held[:, unit_slice(u, size)] = summed(last, ra, rb, rows, p, size)
        v = held[...] + x[rows, :]
        middle[rows, :] = v
        w = (v * rms_scale(v) * gain[...]).astype(BF16)
        for p, u in enumerate(fixed_units(n)):
            out[rows, p * size : (p + 1) * size] = w[:, u * size : (u + 1) * size]


def add_kernel(n, middle, last, ra, rb, out):
    units = fixed_units(n)
    size = middle.shape[1] // len(units)
    for p, u in enumerate(units):
        at = slice(u * size, (u + 1) * size)
        out[:, at] = middle[:, at] + summed(last, ra, rb, slice(None), p, size)


def norm_back(grad_normed, values, gain):
    scale = rms_scale(values)
    scaled = grad_normed * gain
    back = scale * scaled - values * (scale * scale * scale) * jnp.mean(
        scaled * values, axis=-1, keepdims=True
    )
    return back, grad_normed * values * scale


def middle_back_kernel(n, me, values, base, gain, last, ra, rb, grad, branch, gain_grad, held):
    units = near_units(n, me[0])
    size = values.shape[1] // len(units)
    total = jnp.zeros((1, values.shape[1]), F32)
    for i in range(values.shape[0] // ROWS):
        rows = slice(i * ROWS, (i + 1) * ROWS)
        for p, u in enumerate(fixed_units(n)):
            held[:, u * size : (u + 1) * size] = summed(last, ra, rb, rows, p, size)
        back, part = norm_back(held[...], values[rows, :], gain[...])
        total = total + jnp.sum(part, axis=0, keepdims=True)
        out = base[rows, :] + back
        grad[rows, :] = out
        held[...] = out
        for p, u in enumerate(units):
            branch[rows, p * size : (p + 1) * size] = held[:, unit_slice(u, size)].astype(BF16)
    gain_grad[...] = total


def input_back_kernel(n, me, values, base, gain, last, ra, rb, grad, gain_grad, held):
    units = near_units(n, me[0])
    size = values.shape[1] // len(units)
    total = jnp.zeros((1, values.shape[1]), F32)
    for i in range(values.shape[0] // ROWS):
        rows = slice(i * ROWS, (i + 1) * ROWS)
        for p, u in enumerate(units):
            held[:, unit_slice(u, size)] = summed(last, ra, rb, rows, p, size)
        back, part = norm_back(held[...], values[rows, :], gain[...])
        total = total + jnp.sum(part, axis=0, keepdims=True)
        grad[rows, :] = base[rows, :] + back
    gain_grad[...] = total


def gelu_pair(v):
    k = 0.7978845608028654
    sq = v * v
    th = jnp.tanh(k * v * (1.0 + 0.044715 * sq))
    half = 0.5 * (1.0 + th)
    slope = half + 0.5 * v * (1.0 - th * th) * (k * (1.0 + 3.0 * 0.044715 * sq))
    return v * half, slope


def strided(i, tok):
    return pl.ds(i, SIDE, stride=tok)


TILES = CW // 128


def cols(c):
    return slice(c * 128, (c + 1) * 128)


def join(tiles):
    return jnp.concatenate(tiles, axis=1)


def stepwise(tok, step, state, reverse=False):
    def some(o, state):
        for k in range(UNROLL):
            i = o * UNROLL + k
            state = step(tok - 1 - i if reverse else i, state)
        return state

    return lax.fori_loop(0, tok // UNROLL, some, state)


def step_rows(i):
    return pl.ds(pl.multiple_of(i * SIDE, SIDE), SIDE)


def mixer_kernel(
    lin_mine, lin_theirs, halo, keep, halo_keep, taps, r_sq, i_sq, vec,
    lin, low, rg, ig, dec, acc, loc, before, totals, conv,
):
    tok = conv.shape[1] // SIDE
    four = 4 * tok
    for c in range(TILES):
        lin[c, :four, :] = lin_mine[:, CW + c * 128 : CW + (c + 1) * 128]
        lin[c, four:, :] = lin_theirs[:, CW + c * 128 : CW + (c + 1) * 128]
        conv[c, : SIDE * HALO, :] = halo[:, cols(c)]
        for k in range(3):
            before[c, k * SIDE : (k + 1) * SIDE, :] = conv[c, strided(HALO - 1 - k, HALO), :]

    for c in range(TILES):
        t0, t1, t2, t3 = (taps[k : k + 1, cols(c)] for k in range(4))
        bias = vec[0:1, cols(c)]

        def conv_step(i, state):
            v1, v2, v3, k1, k2 = state
            v0 = lin[c, strided(i, tok), :]
            k0 = keep[step_rows(i), :]
            conv[c, strided(i, tok), :] = (
                v0 * t0 + bias + k0 * (v1 * t1 + k1 * (v2 * t2 + k2 * (v3 * t3)))
            )
            return v0, v1, v2, k0, k1

        start = tuple(before[c, k * SIDE : (k + 1) * SIDE, :] for k in range(3))
        start += (halo_keep[2 * SIDE :, :], halo_keep[SIDE : 2 * SIDE, :])
        stepwise(tok, conv_step, start)

    def gates(b, _):
        rows = pl.ds(pl.multiple_of(b * tok, tok), tok)
        low_here = join([conv[c, rows, :].astype(BF16) for c in range(TILES)])
        low[rows, :] = low_here
        r = jax.nn.sigmoid(dot(low_here, r_sq[...]) + vec[1:2, :])
        i = jax.nn.sigmoid(dot(low_here, i_sq[...]) + vec[2:3, :])
        for c in range(TILES):
            conv[c, rows, :] = low_here[:, cols(c)].astype(F32)
            rg[c, rows, :] = r[:, cols(c)]
            ig[c, rows, :] = i[:, cols(c)]
        return 0

    lax.fori_loop(0, SIDE, gates, 0)

    def scan_step(i, state):
        at = strided(i, tok)
        k0 = keep[step_rows(i), :]
        out = []
        for c in range(TILES):
            p, s = state[c]
            a = jnp.exp(rg[c, at, :] * vec[3:4, cols(c)]) * k0
            root = jnp.sqrt(1.0 - a * a + ROOT_GUARD)
            b = (k0 * root + (1.0 - k0)) * ig[c, at, :] * conv[c, at, :]
            p, s = p * a, a * s + b
            dec[c, at, :] = a
            acc[c, at, :] = p
            loc[c, at, :] = s
            out.append((p, s))
        return tuple(out)

    shape = (SIDE, 128)
    start = tuple((jnp.ones(shape, F32), jnp.zeros(shape, F32)) for _ in range(TILES))
    found = stepwise(tok, scan_step, start)
    for c in range(TILES):
        totals[:SIDE, cols(c)], totals[SIDE:, cols(c)] = found[c]


def gelu_kernel(gate_mine, gate_theirs, act, slope):
    four = gate_mine.shape[0]

    def tile(i, _):
        rows = pl.ds(pl.multiple_of(i * 16, 16), 16)
        later = pl.ds(pl.multiple_of(four + i * 16, 16), 16)
        for src, dst in ((gate_mine, rows), (gate_theirs, later)):
            for c in range(TILES):
                act[c, dst, :], slope[c, dst, :] = gelu_pair(src[rows, cols(c)])
        return 0

    lax.fori_loop(0, four // 16, tile, 0)


def chain_kernel(n, span, reverse, me_ref, *refs):
    *parts, out, held = refs
    me = me_ref[0]
    state = jnp.zeros((1, CW), F32)
    order = range(span - 1, -1, -1) if reverse else range(span)
    near = [m for m in far_masks(n) if m < span]

    def place(d):
        r = 0
        for k, m in enumerate(near):
            r = r + (((d >> (m.bit_length() - 1)) & 1) << k)
        return r, side_place(d, n)

    both = 2 * SIDE
    for r, part in enumerate(parts):
        for k in range(both):
            held[r * both + k, 0:1, :] = part[k : k + 1, :]
    base = len(parts) * both
    for i in order:
        r, q = place((me & (span - 1)) ^ i)
        held[base + i, 0:1, :] = state
        scale = held[r * both + q, 0:1, :]
        value = held[r * both + SIDE + q, 0:1, :]
        state = scale * state + value
    for q in range(SIDE):
        at = base + ((me & (span - 1)) ^ side_mask(q, n))
        out[q, :, :] = jnp.broadcast_to(held[at, 0:1, :], (8, CW))


def states_kernel(acc, loc, incoming, act, slope, states, mixed, slope_states):
    tok = acc.shape[1] // SIDE
    for q in range(SIDE):

        def tile(i, _):
            rows = pl.ds(pl.multiple_of(q * tok + i * 16, 16), 16)
            out = []
            for c in range(TILES):
                s = loc[c, rows, :] + acc[c, rows, :] * incoming[q, 0:1, cols(c)]
                states[c, rows, :] = s
                slope_states[c, rows, :] = s * slope[c, rows, :]
                out.append((s * act[c, rows, :]).astype(BF16))
            mixed[rows, :] = join(out)
            return 0

        lax.fori_loop(0, tok // 16, tile, 0)


def back_scan_kernel(gm_mine, gm_theirs, act, dec, grads, suffix, totals):
    tok = act.shape[1] // SIDE
    four = 4 * tok
    for c in range(TILES):
        grads[c, :four, :] = gm_mine[:, cols(c)] * act[c, :four, :]
        grads[c, four:, :] = gm_theirs[:, cols(c)] * act[c, four:, :]

    def step(i, state):
        at = strided(i, tok)
        out = []
        for c in range(TILES):
            ag, aq = state[c]
            g = grads[c, at, :] + ag
            grads[c, at, :] = g
            suffix[c, at, :] = aq
            a = dec[c, at, :]
            out.append((a * g, a * aq))
        return tuple(out)

    shape = (SIDE, 128)
    start = tuple((jnp.zeros(shape, F32), jnp.ones(shape, F32)) for _ in range(TILES))
    found = stepwise(tok, step, start, True)
    for c in range(TILES):
        totals[SIDE:, cols(c)], totals[:SIDE, cols(c)] = found[c]


def gate_back_kernel(gm_mine, gm_theirs, slope_states, out):
    four = gm_mine.shape[0]

    def tile(i, _):
        rows = pl.ds(pl.multiple_of(i * 16, 16), 16)
        later = pl.ds(pl.multiple_of(four + i * 16, 16), 16)
        for src, dst in ((gm_mine, rows), (gm_theirs, later)):
            out[dst, :] = join(
                [(src[rows, cols(c)] * slope_states[c, dst, :]).astype(BF16) for c in range(TILES)]
            )
        return 0

    lax.fori_loop(0, four // 16, tile, 0)


def mixer_back_kernel(
    grads, suffix, from_later, dec, rg, ig, low, states, incoming, lin, before, keep, halo_keep,
    keep_rows, r_sq, i_sq, vec, g_reset, g_input, g_conv, sums, heads,
):
    tok = dec.shape[1] // SIDE
    zero = jnp.zeros((1, 128), F32)

    def block(b, totals):
        rows = pl.ds(pl.multiple_of(b * tok, tok), tok)
        k = keep_rows[rows, :]
        at_first = lax.broadcasted_iota(jnp.int32, (tok, 128), 0) == 0
        out, g_rs, g_is, base = [], [], [], []
        for c in range(TILES):
            gs = grads[c, rows, :] + suffix[c, rows, :] * from_later[b, 0:1, cols(c)]
            a, r, i_g = dec[c, rows, :], rg[c, rows, :], ig[c, rows, :]
            v = low[rows, cols(c)].astype(F32)
            root = jnp.sqrt(1.0 - a * a + ROOT_GUARD)
            mult = k * root + (1.0 - k)
            prior = pltpu.roll(states[c, rows, :], 1, 0)
            prior = jnp.where(at_first, incoming[b, 0:1, cols(c)], prior)
            gv = gs * v
            glr = a * (gs * prior - gv * i_g * a / root) * r
            g_r = (vec[3:4, cols(c)] * glr * (1.0 - r)).astype(BF16)
            gm = gs * mult * i_g
            g_i = (gm * v * (1.0 - i_g)).astype(BF16)
            out.append(
                (
                    totals[c][0] + jnp.sum(glr, axis=0, keepdims=True),
                    totals[c][1] + jnp.sum(g_r.astype(F32), axis=0, keepdims=True),
                    totals[c][2] + jnp.sum(g_i.astype(F32), axis=0, keepdims=True),
                )
            )
            g_rs.append(g_r)
            g_is.append(g_i)
            g_conv[c, rows, :] = gm
        g_r, g_i = join(g_rs), join(g_is)
        g_reset[rows, :] = g_r
        g_input[rows, :] = g_i
        more = dot_last(g_r, r_sq[...]) + dot_last(g_i, i_sq[...])
        for c in range(TILES):
            g_conv[c, rows, :] = g_conv[c, rows, :] + more[:, cols(c)]
        return tuple(out)

    found = lax.fori_loop(0, SIDE, block, ((zero,) * 3,) * TILES)
    for c in range(TILES):
        dec_sum, r_sum, i_sum = found[c]
        sums[0:1, cols(c)] = r_sum
        sums[1:2, cols(c)] = i_sum
        sums[2:3, cols(c)] = -vec[4:5, cols(c)] * dec_sum

    blank = jnp.zeros((SIDE, 128), F32)
    for c in range(TILES):

        def tap_step(i, state):
            v1, v2, v3, k1, k2, s0, s1, s2, s3, sb = state
            v0 = lin[c, strided(i, tok), :]
            k0 = keep[step_rows(i), :]
            g0 = g_conv[c, strided(i, tok), :]
            g1 = g0 * k0
            g2 = g1 * k1
            g3 = g2 * k2
            return (
                (v0, v1, v2, k0, k1)
                + (s0 + g0 * v0, s1 + g1 * v1, s2 + g2 * v2, s3 + g3 * v3, sb + g0)
            )

        start = tuple(before[c, k * SIDE : (k + 1) * SIDE, :] for k in range(3))
        start += (halo_keep[2 * SIDE :, :], halo_keep[SIDE : 2 * SIDE, :]) + (blank,) * 5
        end = stepwise(tok, tap_step, start)
        per_row = [jnp.sum(v, axis=0, keepdims=True) for v in end[5:]]
        sums[3:4, cols(c)] = per_row[4]
        for j in range(4):
            sums[4 + j : 5 + j, cols(c)] = per_row[j]
        k = None
        for i in range(3):
            k_i = keep[i * SIDE : (i + 1) * SIDE, :]
            k = k_i if k is None else k * k_i
            heads[i * SIDE : (i + 1) * SIDE, cols(c)] = g_conv[c, strided(i, tok), :] * k


def linear_back_kernel(n, span, me_ref, g_conv, keep, taps, *refs):
    *parts, out, held, after, conv = refs
    me = me_ref[0]
    tok = g_conv.shape[1] // SIDE
    rows3 = 3 * SIDE
    for k, part in enumerate(parts):
        for m in range(rows3):
            held[k * rows3 + m, 0:1, :] = part[m : m + 1, :]
    low_far = far_masks(n)[-1]
    side = XBIT | CBIT | lbit(n)
    for q in range(SIDE):
        nxt = (me ^ side_mask(q, n)) + 1
        d = nxt ^ me
        far = d & ~side
        ok = ((nxt & (span - 1)) != 0).astype(F32)
        which = jnp.where(far == 0, 0, jnp.where(far == low_far, 1, len(parts) - 1))
        for m in range(3):
            at = which * rows3 + m * SIDE + side_place(d, n)
            after[m * SIDE + q : m * SIDE + q + 1, :] = held[at, 0:1, :] * ok
    one = jnp.ones((SIDE, 128), F32)
    for c in range(TILES):
        t0, t1, t2, t3 = (taps[k : k + 1, cols(c)] for k in range(4))

        def step(i, state):
            g1, g2, g3, k1, k2, k3 = state
            g0 = g_conv[c, strided(i, tok), :]
            conv[c, strided(i, tok), :] = g0 * t0 + k1 * (g1 * t1 + k2 * (g2 * t2 + k3 * (g3 * t3)))
            return g0, g1, g2, keep[step_rows(i), :], k1, k2

        start = tuple(after[m * SIDE : (m + 1) * SIDE, cols(c)] for m in range(3))
        stepwise(tok, step, start + (one, one, one), True)

    def tile(i, _):
        rows = pl.ds(pl.multiple_of(i * 16, 16), 16)
        out[rows, :] = join([conv[c, rows, :].astype(BF16) for c in range(TILES)])
        return 0

    lax.fori_loop(0, SIDE * tok // 16, tile, 0)


def heads_kernel(blk, gate, linear, out_w, first, second):
    first[...] = jnp.zeros(first.shape, BF16)
    second[...] = jnp.zeros(second.shape, BF16)
    for k, w in enumerate((gate, linear, out_w)):
        at = slice(k * SLOT, k * SLOT + blk)
        for s in range(SIDE):
            first[s, :, at] = w[:, s * blk : (s + 1) * blk]
        for s, e in EXTRA.items():
            second[s, :, at] = w[:, e * blk : (e + 1) * blk]


def feed_parts_kernel(*refs):
    *weights, out = refs
    rows, size = weights[0].shape[0], out.shape[2]
    for k, w in enumerate(weights):
        for s in range(SIDE):
            out[s, k * rows : (k + 1) * rows, :] = w[:, s * size : (s + 1) * size]


def feed_join_kernel(parts, out):
    size = parts.shape[2]
    for s in range(SIDE):
        out[:, s * size : (s + 1) * size] = parts[s, :, :].astype(F32)


def turn_kernel(parts, *outs):
    rows = parts.shape[1]
    turned = parts[...].reshape(SIDE * rows, parts.shape[2]).T
    at = 0
    for out in outs:
        out[...] = turned[at : at + out.shape[0]]
        at += out.shape[0]


def assemble_kernel(count, which, *refs):
    first, extra, out = refs[:count], refs[count : 2 * count], refs[2 * count]
    size = first[0].shape[1]
    for r in range(count):
        lanes = slice(r * size, (r + 1) * size)
        for m, k in enumerate(which):
            out[m * CW : m * CW + SLOT, lanes] = first[r][m * SLOT : (m + 1) * SLOT, :]
            out[m * CW + SLOT : m * CW + 2 * SLOT, lanes] = extra[r][k * SLOT : (k + 1) * SLOT, :]
            out[m * CW + 2 * SLOT : (m + 1) * CW, lanes] = jnp.zeros((CW - 2 * SLOT, size), BF16)


def turn_back_kernel(*refs):
    *parts, out = refs
    rows = out.shape[1]
    flat = jnp.concatenate([p[...] for p in parts])
    out[:, :, : flat.shape[0]] = flat.T.reshape(SIDE, rows, flat.shape[0])


def head_rows_kernel(blk, parts, *outs):
    count = len(outs)
    for k, out in enumerate(outs):
        for s in range(SIDE):
            at = k * SLOT
            out[:, s * blk : (s + 1) * blk] = parts[s, :, at : at + blk].astype(F32)
        for s, e in EXTRA.items():
            at = (count + k) * SLOT
            out[:, e * blk : (e + 1) * blk] = parts[s, :, at : at + blk].astype(F32)


def packs_kernel(n, blk, me_ref, mine, theirs, eight, nine, r_out, i_out, vec_out):
    me = me_ref[0]

    def put(ref, e, shift):
        def lanes(v):
            return v[:, shift : shift + blk]

        r_out[e, :, :] = lanes(ref[:SLOT, :384].astype(F32))[:blk]
        i_out[e, :, :] = lanes(ref[:SLOT, 384:].astype(F32))[:blk]
        vec_out[:, e * blk : (e + 1) * blk] = lanes(ref[SLOT:, :384].astype(F32)[:8])

    for s in range(SIDE):
        i = (s & 3) | ((s >> 2) * lbit(n))
        d = jnp.int32(i) ^ (me & (XBIT | CBIT | lbit(n)))
        q = ((d >> (XBIT.bit_length() - 1)) & 1) + ((d >> (lbit(n).bit_length() - 1)) & 1) * 2
        own = ((d >> (CBIT.bit_length() - 1)) & 1) == 0

        @pl.when(own)
        def _():
            put(mine.at[q], s, 0)

        @pl.when(jnp.logical_not(own))
        def _():
            put(theirs.at[q], s, 0)

    put(eight, EXTRA[0], 32)
    put(nine, EXTRA[6], 32)


def body(
    block_input,
    start_flags,
    norm_gain,
    gate_weight,
    linear_weight,
    conv_taps,
    conv_bias,
    reset_weight,
    reset_bias,
    input_weight,
    input_bias,
    decay_param,
    out_weight,
    feed_norm_gain,
    feed_gate_weight,
    feed_value_weight,
    feed_down_weight,
    output_grad,
):
    n = lax.axis_size(AXIS)
    me = lax.axis_index(AXIS)
    me1 = me.reshape(1)
    here = side_code(me, n)
    tok, width = block_input.shape
    heads_count, blk = reset_weight.shape[:2]
    rows_w = gate_weight.shape[0]
    feed = feed_gate_weight.shape[1]
    fs = feed // SIDE
    masks = far_masks(n)
    groups, far = side_groups(n), far_groups(n)
    only = tuple(EXTRA)
    has_extra = (here == only[0]) | (here == only[1])
    extra_here = jnp.where(here == only[1], EXTRA[only[1]], EXTRA[only[0]])
    four = 4 * tok
    side_tok = SIDE * tok
    cols_w = SIDE * rows_w
    places = n // SIDE
    count = len(masks)

    def exchange(v):
        return lax.all_to_all(v, AXIS, 0, 0, axis_index_groups=groups, tiled=True)

    def gather_far(x, sel=None):
        chunks = [x]
        for m in masks:
            chunks += [swap(c, m, sel) for c in chunks]
        return chunks

    gain_one = norm_gain.astype(F32)[None]
    gain_two = feed_norm_gain.astype(F32)[None]
    flags = start_flags.astype(F32)[None]
    parts, more_parts = kernel_call(
        functools.partial(heads_kernel, blk),
        (gate_weight, linear_weight, out_weight),
        [((SIDE, rows_w, 3 * SLOT + 32), BF16)] * 2,
        smem=0,
    )
    tail = kernel_call(
        tail_kernel,
        (after(block_input[-HALO:], parts), gain_one, flags),
        [((HALO, width), BF16)],
        smem=0,
        us=1,
    )[0]
    tail = lax.ppermute(tail, AXIS, [(i, i + 1) for i in range(n - 1)])
    packet = kernel_call(
        functools.partial(norm_one_kernel, n),
        (me1, block_input, gain_one, flags, tail),
        [((tok + HALO, width), BF16)],
        [pltpu.VMEM((ROWS, width), F32)],
    )[0]
    f_parts = kernel_call(
        feed_parts_kernel,
        (after(feed_gate_weight, packet), feed_value_weight, feed_down_weight),
        [((SIDE, 3 * rows_w, fs), BF16)],
        smem=0,
    )[0]
    top = kernel_call(
        functools.partial(top_kernel, n),
        (after(output_grad, f_parts),),
        [((tok, width), BF16)],
        smem=0,
    )[0]
    parts = exchange(parts)
    p_mix, p_out = kernel_call(
        turn_kernel, (parts,), [((k * SLOT, cols_w), BF16) for k in (2, 1)], smem=0
    )
    more_parts = exchange(after(more_parts, parts))
    f_parts = exchange(after(f_parts, more_parts))
    p_extra = kernel_call(turn_kernel, (more_parts,), [((3 * SLOT, cols_w), BF16)], smem=0)[0]

    def gather_start(x, count=2, sel=None):
        return [x] + [swap(x, m, sel) for m in masks[:count]]

    def gather_later(chunks, sel=None, mark=None):
        chunks = list(chunks)
        if mark is not None:
            chunks[1] = after(chunks[1], mark)
        if len(chunks) == 3:
            chunks.append(swap(chunks[1], masks[1], sel))
        for m in masks[len(chunks).bit_length() - 1 :]:
            chunks += [swap(c, m, sel) for c in chunks]
        return chunks

    packet = after(packet, p_mix)
    c_mix = gather_start(p_mix)
    half = tok // 2
    by_l, by_x = swap(packet, lbit(n)), swap(packet, XBIT)
    (c_mix, by_l, by_x, p_extra) = lax.optimization_barrier((c_mix, by_l, by_x, p_extra))
    c_mix = gather_later(c_mix)
    c_extra = gather_start(p_extra, 1, only)
    low, high = swap(by_l[:half], XBIT), swap(by_x[half:], lbit(n))
    (c_mix, c_extra, low, high, p_out) = lax.optimization_barrier(
        (c_mix, c_extra, low, high, p_out)
    )
    f_parts = after(f_parts, c_extra)
    c_extra = gather_later(c_extra, only)
    c_out = gather_start(p_out, 1)
    f_parts = f_parts.reshape(SIDE, 3, rows_w, fs)
    norm_mine = jnp.concatenate([packet[:tok], by_x[:tok], by_l[:tok], low, high[:half]])
    halo_mine = jnp.concatenate([packet[tok:], by_x[tok:], by_l[tok:], high[half:]])
    norm_theirs, halo_theirs = swap(norm_mine, CBIT), swap(halo_mine, CBIT)
    f_parts = [f_parts[:, k].reshape(cols_w, fs) for k in range(3)]
    w_mix = kernel_call(
        functools.partial(assemble_kernel, places, (0, 1)),
        (*c_mix, *c_extra),
        [((2 * CW, width), BF16)],
        smem=0,
        us=5,
    )[0]
    c_out = gather_later([after(p_out, w_mix), c_out[1]], mark=w_mix)
    w_mix = after(w_mix, tuple(f_parts))

    def feed_full(part):
        return lax.all_gather(part, AXIS, axis_index_groups=far, tiled=True)

    w_down, w_gate, w_value = (feed_full(f_parts[k]) for k in (2, 0, 1))

    def pick(p):
        one = lax.dynamic_index_in_dim(p, here, 0, False)
        two = lax.dynamic_index_in_dim(p, extra_here, 0, False)
        return one, jnp.where(has_extra, two, jnp.zeros_like(two))

    vectors = jnp.concatenate(
        [conv_taps]
        + [v[None] for v in (conv_bias, reset_bias, input_bias, decay_param)]
    ).astype(F32)
    vectors = vectors.reshape(8, heads_count, blk).transpose(1, 0, 2)
    vec_one, vec_two = pick(vectors)
    gap = ((0, 0), (0, SLOT - blk))
    vectors = jnp.concatenate([jnp.pad(vec_one, gap), jnp.pad(vec_two, gap)], axis=1)
    vectors = jnp.pad(vectors, ((0, 0), (0, CW - 2 * SLOT)))
    taps = vectors[:4]
    decay_float = vectors[7]
    vec = jnp.concatenate(
        [
            vectors[4:7],
            (-8.0 * jax.nn.softplus(-decay_float))[None],
            (-8.0 * jax.nn.sigmoid(-decay_float))[None],
            jnp.zeros((3, CW), F32),
        ]
    )

    def square(p):
        one, two = pick(p)
        low = CW - SLOT - blk
        return jnp.pad(one, ((0, CW - blk),) * 2) + jnp.pad(two, ((SLOT, low),) * 2)

    r_sq, i_sq = square(reset_weight), square(input_weight)

    halo_all = jnp.concatenate([halo_mine, halo_theirs])
    flag_rows = halo_all.reshape(SIDE, HALO, width)[:, :2, :128].astype(F32)
    keep_blocks = 1.0 - flag_rows[:, 0]
    keep = jnp.broadcast_to(keep_blocks.T[:, :, None], (tok, SIDE, 128)).reshape(side_tok, 128)
    keep_rows = jnp.broadcast_to(keep_blocks[:, :, None], (SIDE, tok, 128)).reshape(side_tok, 128)
    halo_keep = 1.0 - flag_rows[:, 1, tok - 3 :]
    halo_keep = jnp.broadcast_to(halo_keep.T[:, :, None], (3, SIDE, 128)).reshape(3 * SIDE, 128)

    pre_mine, pre_theirs = dot_last(norm_mine, w_mix), dot_last(norm_theirs, w_mix)
    halo = dot_last(halo_all, w_mix[CW:])
    top = after(top, w_mix)
    top_l, top_x = swap(top, lbit(n)), swap(top, XBIT)
    flat, wide = (side_tok, CW), (TILES, side_tok, 128)
    lin, low, rg, ig, dec, acc, loc, before, totals = kernel_call(
        mixer_kernel,
        (pre_mine, pre_theirs, halo, keep, halo_keep, taps, r_sq, i_sq, vec),
        [(wide, F32), (flat, BF16)]
        + [(wide, F32)] * 5
        + [((TILES, 3 * SIDE, 128), F32), ((2 * SIDE, CW), F32)],
        [pltpu.VMEM(wide, F32)],
        smem=0,
        us=29,
    )

    span = row_span(n, tok)

    def chain(totals, reverse, mark):
        near = [far_mask_of(r, n) for r in range(1, n // SIDE)]
        parts = [totals] + [swap(totals, m) for m in near if m < span]
        parts = after(tuple(parts), mark)
        return kernel_call(
            functools.partial(chain_kernel, n, span, reverse),
            (me1, *parts),
            [((SIDE, 8, CW), F32)],
            [pltpu.VMEM((len(parts) * 2 * SIDE + span, 8, CW), F32)],
            us=2,
        )[0]

    top_l, top_x = after((top_l, top_x), totals)
    top_low, top_high = swap(top_l[: tok // 2], XBIT), swap(top_x[tok // 2 :], lbit(n))
    gate_halves = after((pre_mine, pre_theirs), totals, top_l)
    act, slope = kernel_call(gelu_kernel, gate_halves, [(wide, F32)] * 2, smem=0, us=7)
    c_out, c_extra = after((tuple(c_out), tuple(c_extra)), act)
    w_out = kernel_call(
        functools.partial(assemble_kernel, places, (2,)),
        (*c_out, *c_extra),
        [((CW, width), BF16)],
        smem=0,
    )[0]
    incoming = chain(totals, False, w_out)
    top_mine = jnp.concatenate([top, top_x, top_l, top_low, top_high])
    incoming = after(incoming, top_low, top_high)
    states, mixed, slope_states = kernel_call(
        states_kernel,
        (acc, loc, incoming, act, slope),
        [(wide, F32), (flat, BF16), (wide, F32)],
        smem=0,
        us=8,
    )
    theirs = dot(mixed[four:], w_out).astype(BF16)
    mixed_mine = after(mixed[:four], theirs)
    parts, mark_one, mark_two = scatter_side(dot(mixed_mine, w_out), theirs)
    top_theirs = swap(after(top_mine, mark_one), CBIT)
    gh_mine = dot(after(top_mine, mark_one), w_down)
    parts = after(parts, gh_mine)
    held = pltpu.VMEM((ROWS, width), F32)
    middle, normed_two = kernel_call(
        functools.partial(norm_two_kernel, n),
        (me1, block_input, gain_two, *parts),
        [((tok, width), F32), ((tok, width), BF16)],
        [held],
    )

    gh_theirs = dot(after(top_theirs, normed_two), w_down)
    two_mine, two_theirs = gather_side(normed_two, marks=(gh_theirs, None))

    def feed_half(two, grad_hidden):
        inner_gate, inner_value = dot(two, w_gate), dot(two, w_value)
        act, slope = gelu_pair(inner_gate)
        hidden = (act * inner_value).astype(BF16)
        grad_ig = (grad_hidden * inner_value * slope).astype(BF16)
        grad_iv = (grad_hidden * act).astype(BF16)
        return hidden, grad_ig, grad_iv

    hid_t, gig_t, giv_t = feed_half(two_theirs, gh_theirs)
    back_t = (dot_last(gig_t, w_gate) + dot_last(giv_t, w_value)).astype(BF16)
    two_mine = after(two_mine, back_t)
    hid_m, gig_m, giv_m = feed_half(two_mine, gh_mine)
    back_m = dot_last(gig_m, w_gate) + dot_last(giv_m, w_value)

    def feed_grad(a_m, b_m, a_t, b_t, mark):
        a_m, a_t = after((a_m, a_t), mark)
        return (dot_first(a_m, b_m) + dot_first(a_t, b_t)).astype(BF16)

    def halve(x, m, axis, mark, sel):
        half = x.shape[axis] // 2
        kept = lax.slice_in_dim(x, 0, half, axis=axis)
        got = swap(lax.slice_in_dim(x, half, 2 * half, axis=axis), m, sel)
        if mark is not None:
            got = after(got, mark)
        return (kept.astype(F32) + got.astype(F32)).astype(BF16)

    def far_first(x, axis, mark=None, sel=None):
        return halve(x, masks[-1], axis, mark, sel)

    def far_rest(x, axis, mark=None, sel=None):
        for m in reversed(masks[:-1]):
            x = halve(x, m, axis, mark, sel)
        return x

    parts, mark_one, mark_two = scatter_side(back_m, back_t)
    feed_mark = mark_two
    fg_down = feed_grad(top_mine, hid_m, top_theirs, hid_t, mark_one)
    fg_gate = feed_grad(two_mine, gig_m, two_theirs, gig_t, (mark_two, fg_down))
    parts = after(parts, fg_gate)
    grad_middle, branch, gain_grad_two = kernel_call(
        functools.partial(middle_back_kernel, n),
        (me1, middle, output_grad, gain_two, *parts),
        [((tok, width), F32), ((tok, width), BF16), ((1, width), F32)],
        [held],
    )
    fg_value = feed_grad(two_mine, giv_m, two_theirs, giv_t, branch)
    hid_t, hid_m = after((hid_t, hid_m), fg_value)
    out_t = dot_last(hid_t, w_down).astype(BF16)
    out_m = dot_last(after(hid_m, out_t), w_down)
    branch_mine, branch_theirs = gather_side(branch, marks=(fg_value, out_m))

    gm_theirs = dot_last(branch_theirs, w_out)
    gm_mine = dot_last(branch_mine, w_out)
    grads, suffix, totals = kernel_call(
        back_scan_kernel,
        (gm_mine, gm_theirs, act, dec),
        [(wide, F32), (wide, F32), ((2 * SIDE, CW), F32)],
        smem=0,
        us=16,
    )
    scan_done = totals
    slope_states = after(slope_states, totals)
    grad_gate = kernel_call(
        gate_back_kernel, (gm_mine, gm_theirs, slope_states), [(flat, BF16)], smem=0
    )[0]

    def mixer_grad(grad, mine, theirs):
        return (dot_first(grad[:four], mine) + dot_first(grad[four:], theirs)).astype(BF16)

    def feed_send(shard):
        return exchange(shard.reshape(SIDE, rows_w, fs))

    def feed_rows(v, mark):
        return kernel_call(
            feed_join_kernel, (after(v, mark),), [((rows_w, feed), F32)], smem=0, us=2
        )[0]

    mixed_late = after(mixed, grad_gate)
    go = mixer_grad(mixed_late, branch_mine, branch_theirs)
    def feed_sum(g):
        return lax.psum_scatter(g, AXIS, axis_index_groups=far, tiled=True)

    down_sum = feed_sum(after(fg_down, feed_mark))
    gate_sum = feed_sum(after(fg_gate, branch))
    value_sum = feed_sum(fg_value)
    sent_down = feed_send(after(down_sum, scan_done))
    from_later = chain(totals, True, (go, sent_down))
    go = after(go, from_later)
    go0, go1 = far_first(go[:SLOT], 1), far_first(go[SLOT : 2 * SLOT], 1, None, only)
    g_reset, g_input, g_conv, sums, heads = kernel_call(
        mixer_back_kernel,
        (
            grads, suffix, from_later, dec, rg, ig, low, states, incoming, lin, before, keep,
            halo_keep, keep_rows, r_sq, i_sq, vec,
        ),
        [(flat, BF16)] * 2 + [(wide, F32), ((8, CW), F32), ((3 * SIDE, CW), F32)],
        smem=0,
        us=21,
    )
    heads_y = swap(heads, masks[-1])
    head_parts = [heads, heads_y]
    if span == n:
        low_far = masks[-1]
        side = XBIT | CBIT | lbit(n)
        pairs = []
        for i in range(n):
            for j in range(n):
                last = (i | side) + 1
                if last < n and (j & ~side) == (last & ~side) and (j & side) == (i & side):
                    if ((i ^ j) & ~side) != low_far:
                        pairs.append((j, i))
        head_parts.append(lax.ppermute(heads, AXIS, pairs))
    low_late = after(low, heads)
    sq_r, sq_i = dot_first(low_late, g_reset), dot_first(low_late, g_input)

    rows = SLOT + HALO

    def pack(slot):
        r0, c0 = slot * SLOT, slot * 256
        squares = jnp.concatenate(
            [sq_r[r0 : r0 + SLOT, c0 : c0 + 384], sq_i[r0 : r0 + SLOT, c0 : c0 + 384]], axis=1
        )
        vecs = jnp.pad(sums[:, c0 : c0 + 384], ((0, 8), (0, 384)))
        return jnp.concatenate([squares, vecs]).astype(BF16)

    def total_far(v, m, sel=None):
        return (v.astype(F32) + swap(v, m, sel).astype(F32)).astype(BF16)

    packed_one, packed_two = after((pack(0), pack(1)), heads_y)
    packed_one = total_far(packed_one, masks[-1])
    packed_two = total_far(packed_two, masks[-1], only)

    out_parts, out_one, out_two = scatter_side(after(out_m, scan_done), out_t, heads)
    head_parts = after(tuple(head_parts), sq_i, out_two)
    grad_lin = kernel_call(
        functools.partial(linear_back_kernel, n, span),
        (me1, g_conv, keep, taps, *head_parts),
        [(flat, BF16)],
        [
            pltpu.VMEM((9 * SIDE, 8, CW), F32),
            pltpu.VMEM((3 * SIDE, CW), F32),
            pltpu.VMEM(wide, F32),
        ],
        us=8,
    )[0]
    sent_gate = feed_send(after(gate_sum, grad_lin))
    grad_lin = after(grad_lin, out_parts)
    grad_pre = jnp.concatenate([grad_gate, grad_lin], axis=1)
    back_t = dot(grad_pre[four:], w_mix).astype(BF16)
    back_m = dot(after(grad_pre[:four], back_t), w_mix)
    parts, mark_one, mark_two = scatter_side(
        back_m, back_t, (go0, go1, packed_one, packed_two)
    )
    go0, go1 = far_rest(after(go0, mark_two), 1), far_rest(after(go1, mark_two), 1, None, only)
    packed_one, packed_two = after((packed_one, packed_two), mark_two)
    for m in masks[:-1]:
        packed_one, packed_two = total_far(packed_one, m), total_far(packed_two, m, only)
    block_output = kernel_call(
        functools.partial(add_kernel, n),
        (after(middle, mark_one), *out_parts),
        [((tok, width), F32)],
        smem=0,
    )[0]

    gp = mixer_grad(after(grad_pre, mark_one), norm_mine, norm_theirs)
    gp0 = jnp.concatenate([gp[:SLOT], gp[CW : CW + SLOT]])
    gp1 = jnp.concatenate([gp[SLOT : 2 * SLOT], gp[CW + SLOT : CW + 2 * SLOT]])
    gp0, gp1 = after((gp0, gp1), mark_two)
    gp0, gp1 = far_first(gp0, 1), far_first(gp1, 1, None, only)
    input_grad, gain_grad_one = kernel_call(
        functools.partial(input_back_kernel, n),
        (me1, block_input, grad_middle, gain_one, *after(parts, block_output)),
        [((tok, width), F32), ((1, width), F32)],
        [held],
    )
    done = input_grad
    sent_value = feed_send(after(value_sum, done))
    grad_w_down = feed_rows(sent_down, done)
    grad_w_gate = feed_rows(sent_gate, done)
    grad_w_value = feed_rows(sent_value, done)

    def to_rows(parts, kinds):
        size = (2 * kinds * SLOT + 127) // 128 * 128
        back = kernel_call(turn_back_kernel, parts, [((SIDE, rows_w, size), BF16)], smem=0)[0]
        return kernel_call(
            functools.partial(head_rows_kernel, blk),
            (exchange(back),),
            [((rows_w, heads_count * blk), F32)] * kinds,
            smem=0,
        )

    gp0, gp1 = far_rest(gp0, 1), far_rest(gp1, 1, None, only)
    go0, go1 = after((go0, go1), done)
    grad_w_out = to_rows((go0, go1), 1)[0]
    grad_w_g, grad_w_l = to_rows((gp0, gp1), 2)

    pack_one, pack_two = after((packed_one, packed_two), done)
    packs_mine, packs_theirs = gather_side(pack_one)
    two_x = swap(pack_two, XBIT, only)
    head = here >> 1
    mine_is_eight = (head == 0) | (head == 1)
    both = jnp.where(head == 0, pack_two, jnp.where(head == 3, pack_two, two_x))
    two_l = swap(both, lbit(n))
    eight = jnp.where(mine_is_eight, both, two_l)
    nine = jnp.where(mine_is_eight, two_l, both)
    pair = jnp.stack([eight, nine])
    pair_c = swap(pair, CBIT)
    pair = jnp.where((here & 1) == 0, pair, pair_c)
    shape = (4, rows, 768)
    grad_r_weight, grad_i_weight, small = kernel_call(
        functools.partial(packs_kernel, n, blk),
        (me1, packs_mine.reshape(shape), packs_theirs.reshape(shape), pair[0], pair[1]),
        [((heads_count, blk, blk), F32)] * 2 + [((8, heads_count * blk), F32)],
    )

    gains = jnp.concatenate([gain_grad_one, gain_grad_two]).reshape(-1, 256)
    gains = gains + swap(gains, CBIT)
    rest = [XBIT, lbit(n)] + masks
    while rest:
        one, two, rest = rest[0], rest[1], rest[2:]
        gains = (gains + swap(gains, one)) + (swap(gains, two) + swap(gains, one | two))
    gains = gains.reshape(2, width)

    return (
        block_output,
        input_grad,
        gains[0],
        grad_w_g,
        grad_w_l,
        small[4:],
        small[3],
        grad_r_weight,
        small[0],
        grad_i_weight,
        small[1],
        small[2],
        grad_w_out,
        gains[1],
        grad_w_gate,
        grad_w_value,
        grad_w_down,
    )


def solution(mesh):
    split, whole = P(AXIS, None), P()
    in_specs = (split, P(AXIS), whole, split, split) + (whole,) * 7
    in_specs += (split, whole, split, split, split, split)
    out_specs = (split, split, whole, split, split) + (whole,) * 7
    out_specs += (split, whole, split, split, split)
    return jax.shard_map(body, mesh=mesh, in_specs=in_specs, out_specs=out_specs, check_vma=False)
```

time: 3640 us -> 780 us (0.21)
  waiting for transfers between devices: 2540 us -> 196 us
  local copies, waits for them, and re-layouts: 521 us -> 61.5 us
  Pallas kernels: 0 us -> 194 us
  other arithmetic: 183 us -> 33 us
  starting transfers between devices: 4.21 us -> 137 us
  blocking collectives: 123 us -> 0 us
  matrix products: 240 us -> 136 us
    reduce_scatter x1 -> x3, waiting for transfers between devices: 1280 us -> 0.01 us  [feed_sum(): return lax.psum_scatter(g, AXIS, axis_index_groups=far, tiled=True)]
    unnamed x11 -> x6, waiting for transfers between devices: 499 us -> 0.1 us
    all_gather x6 -> x3, waiting for transfers between devices: 445 us -> 22.1 us  [feed_full(): return lax.all_gather(part, AXIS, axis_index_groups=far, tiled=True)]
    psum x2 -> x0, waiting for transfers between devices: 317 us -> none  [body(): lax.psum((grad_gain_one, grad_taps, grad_bias_conv, grad_reset_w, grad_re...]
    pallas_call x0 -> x38, Pallas kernels: none -> 194 us  [kernel_call(): pl.pallas_call(kernel, in_specs=specs, out_specs=[pl.BlockSpec(memory_spa...]
    concatenate x3 -> x14, local copies, waits for them, and re-layouts: 164 us -> 5.55 us  [the longest x3 2.4 us: gather_side(): mine = jnp.concatenate([x, by_x, by_l, low, high])]
    ppermute x2 -> x81, waiting for transfers between devices: 0.38 us -> 158 us  [the longest x80 158 us: swap(): return lax.ppermute(v, AXIS, pairs)]
    all_gather x3 -> x0, blocking collectives: 123 us -> none  [carried_in(): gathered = jax.tree.map(lambda a: lax.all_gather(a, axis), part)]
  transfers between devices with their start and end apart: 12 -> 95, of which waited for: 9 -> 29; matrix products, arithmetic and copies ran while one was open for 12% -> 27% of each run, Pallas kernels for 0% -> 23%
where the time goes in v2:
time: 780 us; the launch traced here: 773 us
  waiting for transfers between devices  196 us (25%)
  Pallas kernels  194 us (25%)
  starting transfers between devices  137 us (18%)
  matrix products  136 us (17%)
  local copies, waits for them, and re-layouts  61.5 us (8%)
  other arithmetic  33 us (4%)
  between operations  15.7 us (2%)
    pallas_call x38, Pallas kernels, kernel_call(): pl.pallas_call(kernel, in_specs=specs, out_specs=[pl.BlockSpec(memory_spa...  194 us
    ppermute x80, waiting for transfers between devices, swap(): return lax.ppermute(v, AXIS, pairs)  158 us
    ppermute x80, starting transfers between devices, swap(): return lax.ppermute(v, AXIS, pairs)  97.3 us
    dot_general x10, matrix products, dot(): lax.dot_general(a, b, (((1,), (0,)), ((), ())), preferred_element_type=F32)  49.2 us
    dot_general x11, matrix products, dot_last(): lax.dot_general(a, b, (((1,), (1,)), ((), ())), preferred_element_type=F32)  44.4 us
    dot_general x12, matrix products, dot_first(): lax.dot_general(a, b, (((0,), (0,)), ((), ())), preferred_element_type=F32)  42.1 us
    all_to_all x8, starting transfers between devices, exchange(): return lax.all_to_all(v, AXIS, 0, 0, axis_index_groups=groups, tiled=True)  36.8 us
    unnamed x153, local copies, waits for them, and re-layouts  29.2 us
  transfers between devices with their start and end apart: 95, of which 29 were waited for; matrix products, arithmetic and copies ran while one was open for 27% of the time, Pallas kernels for 23%

profile of v2, /device:TPU:0, one launch (start us, length us, event | category | flops | bytes accessed | tf_op | source)
XLA Modules:
  0.0 772.8 jit_solution(12718836744694519377)
XLA Ops:
  10.2 5.4 all-to-all-start
  31.2 4.9 all-to-all-start.1
  55.9 18.6 %collective-permute-done.3 = bf16[144,2048]{1,0:T(8,128)(2,1)S(1)} collective-permute-done((bf16[144,2048]{1,0:T(8,128)(2,1)S(1)}, bf16[144,2048]{1,0:T(8,128)(2,1)S(1)}, u32[]{:S(2)}, u32[]{:S(2)}) %collective-permute-start.3) | collective-permute-done | bytes 589856 | tf_op jit(solution)/shard_map/ppermute | solution.py:94
  89.6 6.7 collective-permute-done.5.refs_3_
  114.6 13.2 %all-to-all-done.2 = bf16[8,192,768]{2,1,0:T(8,128)(2,1)S(1)} async-done(((bf16[8,192,768]{2,1,0:T(8,128)(2,1)}), bf16[8,192,768]{2,1,0:T(8,128)(2,1)S(1)}, u32[]{:S(2)}, u32[]{:S(2)}) %all-to-all-start.2) | async-done | bytes 2359328 | tf_op jit(solution)/shard_map/all_to_all | solution.py:794
  129.5 5.4 shard_map.310
  140.6 7.6 fusion.32.lin_mine.gate_mine
  148.3 6.1 fusion.33.lin_theirs.gate_theirs
  156.0 29.3 %shard_map.312 = (f32[5,1024,128]{2,1,0:T(8,128)}, bf16[1024,640]{1,0:T(8,128)(2,1)}, f32[5,1024,128]{2,1,0:T(8,128)}, f32[5,1024,128]{2,1,0:T(8,128)}, f32[5,10...) custom-call(f32[512,1280]{1,0:T(8,128)} %fusion.32.lin_mine.gate_min, ...), custom_call_target="tpu_custom_call" | custom-call | flops 28999999488 | bytes 87000000 | tf_op jit(solution)/shard_map/pallas_call | solution.py:116
  189.7 6.9 shard_map.314
  197.4 4.1 shard_map.315
  203.7 8.6 %shard_map.317 = (f32[5,1024,128]{2,1,0:T(8,128)}, bf16[1024,640]{1,0:T(8,128)(2,1)}, f32[5,1024,128]{2,1,0:T(8,128)}) custom-call(f32[5,1024,128]{2,1,0:T(8,128)} %get-tuple-element.212.acc, f32[5,1024,128]{2,1,0:T(8,128)} %get-tuple-element.213.loc, f32[8,8,640]{2,1,0:T(8,128)} %shard_map.316.incoming, f32[5,1024,128]{2,1,0:T(8,128)} %get-tuple-element.223.act, ...), custom_call_target="tpu_custom_call" | custom-call | flops 8000000000 | bytes 24000000 | tf_op jit(solution)/shard_map/pallas_call | solution.py:116
  212.3 3.7 convolution_convert_fusion.2
  220.1 3.8 fusion.34.mine
  224.0 4.9 shard_map.318
  230.3 22.2 %collective-permute-done.22.recv_a = bf16[256,1024]{1,0:T(8,128)(2,1)S(1)} collective-permute-done((bf16[256,1024]{1,0:T(8,128)(2,1)}, bf16[256,1024]{1,0:T(8,128)(2,1)S(1)}, u32[]{:S(2)}, u32[]{:S(2)}) %collective-permute-start.22) | collective-permute-done | bytes 524320 | tf_op jit(solution)/shard_map/ppermute | solution.py:94
  258.7 5.5 fusion.35
  264.1 7.6 collective-permute-done.25.rb
  279.0 5.5 fusion.36
  284.5 10.2 %collective-permute-done.26 = bf16[128,2048]{1,0:T(8,128)(2,1)S(1)} collective-permute-done((bf16[128,2048]{1,0:T(8,128)(2,1)}, bf16[128,2048]{1,0:T(8,128)(2,1)S(1)}, u32[]{:S(2)}, u32[]{:S(2)}) %collective-permute-start.26) | collective-permute-done | bytes 524320 | tf_op jit(solution)/shard_map/ppermute | solution.py:94
  294.6 4.0 collective-permute-start.29
  303.1 4.8 collective-permute-done.30
  308.0 4.2 collective-permute-done.31
  312.2 5.4 fusion.37
  317.7 22.1 %all-gather.6.cloned.1.call-done = bf16[2048,768]{1,0:T(8,128)(2,1)} async-done(((bf16[512,768]{1,0:T(8,128)(2,1)}), bf16[2048,768]{1,0:T(8,128)(2,1)}) %all-gather.6.cloned.1.call-update) | async-done | bytes 3145744 | tf_op jit(solution)/shard_map/all_gather | solution.py:888
  339.8 7.1 multiply_convert_fusion
  353.1 3.7 multiply_convert_fusion.1
  358.6 3.9 convolution_add_fusion.mine
  362.4 4.9 shard_map.321
  368.8 3.7 fusion.41
  372.5 5.3 add_convert_fusion.3
  377.8 4.1 collective-permute-done.33.recv_a
  392.1 3.7 add_convert_fusion.2
  398.0 3.8 shard_map.323
  404.9 3.8 fusion.43
  408.8 3.7 add_convert_fusion.1
  412.5 5.7 convolution_convert_fusion.1
  419.0 3.8 fusion.44.mine
  422.8 6.4 collective-permute-done.37
  440.8 5.4 fusion.45.gm_mine
  450.5 15.4 %shard_map.324 = (f32[5,1024,128]{2,1,0:T(8,128)}, f32[5,1024,128]{2,1,0:T(8,128)}, f32[16,640]{1,0:T(8,128)}) custom-call(f32[512,640]{1,0:T(8,128)} %fusion.45.gm_mine, f32[512,640]{1,0:T(8,128)} %fusion.46.gm_theirs, f32[5,1024,128]{2,1,0:T(8,128)} %get-tuple-element.223.act, f32[5,1024,128]{2,1,0:T(8,128)} %get-tuple-element.281.dec), custom_call_target="tpu_custom_call" | custom-call | flops 16000000000 | bytes 48000000 | tf_op jit(solution)/shard_map/pallas_call | solution.py:116
  467.3 6.2 all-to-all-start.3
  473.5 4.1 shard_map.325
  482.3 5.8 shard_map.328
  496.8 20.7 %shard_map.327 = (bf16[1024,640]{1,0:T(8,128)(2,1)}, bf16[1024,640]{1,0:T(8,128)(2,1)}, f32[5,1024,128]{2,1,0:T(8,128)}, f32[8,640]{1,0:T(8,128)}, f32[24,640]{1,0:T(8,128)}) custom-call(f32[5,1024,128]{2,1,0:T(8,128)} %get-tuple-element.284.grads, f32[5,1024,128]{2,1,0:T(8,128)} %get-tuple-element.285.suffix, f32[8,8,640]{2,1,0:T(8,128)} %shard_map.326.from_later, ...), custom_call_target="tpu_custom_call" | custom-call | flops 20999999488 | bytes 63000000 | tf_op jit(solution)/shard_map/pallas_call | solution.py:116
  534.6 8.6 %shard_map.330 = bf16[1024,640]{1,0:T(8,128)(2,1)} custom-call(s32[1]{0:T(128)} %bitcast.me.me_ref, f32[5,1024,128]{2,1,0:T(8,128)} %get-tuple-element.297.g_conv, f32[1024,128]{1,0:T(8,128)} %broadcast_in_dim.53.keep, f32[4,640]{1,0:T(4,128)} %pad_slice_fusion.7.taps, f32[24,640]{1,0:T(8,128)} %get-tuple-element.308.refs_0_, f32[24,640]{1,0:T(8,128)} %copy-done.54), custom_call_target="tpu_custom_call" | custom-call | flops 8000000000 | bytes 24000000 | tf_op jit(solution)/shard_map/pallas_call | solution.py:116
  543.2 4.4 all-to-all-start.6
  548.0 5.6 convolution_convert_fusion
  554.0 7.1 fusion.48.mine
  562.9 6.8 collective-permute-done.53
  578.3 5.0 shard_map.331
  584.2 4.5 fusion.8
  588.7 4.8 add_convert_fusion
  595.8 4.9 collective-permute-done.54.recv_a
  623.2 3.9 shard_map.334
  637.8 3.7 collective-permute-done.79
  643.7 4.5 collective-permute-done.70
  649.5 3.7 collective-permute-done.69
  657.6 4.5 all-to-all-start.5
  663.2 3.9 collective-permute-start.76
  690.6 4.2 all-to-all-start.7
  705.4 21.7 %collective-permute-done.68 = bf16[576,512]{1,0:T(8,128)(2,1)S(1)} collective-permute-done((bf16[576,512]{1,0:T(8,128)(2,1)}, bf16[576,512]{1,0:T(8,128)(2,1)S(1)}, u32[]{:S(2)}, u32[]{:S(2)}) %collective-permute-start.68) | collective-permute-done | bytes 589856 | tf_op jit(solution)/shard_map/ppermute | solution.py:94
  728.1 5.3 collective-permute-done.66
  752.1 6.6 shard_map.337
  (455 shorter events, 301.4 us)
Async XLA Ops:
  10.2 21.0 %all-to-all-start = ((bf16[8,64,896]{2,1,0:T(8,128)(2,1)}), bf16[8,64,896]{2,1,0:T(8,128)(2,1)S(1)}, u32[]{:S(2)}, u32[]{:S(2)}) async-start(bf16[8,64,896]{2,1,0:T(8,128)(2,1)} %get-tuple-element.187), calls=%async_computation | async-start | bytes 1835008 | tf_op jit(solution)/shard_map/all_to_all | solution.py:794
  31.2 21.4 %all-to-all-start.1 = ((bf16[8,64,896]{2,1,0:T(8,128)(2,1)}), bf16[8,64,896]{2,1,0:T(8,128)(2,1)S(1)}, u32[]{:S(2)}, u32[]{:S(2)}) async-start(bf16[8,64,896]{2,1,0:T(8,128)(2,1)} %get-tuple-element.192), calls=%async_computation.1 | async-start | bytes 1835008 | tf_op jit(solution)/shard_map/all_to_all | solution.py:794
  43.8 30.7 %collective-permute-start.3 = (bf16[144,2048]{1,0:T(8,128)(2,1)S(1)}, bf16[144,2048]{1,0:T(8,128)(2,1)S(1)}, u32[]{:S(2)}, u32[]{:S(2)}) collective-permute-start(bf16[144,2048]{1,0:T(8,128)(2,1)S(1)} %copy-done.19), channel_id=1, source_target_pairs={{0,8},{1,9},{2,10},{3,11},{4,12},{5,13},{6,14},{7,15},{8,0},{9,1},... | collective-permute-start | bytes 1769480 | tf_op jit(solution)/shard_map/ppermute | solution.py:94
  46.0 28.5 %collective-permute-start.4 = (bf16[144,2048]{1,0:T(8,128)(2,1)S(1)}, bf16[144,2048]{1,0:T(8,128)(2,1)S(1)}, u32[]{:S(2)}, u32[]{:S(2)}) collective-permute-start(bf16[144,2048]{1,0:T(8,128)(2,1)S(1)} %copy-done.19), channel_id=1, source_target_pairs={{0,2},{1,3},{2,0},{3,1},{4,6},{5,7},{6,4},{7,5},{8,10},{9,11},{10,... | collective-permute-start | bytes 1769480 | tf_op jit(solution)/shard_map/ppermute | solution.py:94
  47.3 27.2 %collective-permute-start.1 = (bf16[576,512]{1,0:T(8,128)(2,1)}, bf16[576,512]{1,0:T(8,128)(2,1)}, u32[]{:S(2)}, u32[]{:S(2)}) collective-permute-start(bf16[576,512]{1,0:T(8,128)(2,1)} %get-tuple-element.202.refs_0_), channel_id=1, source_target_pairs={{0,16},{1,17},{2,18},{3,19},{4,20},{5,21},{6,22},{7,23},{8,24},{9,... | collective-permute-start | bytes 1769480 | tf_op jit(solution)/shard_map/ppermute | solution.py:94
  49.9 24.6 %collective-permute-start.2 = (bf16[576,512]{1,0:T(8,128)(2,1)}, bf16[576,512]{1,0:T(8,128)(2,1)}, u32[]{:S(2)}, u32[]{:S(2)}) collective-permute-start(bf16[576,512]{1,0:T(8,128)(2,1)} %get-tuple-element.202.refs_0_), channel_id=1, source_target_pairs={{0,4},{1,5},{2,6},{3,7},{4,0},{5,1},{6,2},{7,3},{8,12},{9,13},{10,... | collective-permute-start | bytes 1769480 | tf_op jit(solution)/shard_map/ppermute | solution.py:94
  80.1 19.7 %collective-permute-start.6 = (bf16[864,512]{1,0:T(8,128)(2,1)}, bf16[864,512]{1,0:T(8,128)(2,1)}, u32[]{:S(2)}, u32[]{:S(2)}) collective-permute-start(bf16[864,512]{1,0:T(8,128)(2,1)} %shard_map.309.refs_4_), channel_id=1, source_target_pairs={{0,16},{4,20},{10,26},{14,30},{16,0},{20,4},{26,10},{30,14}} | collective-permute-start | bytes 2654216 | tf_op jit(solution)/shard_map/ppermute | solution.py:94
  84.2 43.6 %all-to-all-start.2 = ((bf16[8,192,768]{2,1,0:T(8,128)(2,1)}), bf16[8,192,768]{2,1,0:T(8,128)(2,1)S(1)}, u32[]{:S(2)}, u32[]{:S(2)}) async-start(bf16[8,192,768]{2,1,0:T(8,128)(2,1)} %shard_map.311), calls=%async_computation.2 | async-start | bytes 4718592 | tf_op jit(solution)/shard_map/all_to_all | solution.py:794
  87.8 170.9 %all-gather.4.cloned.1.call-start = ((), (), s32[]{:S(2)}) async-start(), calls=%async_computation.11 | async-start | bytes 3932160 | tf_op jit(solution)/shard_map/all_gather | solution.py:888
  100.8 28.8 %collective-permute-start.10 = (bf16[864,512]{1,0:T(8,128)(2,1)}, bf16[864,512]{1,0:T(8,128)(2,1)}, u32[]{:S(2)}, u32[]{:S(2)}) collective-permute-start(bf16[864,512]{1,0:T(8,128)(2,1)} %collective-permute-done.6.refs_5_), channel_id=1, source_target_pairs={{0,4},{4,0},{10,14},{14,10},{16,20},{20,16},{26,30},{30,26}} | collective-permute-start | bytes 2654216 | tf_op jit(solution)/shard_map/ppermute | solution.py:94
  104.4 25.2 %collective-permute-start.9 = (bf16[864,512]{1,0:T(8,128)(2,1)}, bf16[864,512]{1,0:T(8,128)(2,1)}, u32[]{:S(2)}, u32[]{:S(2)}) collective-permute-start(bf16[864,512]{1,0:T(8,128)(2,1)} %shard_map.309.refs_4_), channel_id=1, source_target_pairs={{0,4},{4,0},{10,14},{14,10},{16,20},{20,16},{26,30},{30,26}} | collective-permute-start | bytes 2654216 | tf_op jit(solution)/shard_map/ppermute | solution.py:94
  110.0 38.3 %collective-permute-start.11 = (bf16[512,2048]{1,0:T(8,128)(2,1)}, bf16[512,2048]{1,0:T(8,128)(2,1)}, u32[]{:S(2)}, u32[]{:S(2)}) collective-permute-start(bf16[512,2048]{1,0:T(8,128)(2,1)} %slice_dynamic-update-slice_fusion.3), channel_id=1, source_target_pairs={{0,1},{1,0},{2,3},{3,2},{4,5},{5,4},{6,7},{7,6},{8,9},{9,8},{10,11... | collective-permute-start | bytes 6291464 | tf_op jit(solution)/shard_map/ppermute | solution.py:94
  110.0 25.0 %collective-permute-start.14 = (bf16[288,512]{1,0:T(8,128)(2,1)}, bf16[288,512]{1,0:T(8,128)(2,1)S(1)}, u32[]{:S(2)}, u32[]{:S(2)}) collective-permute-start(bf16[288,512]{1,0:T(8,128)(2,1)} %get-tuple-element.224.refs_0_), channel_id=1, source_target_pairs={{0,16},{1,17},{2,18},{3,19},{4,20},{5,21},{6,22},{7,23},{8,24},{9,... | collective-permute-start | bytes 884744 | tf_op jit(solution)/shard_map/ppermute | solution.py:94
  129.3 178.7 %all-gather.8.cloned.1.call-start = ((), (), s32[]{:S(2)}) async-start(), calls=%async_computation.13 | async-start | bytes 3932160 | tf_op jit(solution)/shard_map/all_gather | solution.py:888
  134.9 61.6 %collective-permute-start.16 = (bf16[288,512]{1,0:T(8,128)(2,1)S(1)}, bf16[288,512]{1,0:T(8,128)(2,1)S(1)}, u32[]{:S(2)}, u32[]{:S(2)}) collective-permute-start(bf16[288,512]{1,0:T(8,128)(2,1)S(1)} %collective-permute-done.14.refs_1_), channel_id=1, source_target_pairs={{0,4},{1,5},{2,6},{3,7},{4,0},{5,1},{6,2},{7,3},{8,12},{9,13},{10,... | collective-permute-start | bytes 884744 | tf_op jit(solution)/shard_map/ppermute | solution.py:94
  135.0 61.6 %collective-permute-start.15 = (bf16[288,512]{1,0:T(8,128)(2,1)}, bf16[288,512]{1,0:T(8,128)(2,1)S(1)}, u32[]{:S(2)}, u32[]{:S(2)}) collective-permute-start(bf16[288,512]{1,0:T(8,128)(2,1)} %get-tuple-element.224.refs_0_), channel_id=1, source_target_pairs={{0,4},{1,5},{2,6},{3,7},{4,0},{5,1},{6,2},{7,3},{8,12},{9,13},{10,... | collective-permute-start | bytes 884744 | tf_op jit(solution)/shard_map/ppermute | solution.py:94
  137.0 48.6 %collective-permute-start.17 = (bf16[128,2048]{1,0:T(8,128)(2,1)S(1)}, bf16[128,2048]{1,0:T(8,128)(2,1)S(1)}, u32[]{:S(2)}, u32[]{:S(2)}) collective-permute-start(bf16[128,2048]{1,0:T(8,128)(2,1)S(1)} %copy-done.20), channel_id=1, source_target_pairs={{0,8},{1,9},{2,10},{3,11},{4,12},{5,13},{6,14},{7,15},{8,0},{9,1},... | collective-permute-start | bytes 1572872 | tf_op jit(solution)/shard_map/ppermute | solution.py:94
  137.0 48.7 %collective-permute-start.18 = (bf16[128,2048]{1,0:T(8,128)(2,1)S(1)}, bf16[128,2048]{1,0:T(8,128)(2,1)S(1)}, u32[]{:S(2)}, u32[]{:S(2)}) collective-permute-start(bf16[128,2048]{1,0:T(8,128)(2,1)S(1)} %copy-done.20), channel_id=1, source_target_pairs={{0,2},{1,3},{2,0},{3,1},{4,6},{5,7},{6,4},{7,5},{8,10},{9,11},{10,... | collective-permute-start | bytes 1572872 | tf_op jit(solution)/shard_map/ppermute | solution.py:94
  185.6 154.1 %all-gather.6.cloned.1.call-start = ((), (), s32[]{:S(2)}) async-start(), calls=%async_computation.12 | async-start | bytes 3932160 | tf_op jit(solution)/shard_map/all_gather | solution.py:888
  185.7 18.0 %collective-permute-start.19 = (bf16[64,2048]{1,0:T(8,128)(2,1)S(1)}, bf16[64,2048]{1,0:T(8,128)(2,1)S(1)}, u32[]{:S(2)}, u32[]{:S(2)}) collective-permute-start(bf16[64,2048]{1,0:T(8,128)(2,1)S(1)} %slice.251), channel_id=1, source_target_pairs={{0,2},{1,3},{2,0},{3,1},{4,6},{5,7},{6,4},{7,5},{8,10},{9,11},{10,... | collective-permute-start | bytes 786440 | tf_op jit(solution)/shard_map/ppermute | solution.py:94
  228.9 50.1 %collective-permute-start.28 = (bf16[512,2048]{1,0:T(8,128)(2,1)}, bf16[512,2048]{1,0:T(8,128)(2,1)}, u32[]{:S(2)}, u32[]{:S(2)}) collective-permute-start(bf16[512,2048]{1,0:T(8,128)(2,1)} %constant_dynamic-update-slice_fusion.6), channel_id=1, source_target_pairs={{0,1},{1,0},{2,3},{3,2},{4,5},{5,4},{6,7},{7,6},{8,9},{9,8},{10,11... | collective-permute-start | bytes 6291464 | tf_op jit(solution)/shard_map/ppermute | solution.py:94
  229.4 23.1 %collective-permute-start.22 = (bf16[256,1024]{1,0:T(8,128)(2,1)}, bf16[256,1024]{1,0:T(8,128)(2,1)S(1)}, u32[]{:S(2)}, u32[]{:S(2)}) collective-permute-start(bf16[256,1024]{1,0:T(8,128)(2,1)} %get-tuple-element.240), channel_id=1, source_target_pairs={{0,8},{1,9},{2,10},{3,11},{4,12},{5,13},{6,14},{7,15},{8,0},{9,1},... | collective-permute-start | bytes 1572872 | tf_op jit(solution)/shard_map/ppermute | solution.py:94
  229.4 23.1 %collective-permute-start.23 = (bf16[256,1024]{1,0:T(8,128)(2,1)}, bf16[256,1024]{1,0:T(8,128)(2,1)S(1)}, u32[]{:S(2)}, u32[]{:S(2)}) collective-permute-start(bf16[256,1024]{1,0:T(8,128)(2,1)} %get-tuple-element.242), channel_id=1, source_target_pairs={{0,2},{1,3},{2,0},{3,1},{4,6},{5,7},{6,4},{7,5},{8,10},{9,11},{10,... | collective-permute-start | bytes 1572872 | tf_op jit(solution)/shard_map/ppermute | solution.py:94
  230.2 237.1 %reduce-scatter.4.cloned.1.call-start = ((), (), s32[]{:S(2)}) async-start(), calls=%async_computation.14 | async-start | bytes 3932160 | tf_op jit(solution)/shard_map/reduce_scatter | solution.py:1080
  275.6 19.1 %collective-permute-start.26 = (bf16[128,2048]{1,0:T(8,128)(2,1)}, bf16[128,2048]{1,0:T(8,128)(2,1)S(1)}, u32[]{:S(2)}, u32[]{:S(2)}) collective-permute-start(bf16[128,2048]{1,0:T(8,128)(2,1)} %get-tuple-element.251), channel_id=1, source_target_pairs={{0,8},{1,9},{2,10},{3,11},{4,12},{5,13},{6,14},{7,15},{8,0},{9,1},... | collective-permute-start | bytes 1572872 | tf_op jit(solution)/shard_map/ppermute | solution.py:94
  275.6 19.1 %collective-permute-start.27 = (bf16[128,2048]{1,0:T(8,128)(2,1)}, bf16[128,2048]{1,0:T(8,128)(2,1)S(1)}, u32[]{:S(2)}, u32[]{:S(2)}) collective-permute-start(bf16[128,2048]{1,0:T(8,128)(2,1)} %get-tuple-element.251), channel_id=1, source_target_pairs={{0,2},{1,3},{2,0},{3,1},{4,6},{5,7},{6,4},{7,5},{8,10},{9,11},{10,... | collective-permute-start | bytes 1572872 | tf_op jit(solution)/shard_map/ppermute | solution.py:94
  385.2 158.0 %reduce-scatter.6.cloned.1.call-start = ((), (), s32[]{:S(2)}) async-start(), calls=%async_computation.15 | async-start | bytes 3932160 | tf_op jit(solution)/shard_map/reduce_scatter | solution.py:1080
  401.9 229.7 %reduce-scatter.8.cloned.1.call-start = ((), (), s32[]{:S(2)}) async-start(), calls=%async_computation.16 | async-start | bytes 3932160 | tf_op jit(solution)/shard_map/reduce_scatter | solution.py:1080
  402.1 27.1 %collective-permute-start.37 = (bf16[128,2048]{1,0:T(8,128)(2,1)}, bf16[128,2048]{1,0:T(8,128)(2,1)}, u32[]{:S(2)}, u32[]{:S(2)}) collective-permute-start(bf16[128,2048]{1,0:T(8,128)(2,1)} %get-tuple-element.270), channel_id=1, source_target_pairs={{0,8},{1,9},{2,10},{3,11},{4,12},{5,13},{6,14},{7,15},{8,0},{9,1},... | collective-permute-start | bytes 1572872 | tf_op jit(solution)/shard_map/ppermute | solution.py:94
  404.9 24.3 %collective-permute-start.38 = (bf16[128,2048]{1,0:T(8,128)(2,1)}, bf16[128,2048]{1,0:T(8,128)(2,1)}, u32[]{:S(2)}, u32[]{:S(2)}) collective-permute-start(bf16[128,2048]{1,0:T(8,128)(2,1)} %get-tuple-element.270), channel_id=1, source_target_pairs={{0,2},{1,3},{2,0},{3,1},{4,6},{5,7},{6,4},{7,5},{8,10},{9,11},{10,... | collective-permute-start | bytes 1572872 | tf_op jit(solution)/shard_map/ppermute | solution.py:94
  440.2 42.1 %collective-permute-start.44 = (bf16[512,2048]{1,0:T(8,128)(2,1)}, bf16[512,2048]{1,0:T(8,128)(2,1)}, u32[]{:S(2)}, u32[]{:S(2)}) collective-permute-start(bf16[512,2048]{1,0:T(8,128)(2,1)} %convolution_convert_fusion.1), channel_id=1, source_target_pairs={{0,1},{1,0},{2,3},{3,2},{4,5},{5,4},{6,7},{7,6},{8,9},{9,8},{10,11... | collective-permute-start | bytes 6291464 | tf_op jit(solution)/shard_map/ppermute | solution.py:94
  465.9 25.9 %collective-permute-start.42 = (f32[16,640]{1,0:T(8,128)}, f32[16,640]{1,0:T(8,128)S(1)}, u32[]{:S(2)}, u32[]{:S(2)}) collective-permute-start(f32[16,640]{1,0:T(8,128)} %get-tuple-element.289.refs_0_), channel_id=1, source_target_pairs={{0,4},{1,5},{2,6},{3,7},{4,0},{5,1},{6,2},{7,3},{8,12},{9,13},{10,... | collective-permute-start | bytes 122888 | tf_op jit(solution)/shard_map/ppermute | solution.py:94
  467.3 26.9 %all-to-all-start.3 = ((bf16[8,64,768]{2,1,0:T(8,128)(2,1)}), bf16[8,64,768]{2,1,0:T(8,128)(2,1)}, u32[]{:S(2)}, u32[]{:S(2)}) async-start(bf16[8,64,768]{2,1,0:T(8,128)(2,1)} %bitcast.115), calls=%async_computation.4 | async-start | bytes 1572864 | tf_op jit(solution)/shard_map/all_to_all | solution.py:794
  488.2 39.2 %collective-permute-start.45 = (bf16[256,1024]{1,0:T(8,128)(2,1)}, bf16[256,1024]{1,0:T(8,128)(2,1)}, u32[]{:S(2)}, u32[]{:S(2)}) collective-permute-start(bf16[256,1024]{1,0:T(8,128)(2,1)} %get-tuple-element.304), channel_id=1, source_target_pairs={{0,8},{1,9},{2,10},{3,11},{4,12},{5,13},{6,14},{7,15},{8,0},{9,1},... | collective-permute-start | bytes 1572872 | tf_op jit(solution)/shard_map/ppermute | solution.py:94
  490.3 37.0 %collective-permute-start.46 = (bf16[256,1024]{1,0:T(8,128)(2,1)}, bf16[256,1024]{1,0:T(8,128)(2,1)}, u32[]{:S(2)}, u32[]{:S(2)}) collective-permute-start(bf16[256,1024]{1,0:T(8,128)(2,1)} %get-tuple-element.306), channel_id=1, source_target_pairs={{0,2},{1,3},{2,0},{3,1},{4,6},{5,7},{6,4},{7,5},{8,10},{9,11},{10,... | collective-permute-start | bytes 1572872 | tf_op jit(solution)/shard_map/ppermute | solution.py:94
  522.1 53.3 %collective-permute-start.50 = (bf16[288,1024]{1,0:T(8,128)(2,1)}, bf16[288,1024]{1,0:T(8,128)(2,1)S(1)}, u32[]{:S(2)}, u32[]{:S(2)}) collective-permute-start(bf16[288,1024]{1,0:T(8,128)(2,1)} %get-tuple-element.374), channel_id=1, source_target_pairs={{0,4},{1,5},{2,6},{3,7},{4,0},{5,1},{6,2},{7,3},{8,12},{9,13},{10,... | collective-permute-start | bytes 1769480 | tf_op jit(solution)/shard_map/ppermute | solution.py:94
  523.6 52.7 %collective-permute-start.51 = (bf16[288,1024]{1,0:T(8,128)(2,1)S(1)}, bf16[288,1024]{1,0:T(8,128)(2,1)}, u32[]{:S(2)}, u32[]{:S(2)}) collective-permute-start(bf16[288,1024]{1,0:T(8,128)(2,1)S(1)} %get-tuple-element.373), channel_id=1, source_target_pairs={{0,4},{4,0},{10,14},{14,10},{16,20},{20,16},{26,30},{30,26}} | collective-permute-start | bytes 1769480 | tf_op jit(solution)/shard_map/ppermute | solution.py:94
  530.6 17.0 %collective-permute-start.47 = (bf16[128,1024]{1,0:T(8,128)(2,1)}, bf16[128,1024]{1,0:T(8,128)(2,1)}, u32[]{:S(2)}, u32[]{:S(2)}) collective-permute-start(bf16[128,1024]{1,0:T(8,128)(2,1)} %get-tuple-element.310), channel_id=1, source_target_pairs={{0,2},{1,3},{2,0},{3,1},{4,6},{5,7},{6,4},{7,5},{8,10},{9,11},{10,... | collective-permute-start | bytes 786440 | tf_op jit(solution)/shard_map/ppermute | solution.py:94
  531.1 16.9 %collective-permute-start.48 = (bf16[128,1024]{1,0:T(8,128)(2,1)}, bf16[128,1024]{1,0:T(8,128)(2,1)}, u32[]{:S(2)}, u32[]{:S(2)}) collective-permute-start(bf16[128,1024]{1,0:T(8,128)(2,1)} %get-tuple-element.311), channel_id=1, source_target_pairs={{0,8},{1,9},{2,10},{3,11},{4,12},{5,13},{6,14},{7,15},{8,0},{9,1},... | collective-permute-start | bytes 786440 | tf_op jit(solution)/shard_map/ppermute | solution.py:94
  531.2 38.4 %collective-permute-start.53 = (bf16[304,768]{1,0:T(8,128)(2,1)S(1)}, bf16[304,768]{1,0:T(8,128)(2,1)}, u32[]{:S(2)}, u32[]{:S(2)}) collective-permute-start(bf16[304,768]{1,0:T(8,128)(2,1)S(1)} %fusion.17), channel_id=1, source_target_pairs={{0,4},{4,0},{10,14},{14,10},{16,20},{20,16},{26,30},{30,26}} | collective-permute-start | bytes 1400840 | tf_op jit(solution)/shard_map/ppermute | solution.py:94
  543.2 88.4 %all-to-all-start.6 = ((bf16[8,64,768]{2,1,0:T(8,128)(2,1)}), bf16[8,64,768]{2,1,0:T(8,128)(2,1)}, u32[]{:S(2)}, u32[]{:S(2)}) async-start(bf16[8,64,768]{2,1,0:T(8,128)(2,1)} %bitcast.114), calls=%async_computation.8 | async-start | bytes 1572864 | tf_op jit(solution)/shard_map/all_to_all | solution.py:794
  547.6 26.9 %collective-permute-start.52 = (bf16[304,768]{1,0:T(8,128)(2,1)S(1)}, bf16[304,768]{1,0:T(8,128)(2,1)S(1)}, u32[]{:S(2)}, u32[]{:S(2)}) collective-permute-start(bf16[304,768]{1,0:T(8,128)(2,1)S(1)} %fusion.16), channel_id=1, source_target_pairs={{0,4},{1,5},{2,6},{3,7},{4,0},{5,1},{6,2},{7,3},{8,12},{9,13},{10,... | collective-permute-start | bytes 1400840 | tf_op jit(solution)/shard_map/ppermute | solution.py:94
  553.6 24.7 %collective-permute-start.49 = (bf16[512,2048]{1,0:T(8,128)(2,1)S(1)}, bf16[512,2048]{1,0:T(8,128)(2,1)}, u32[]{:S(2)}, u32[]{:S(2)}) collective-permute-start(bf16[512,2048]{1,0:T(8,128)(2,1)S(1)} %convolution_convert_fusion), channel_id=1, source_target_pairs={{0,1},{1,0},{2,3},{3,2},{4,5},{5,4},{6,7},{7,6},{8,9},{9,8},{10,11... | collective-permute-start | bytes 6291464 | tf_op jit(solution)/shard_map/ppermute | solution.py:94
  583.4 17.3 %collective-permute-start.54 = (bf16[256,1024]{1,0:T(8,128)(2,1)}, bf16[256,1024]{1,0:T(8,128)(2,1)}, u32[]{:S(2)}, u32[]{:S(2)}) collective-permute-start(bf16[256,1024]{1,0:T(8,128)(2,1)} %get-tuple-element.323), channel_id=1, source_target_pairs={{0,8},{1,9},{2,10},{3,11},{4,12},{5,13},{6,14},{7,15},{8,0},{9,1},... | collective-permute-start | bytes 1572872 | tf_op jit(solution)/shard_map/ppermute | solution.py:94
  583.4 17.3 %collective-permute-start.55 = (bf16[256,1024]{1,0:T(8,128)(2,1)}, bf16[256,1024]{1,0:T(8,128)(2,1)}, u32[]{:S(2)}, u32[]{:S(2)}) collective-permute-start(bf16[256,1024]{1,0:T(8,128)(2,1)} %get-tuple-element.325), channel_id=1, source_target_pairs={{0,2},{1,3},{2,0},{3,1},{4,6},{5,7},{6,4},{7,5},{8,10},{9,11},{10,... | collective-permute-start | bytes 1572872 | tf_op jit(solution)/shard_map/ppermute | solution.py:94
  604.9 17.6 %collective-permute-start.57 = (bf16[128,1024]{1,0:T(8,128)(2,1)}, bf16[128,1024]{1,0:T(8,128)(2,1)S(1)}, u32[]{:S(2)}, u32[]{:S(2)}) collective-permute-start(bf16[128,1024]{1,0:T(8,128)(2,1)} %get-tuple-element.328), channel_id=1, source_target_pairs={{0,8},{1,9},{2,10},{3,11},{4,12},{5,13},{6,14},{7,15},{8,0},{9,1},... | collective-permute-start | bytes 786440 | tf_op jit(solution)/shard_map/ppermute | solution.py:94
  608.6 27.4 %collective-permute-start.80 = (bf16[288,512]{1,0:T(8,128)(2,1)}, bf16[288,512]{1,0:T(8,128)(2,1)}, u32[]{:S(2)}, u32[]{:S(2)}) collective-permute-start(bf16[288,512]{1,0:T(8,128)(2,1)} %slice.300), channel_id=1, source_target_pairs={{0,16},{4,20},{10,26},{14,30},{16,0},{20,4},{26,10},{30,14}} | collective-permute-start | bytes 884744 | tf_op jit(solution)/shard_map/ppermute | solution.py:94
  611.2 30.2 %collective-permute-start.79 = (bf16[288,512]{1,0:T(8,128)(2,1)}, bf16[288,512]{1,0:T(8,128)(2,1)}, u32[]{:S(2)}, u32[]{:S(2)}) collective-permute-start(bf16[288,512]{1,0:T(8,128)(2,1)} %slice.298), channel_id=1, source_target_pairs={{0,16},{1,17},{2,18},{3,19},{4,20},{5,21},{6,22},{7,23},{8,24},{9,... | collective-permute-start | bytes 884744 | tf_op jit(solution)/shard_map/ppermute | solution.py:94
  614.1 34.1 %collective-permute-start.70 = (bf16[304,768]{1,0:T(8,128)(2,1)}, bf16[304,768]{1,0:T(8,128)(2,1)}, u32[]{:S(2)}, u32[]{:S(2)}) collective-permute-start(bf16[304,768]{1,0:T(8,128)(2,1)} %add_convert_fusion.14), channel_id=1, source_target_pairs={{0,16},{4,20},{10,26},{14,30},{16,0},{20,4},{26,10},{30,14}} | collective-permute-start | bytes 1400840 | tf_op jit(solution)/shard_map/ppermute | solution.py:94
  619.6 33.7 %collective-permute-start.69 = (bf16[304,768]{1,0:T(8,128)(2,1)}, bf16[304,768]{1,0:T(8,128)(2,1)}, u32[]{:S(2)}, u32[]{:S(2)}) collective-permute-start(bf16[304,768]{1,0:T(8,128)(2,1)} %add_convert_fusion.15), channel_id=1, source_target_pairs={{0,16},{1,17},{2,18},{3,19},{4,20},{5,21},{6,22},{7,23},{8,24},{9,... | collective-permute-start | bytes 1400840 | tf_op jit(solution)/shard_map/ppermute | solution.py:94
  631.6 55.7 %collective-permute-start.67 = (bf16[576,1024]{1,0:T(8,128)(2,1)}, bf16[576,1024]{1,0:T(8,128)(2,1)}, u32[]{:S(2)}, u32[]{:S(2)}) collective-permute-start(bf16[576,1024]{1,0:T(8,128)(2,1)} %slice.285), channel_id=1, source_target_pairs={{0,4},{4,0},{10,14},{14,10},{16,20},{20,16},{26,30},{30,26}} | collective-permute-start | bytes 3538952 | tf_op jit(solution)/shard_map/ppermute | solution.py:94
  636.0 18.9 %collective-permute-start.59 = (f32[16,256]{1,0:T(8,128)S(1)}, f32[16,256]{1,0:T(8,128)S(1)}, u32[]{:S(2)}, u32[]{:S(2)}) collective-permute-start(f32[16,256]{1,0:T(8,128)S(1)} %add.176), channel_id=1, source_target_pairs={{0,2},{1,3},{2,0},{3,1},{4,6},{5,7},{6,4},{7,5},{8,10},{9,11},{10,... | collective-permute-start | bytes 49160 | tf_op jit(solution)/shard_map/ppermute | solution.py:94
  641.5 20.6 %collective-permute-start.60 = (f32[16,256]{1,0:T(8,128)S(1)}, f32[16,256]{1,0:T(8,128)S(1)}, u32[]{:S(2)}, u32[]{:S(2)}) collective-permute-start(f32[16,256]{1,0:T(8,128)S(1)} %add.176), channel_id=1, source_target_pairs={{0,8},{1,9},{2,10},{3,11},{4,12},{5,13},{6,14},{7,15},{8,0},{9,1},... | collective-permute-start | bytes 49160 | tf_op jit(solution)/shard_map/ppermute | solution.py:94
  657.6 33.0 %all-to-all-start.5 = ((bf16[8,64,640]{2,1,0:T(8,128)(2,1)}), bf16[8,64,640]{2,1,0:T(8,128)(2,1)}, u32[]{:S(2)}, u32[]{:S(2)}) async-start(bf16[8,64,640]{2,1,0:T(8,128)(2,1)} %shard_map.338), calls=%async_computation.6 | async-start | bytes 1310720 | tf_op jit(solution)/shard_map/all_to_all | solution.py:794
  662.1 32.8 %collective-permute-start.65 = (bf16[576,1024]{1,0:T(8,128)(2,1)}, bf16[576,1024]{1,0:T(8,128)(2,1)}, u32[]{:S(2)}, u32[]{:S(2)}) collective-permute-start(bf16[576,1024]{1,0:T(8,128)(2,1)} %slice.281), channel_id=1, source_target_pairs={{0,4},{1,5},{2,6},{3,7},{4,0},{5,1},{6,2},{7,3},{8,12},{9,13},{10,... | collective-permute-start | bytes 3538952 | tf_op jit(solution)/shard_map/ppermute | solution.py:94
  669.2 75.2 %collective-permute-start.62 = (f32[16,256]{1,0:T(8,128)S(1)}, f32[16,256]{1,0:T(8,128)}, u32[]{:S(2)}, u32[]{:S(2)}) collective-permute-start(f32[16,256]{1,0:T(8,128)S(1)} %add_add_fusion.1), channel_id=1, source_target_pairs={{0,16},{1,17},{2,18},{3,19},{4,20},{5,21},{6,22},{7,23},{8,24},{9,... | collective-permute-start | bytes 49160 | tf_op jit(solution)/shard_map/ppermute | solution.py:94
  670.2 74.2 %collective-permute-start.63 = (f32[16,256]{1,0:T(8,128)S(1)}, f32[16,256]{1,0:T(8,128)}, u32[]{:S(2)}, u32[]{:S(2)}) collective-permute-start(f32[16,256]{1,0:T(8,128)S(1)} %add_add_fusion.1), channel_id=1, source_target_pairs={{0,4},{1,5},{2,6},{3,7},{4,0},{5,1},{6,2},{7,3},{8,12},{9,13},{10,... | collective-permute-start | bytes 49160 | tf_op jit(solution)/shard_map/ppermute | solution.py:94
  685.3 17.9 %collective-permute-start.77 = (bf16[304,768]{1,0:T(8,128)(2,1)}, bf16[304,768]{1,0:T(8,128)(2,1)}, u32[]{:S(2)}, u32[]{:S(2)}) collective-permute-start(bf16[304,768]{1,0:T(8,128)(2,1)} %select_select_fusion), channel_id=1, source_target_pairs={{0,8},{1,9},{2,10},{3,11},{4,12},{5,13},{6,14},{7,15},{8,0},{9,1},... | collective-permute-start | bytes 1400840 | tf_op jit(solution)/shard_map/ppermute | solution.py:94
  690.6 46.4 %all-to-all-start.7 = ((bf16[8,64,768]{2,1,0:T(8,128)(2,1)}), bf16[8,64,768]{2,1,0:T(8,128)(2,1)}, u32[]{:S(2)}, u32[]{:S(2)}) async-start(bf16[8,64,768]{2,1,0:T(8,128)(2,1)} %bitcast.113), calls=%async_computation.10 | async-start | bytes 1572864 | tf_op jit(solution)/shard_map/all_to_all | solution.py:794
  694.9 32.2 %collective-permute-start.68 = (bf16[576,512]{1,0:T(8,128)(2,1)}, bf16[576,512]{1,0:T(8,128)(2,1)S(1)}, u32[]{:S(2)}, u32[]{:S(2)}) collective-permute-start(bf16[576,512]{1,0:T(8,128)(2,1)} %slice.326), channel_id=1, source_target_pairs={{0,16},{4,20},{10,26},{14,30},{16,0},{20,4},{26,10},{30,14}} | collective-permute-start | bytes 1769480 | tf_op jit(solution)/shard_map/ppermute | solution.py:94
  698.7 34.7 %collective-permute-start.66 = (bf16[576,512]{1,0:T(8,128)(2,1)S(1)}, bf16[576,512]{1,0:T(8,128)(2,1)S(1)}, u32[]{:S(2)}, u32[]{:S(2)}) collective-permute-start(bf16[576,512]{1,0:T(8,128)(2,1)S(1)} %slice.324), channel_id=1, source_target_pairs={{0,16},{1,17},{2,18},{3,19},{4,20},{5,21},{6,22},{7,23},{8,24},{9,... | collective-permute-start | bytes 1769480 | tf_op jit(solution)/shard_map/ppermute | solution.py:94
  703.2 41.2 %collective-permute-start.64 = (f32[16,256]{1,0:T(8,128)S(1)}, f32[16,256]{1,0:T(8,128)}, u32[]{:S(2)}, u32[]{:S(2)}) collective-permute-start(f32[16,256]{1,0:T(8,128)S(1)} %add_add_fusion.1), channel_id=1, source_target_pairs={{0,20},{1,21},{2,22},{3,23},{4,16},{5,17},{6,18},{7,19},{8,28},{9,... | collective-permute-start | bytes 49160 | tf_op jit(solution)/shard_map/ppermute | solution.py:94
  727.1 25.0 %collective-permute-start.75 = (bf16[1216,768]{1,0:T(8,128)(2,1)}, bf16[1216,768]{1,0:T(8,128)(2,1)}, u32[]{:S(2)}, u32[]{:S(2)}) collective-permute-start(bf16[1216,768]{1,0:T(8,128)(2,1)} %constant_dynamic-update-slice_fusion.21), channel_id=1, source_target_pairs={{0,1},{1,0},{2,3},{3,2},{4,5},{5,4},{6,7},{7,6},{8,9},{9,8},{10,11... | collective-permute-start | bytes 5603336 | tf_op jit(solution)/shard_map/ppermute | solution.py:94
  737.1 25.0 %all-to-all-start.4 = ((bf16[8,64,1152]{2,1,0:T(8,128)(2,1)}), bf16[8,64,1152]{2,1,0:T(8,128)(2,1)S(1)}, u32[]{:S(2)}, u32[]{:S(2)}) async-start(bf16[8,64,1152]{2,1,0:T(8,128)(2,1)} %shard_map.335), calls=%async_computation.5 | async-start | bytes 2359296 | tf_op jit(solution)/shard_map/all_to_all | solution.py:794
  (96 other events, 718.3 us)
Sparse Core Ops, SparseCore 0:
  129.4 68.1 all-gather.3
  199.4 69.2 all-gather.7
  270.5 69.2 all-gather.5
  385.3 69.3 reduce-scatter.3
  458.1 69.0 reduce-scatter.5
  530.0 69.1 reduce-scatter.7

commit v3 on v2

--- a/solution.py
+++ b/solution.py
@@ -119,7 +119,7 @@
         out_specs=[pl.BlockSpec(memory_space=pltpu.VMEM)] * len(outs),
         out_shape=[jax.ShapeDtypeStruct(s, d) for s, d in outs],
         scratch_shapes=list(scratch),
-        compiler_params=pltpu.CompilerParams(vmem_limit_bytes=60 * 1024 * 1024),
+        compiler_params=pltpu.CompilerParams(vmem_limit_bytes=12 * 1024 * 1024),
         cost_estimate=pl.CostEstimate(
             flops=us * 10**9, bytes_accessed=us * 3 * 10**6, transcendentals=0
         ),

time: 780 us -> 758 us (0.972)
  Pallas kernels: 194 us -> 96.4 us
  local copies, waits for them, and re-layouts: 61.5 us -> 124 us
  waiting for transfers between devices: 196 us -> 212 us
  other arithmetic: 33 us -> 20.5 us
  starting transfers between devices: 137 us -> 149 us
    pallas_call x38, Pallas kernels: 194 us -> 96.4 us  [kernel_call(): pl.pallas_call(kernel, in_specs=specs, out_specs=[pl.BlockSpec(memory_spa...]
    unnamed x153 -> x283, local copies, waits for them, and re-layouts: 29.2 us -> 92.4 us
    ppermute x80, starting transfers between devices: 97.3 us -> 111 us  [swap(): return lax.ppermute(v, AXIS, pairs)]
  transfers between devices with their start and end apart: 95 -> 95, of which waited for: 29 -> 30; matrix products, arithmetic and copies ran while one was open for 27% -> 26% of each run, Pallas kernels for 23% -> 12%
where the time goes in v3:
time: 758 us; the launch traced here: 750 us
  waiting for transfers between devices  212 us (28%)
  starting transfers between devices  149 us (20%)
  matrix products  132 us (17%)
  local copies, waits for them, and re-layouts  124 us (16%)
  Pallas kernels  96.4 us (13%)
  other arithmetic  20.5 us (3%)
  between operations  16.4 us (2%)
    ppermute x80, waiting for transfers between devices, swap(): return lax.ppermute(v, AXIS, pairs)  161 us
    ppermute x80, starting transfers between devices, swap(): return lax.ppermute(v, AXIS, pairs)  111 us
    pallas_call x38, Pallas kernels, kernel_call(): pl.pallas_call(kernel, in_specs=specs, out_specs=[pl.BlockSpec(memory_spa...  96.4 us
    unnamed x283, local copies, waits for them, and re-layouts  92.4 us
    dot_general x12, matrix products, dot_first(): lax.dot_general(a, b, (((0,), (0,)), ((), ())), preferred_element_type=F32)  49.3 us
    dot_general x10, matrix products, dot(): lax.dot_general(a, b, (((1,), (0,)), ((), ())), preferred_element_type=F32)  43.7 us
    dot_general x11, matrix products, dot_last(): lax.dot_general(a, b, (((1,), (1,)), ((), ())), preferred_element_type=F32)  38.9 us
    all_to_all x8, starting transfers between devices, exchange(): return lax.all_to_all(v, AXIS, 0, 0, axis_index_groups=groups, tiled=True)  34.7 us
  transfers between devices with their start and end apart: 95, of which 30 were waited for; matrix products, arithmetic and copies ran while one was open for 26% of the time, Pallas kernels for 12%

profile of v3, /device:TPU:0, one launch (start us, length us, event | category | flops | bytes accessed | tf_op | source)
XLA Modules:
  0.0 750.1 jit_solution(10696804899452630862)
XLA Ops:
  12.0 5.4 all-to-all-start
  24.9 5.9 all-to-all-done.parts
  30.9 5.1 all-to-all-start.1
  55.5 18.9 %collective-permute-done.3 = bf16[144,2048]{1,0:T(8,128)(2,1)} collective-permute-done((bf16[144,2048]{1,0:T(8,128)(2,1)}, bf16[144,2048]{1,0:T(8,128)(2,1)}, u32[]{:S(2)}, u32[]{:S(2)}) %collective-permute-start.3) | collective-permute-done | bytes 589856 | tf_op jit(solution)/shard_map/ppermute | solution.py:94
  86.1 4.4 all-to-all-start.2
  100.6 3.6 collective-permute-start.10
  109.8 3.3 collective-permute-start.14
  114.2 15.5 %all-to-all-done.2 = bf16[8,192,768]{2,1,0:T(8,128)(2,1)} async-done(((bf16[8,192,768]{2,1,0:T(8,128)(2,1)}), bf16[8,192,768]{2,1,0:T(8,128)(2,1)}, u32[]{:S(2)}, u32[]{:S(2)}) %all-to-all-start.2) | async-done | bytes 2359328 | tf_op jit(solution)/shard_map/all_to_all | solution.py:794
  144.3 5.5 fusion.32.lin_mine.gate_mine
  149.8 5.5 fusion.33.lin_theirs.gate_theirs
  155.7 20.1 %shard_map.312 = (f32[5,1024,128]{2,1,0:T(8,128)S(1)}, bf16[1024,640]{1,0:T(8,128)(2,1)S(1)}, f32[5,1024,128]{2,1,0:T(8,128)S(1)}, f32[5,1024,128]{2,1,0:T(8,128...) custom-call(f32[512,1280]{1,0:T(8,128)S(1)} %fusion.32.lin_mine.gate, ...), custom_call_target="tpu_custom_call" | custom-call | flops 28999999488 | bytes 87000000 | tf_op jit(solution)/shard_map/pallas_call | solution.py:116
  202.6 3.7 collective-permute-done.20
  223.7 19.6 %collective-permute-done.22.recv_a = bf16[256,1024]{1,0:T(8,128)(2,1)S(1)} collective-permute-done((bf16[256,1024]{1,0:T(8,128)(2,1)}, bf16[256,1024]{1,0:T(8,128)(2,1)S(1)}, u32[]{:S(2)}, u32[]{:S(2)}) %collective-permute-start.22) | collective-permute-done | bytes 524320 | tf_op jit(solution)/shard_map/ppermute | solution.py:94
  250.2 5.6 fusion.35
  257.4 16.4 %collective-permute-done.25.rb = bf16[128,1024]{1,0:T(8,128)(2,1)} collective-permute-done((bf16[128,1024]{1,0:T(8,128)(2,1)S(1)}, bf16[128,1024]{1,0:T(8,128)(2,1)}, u32[]{:S(2)}, u32[]{:S(2)}) %collective-permute-start.25) | collective-permute-done | bytes 262176 | tf_op jit(solution)/shard_map/ppermute | solution.py:94
  277.6 4.6 fusion.36
  282.2 11.5 %collective-permute-done.26 = bf16[128,2048]{1,0:T(8,128)(2,1)S(1)} collective-permute-done((bf16[128,2048]{1,0:T(8,128)(2,1)S(1)}, bf16[128,2048]{1,0:T(8,128)(2,1)S(1)}, u32[]{:S(2)}, u32[]{:S(2)}) %collective-permute-start.26) | collective-permute-done | bytes 524320 | tf_op jit(solution)/shard_map/ppermute | solution.py:94
  300.9 3.7 collective-permute-done.30
  305.4 4.5 collective-permute-done.31
  309.9 5.5 fusion.37
  315.3 28.7 %all-gather.6.cloned.1.call-done = bf16[2048,768]{1,0:T(8,128)(2,1)} async-done(((bf16[512,768]{1,0:T(8,128)(2,1)}), bf16[2048,768]{1,0:T(8,128)(2,1)}) %all-gather.6.cloned.1.call-update) | async-done | bytes 3145744 | tf_op jit(solution)/shard_map/all_gather | solution.py:888
  344.0 6.2 multiply_convert_fusion
  354.8 3.5 fusion.39
  358.4 4.4 multiply_convert_fusion.1
  371.1 3.5 fusion.41
  374.6 5.3 add_convert_fusion.3
  379.9 4.2 collective-permute-done.33.recv_a
  392.0 3.6 fusion.42
  395.6 5.3 add_convert_fusion.2
  411.0 3.8 fusion.43
  414.8 5.4 add_convert_fusion.1
  420.2 5.4 convolution_convert_fusion.1
  426.5 3.8 fusion.44.mine
  430.4 3.8 collective-permute-done.37
  442.2 6.8 collective-permute-done.40
  450.9 4.4 fusion.45.gm_mine
  455.3 3.9 fusion.46.gm_theirs
  459.3 8.9 %shard_map.324 = (f32[5,1024,128]{2,1,0:T(8,128)S(1)}, f32[5,1024,128]{2,1,0:T(8,128)S(1)}, f32[16,640]{1,0:T(8,128)S(1)}) custom-call(f32[512,640]{1,0:T(8,128)S(1)} %fusion.45.gm_mine, f32[512,640]{1,0:T(8,128)S(1)} %fusion.46.gm_theirs, f32[5,1024,128]{2,1,0:T(8,128)S(1)} %copy-done.72, f32[5,1024,128]{2,1,0:T(8,128)S(1)} %copy-done.80), custom_call_target="tpu_custom_call" | custom-call | flops 16000000000 | bytes 48000000 | tf_op jit(solution)/shard_map/pallas_call | solution.py:116
  472.7 4.6 all-to-all-start.3
  482.1 3.2 fusion.12
  485.3 4.8 add_convert_fusion.4
  511.5 11.2 %shard_map.327 = (bf16[1024,640]{1,0:T(8,128)(2,1)S(1)}, bf16[1024,640]{1,0:T(8,128)(2,1)S(1)}, f32[5,1024,128]{2,1,0:T(8,128)S(1)}, f32[8,640]{1,0:T(8,128)S(1)}, f32[24,640]{1,0:T(8,128)S(1)}) custom-call(f32[5,1024,128]{2,1,0:T(8,128)S(1)} %copy-done.83, f32[5,1024,128]{2,1,0:T(8,128)S(1)} %copy-done.85, f32[8,8,640]{2,1,0:T(8,128)S(1)} %shard_map.326.from_later, ...), custom_call_target="tpu_custom_call" | custom-call | flops 20999999488 | bytes 63000000 | tf_op jit(solution)/shard_map/pallas_call | solution.py:116
  537.1 3.3 collective-permute-start.53
  540.4 4.9 shard_map.330
  545.4 4.3 all-to-all-start.6
  550.4 5.6 convolution_convert_fusion
  556.4 4.9 fusion.48.mine
  561.5 13.5 %collective-permute-done.53 = bf16[304,768]{1,0:T(8,128)(2,1)} collective-permute-done((bf16[304,768]{1,0:T(8,128)(2,1)}, bf16[304,768]{1,0:T(8,128)(2,1)}, u32[]{:S(2)}, u32[]{:S(2)}) %collective-permute-start.53) | collective-permute-done | bytes 466976 | tf_op jit(solution)/shard_map/ppermute | solution.py:94
  576.3 3.6 collective-permute-done.52
  583.9 5.5 fusion.8
  589.4 6.4 add_convert_fusion
  633.0 3.2 collective-permute-start.60
  637.9 3.2 collective-permute-start.61
  646.2 3.9 all-to-all-start.5
  651.2 4.0 collective-permute-start.76
  662.3 3.3 collective-permute-done.76
  668.9 3.1 collective-permute-done.73
  672.0 3.1 collective-permute-start.77
  678.4 3.5 all-to-all-start.7
  682.0 4.7 collective-permute-start.68
  695.7 18.2 %collective-permute-done.68 = bf16[576,512]{1,0:T(8,128)(2,1)S(1)} collective-permute-done((bf16[576,512]{1,0:T(8,128)(2,1)}, bf16[576,512]{1,0:T(8,128)(2,1)S(1)}, u32[]{:S(2)}, u32[]{:S(2)}) %collective-permute-start.68) | collective-permute-done | bytes 589856 | tf_op jit(solution)/shard_map/ppermute | solution.py:94
  714.1 6.6 collective-permute-done.66
  722.3 3.6 all-to-all-start.4
  733.0 6.4 shard_map.337
  (585 shorter events, 312.0 us)
Async XLA Ops:
  12.0 18.9 %all-to-all-start = ((bf16[8,64,896]{2,1,0:T(8,128)(2,1)}), bf16[8,64,896]{2,1,0:T(8,128)(2,1)S(1)}, u32[]{:S(2)}, u32[]{:S(2)}) async-start(bf16[8,64,896]{2,1,0:T(8,128)(2,1)} %get-tuple-element.187), calls=%async_computation | async-start | bytes 1835008 | tf_op jit(solution)/shard_map/all_to_all | solution.py:794
  30.9 23.4 %all-to-all-start.1 = ((bf16[8,64,896]{2,1,0:T(8,128)(2,1)}), bf16[8,64,896]{2,1,0:T(8,128)(2,1)S(1)}, u32[]{:S(2)}, u32[]{:S(2)}) async-start(bf16[8,64,896]{2,1,0:T(8,128)(2,1)} %get-tuple-element.192), calls=%async_computation.1 | async-start | bytes 1835008 | tf_op jit(solution)/shard_map/all_to_all | solution.py:794
  43.6 30.8 %collective-permute-start.3 = (bf16[144,2048]{1,0:T(8,128)(2,1)}, bf16[144,2048]{1,0:T(8,128)(2,1)}, u32[]{:S(2)}, u32[]{:S(2)}) collective-permute-start(bf16[144,2048]{1,0:T(8,128)(2,1)} %shard_map.307), channel_id=1, source_target_pairs={{0,8},{1,9},{2,10},{3,11},{4,12},{5,13},{6,14},{7,15},{8,0},{9,1},... | collective-permute-start | bytes 1769480 | tf_op jit(solution)/shard_map/ppermute | solution.py:94
  45.8 28.6 %collective-permute-start.4 = (bf16[144,2048]{1,0:T(8,128)(2,1)}, bf16[144,2048]{1,0:T(8,128)(2,1)}, u32[]{:S(2)}, u32[]{:S(2)}) collective-permute-start(bf16[144,2048]{1,0:T(8,128)(2,1)} %shard_map.307), channel_id=1, source_target_pairs={{0,2},{1,3},{2,0},{3,1},{4,6},{5,7},{6,4},{7,5},{8,10},{9,11},{10,... | collective-permute-start | bytes 1769480 | tf_op jit(solution)/shard_map/ppermute | solution.py:94
  47.1 27.3 %collective-permute-start.1 = (bf16[576,512]{1,0:T(8,128)(2,1)}, bf16[576,512]{1,0:T(8,128)(2,1)S(1)}, u32[]{:S(2)}, u32[]{:S(2)}) collective-permute-start(bf16[576,512]{1,0:T(8,128)(2,1)} %get-tuple-element.202.refs_0_), channel_id=1, source_target_pairs={{0,16},{1,17},{2,18},{3,19},{4,20},{5,21},{6,22},{7,23},{8,24},{9,... | collective-permute-start | bytes 1769480 | tf_op jit(solution)/shard_map/ppermute | solution.py:94
  49.7 24.7 %collective-permute-start.2 = (bf16[576,512]{1,0:T(8,128)(2,1)}, bf16[576,512]{1,0:T(8,128)(2,1)}, u32[]{:S(2)}, u32[]{:S(2)}) collective-permute-start(bf16[576,512]{1,0:T(8,128)(2,1)} %get-tuple-element.202.refs_0_), channel_id=1, source_target_pairs={{0,4},{1,5},{2,6},{3,7},{4,0},{5,1},{6,2},{7,3},{8,12},{9,13},{10,... | collective-permute-start | bytes 1769480 | tf_op jit(solution)/shard_map/ppermute | solution.py:94
  76.4 19.8 %collective-permute-start.8 = (bf16[80,2048]{1,0:T(8,128)(2,1)}, bf16[80,2048]{1,0:T(8,128)(2,1)}, u32[]{:S(2)}, u32[]{:S(2)}) collective-permute-start(bf16[80,2048]{1,0:T(8,128)(2,1)} %slice.235), channel_id=1, source_target_pairs={{0,8},{1,9},{2,10},{3,11},{4,12},{5,13},{6,14},{7,15},{8,0},{9,1},... | collective-permute-start | bytes 983048 | tf_op jit(solution)/shard_map/ppermute | solution.py:94
  82.0 17.6 %collective-permute-start.6 = (bf16[864,512]{1,0:T(8,128)(2,1)}, bf16[864,512]{1,0:T(8,128)(2,1)S(1)}, u32[]{:S(2)}, u32[]{:S(2)}) collective-permute-start(bf16[864,512]{1,0:T(8,128)(2,1)} %shard_map.309.refs_4_), channel_id=1, source_target_pairs={{0,16},{4,20},{10,26},{14,30},{16,0},{20,4},{26,10},{30,14}} | collective-permute-start | bytes 2654216 | tf_op jit(solution)/shard_map/ppermute | solution.py:94
  86.1 43.7 %all-to-all-start.2 = ((bf16[8,192,768]{2,1,0:T(8,128)(2,1)}), bf16[8,192,768]{2,1,0:T(8,128)(2,1)}, u32[]{:S(2)}, u32[]{:S(2)}) async-start(bf16[8,192,768]{2,1,0:T(8,128)(2,1)} %shard_map.311), calls=%async_computation.2 | async-start | bytes 4718592 | tf_op jit(solution)/shard_map/all_to_all | solution.py:794
  90.5 159.7 %all-gather.4.cloned.1.call-start = ((), (), s32[]{:S(2)}) async-start(), calls=%async_computation.11 | async-start | bytes 3932160 | tf_op jit(solution)/shard_map/all_gather | solution.py:888
  100.6 32.5 %collective-permute-start.10 = (bf16[864,512]{1,0:T(8,128)(2,1)S(1)}, bf16[864,512]{1,0:T(8,128)(2,1)}, u32[]{:S(2)}, u32[]{:S(2)}) collective-permute-start(bf16[864,512]{1,0:T(8,128)(2,1)S(1)} %collective-permute-done.6.refs_5_), channel_id=1, source_target_pairs={{0,4},{4,0},{10,14},{14,10},{16,20},{20,16},{26,30},{30,26}} | collective-permute-start | bytes 2654216 | tf_op jit(solution)/shard_map/ppermute | solution.py:94
  104.2 28.9 %collective-permute-start.9 = (bf16[864,512]{1,0:T(8,128)(2,1)}, bf16[864,512]{1,0:T(8,128)(2,1)}, u32[]{:S(2)}, u32[]{:S(2)}) collective-permute-start(bf16[864,512]{1,0:T(8,128)(2,1)} %shard_map.309.refs_4_), channel_id=1, source_target_pairs={{0,4},{4,0},{10,14},{14,10},{16,20},{20,16},{26,30},{30,26}} | collective-permute-start | bytes 2654216 | tf_op jit(solution)/shard_map/ppermute | solution.py:94
  109.8 40.0 %collective-permute-start.11 = (bf16[512,2048]{1,0:T(8,128)(2,1)}, bf16[512,2048]{1,0:T(8,128)(2,1)}, u32[]{:S(2)}, u32[]{:S(2)}) collective-permute-start(bf16[512,2048]{1,0:T(8,128)(2,1)} %slice_dynamic-update-slice_fusion.3), channel_id=1, source_target_pairs={{0,1},{1,0},{2,3},{3,2},{4,5},{5,4},{6,7},{7,6},{8,9},{9,8},{10,11... | collective-permute-start | bytes 6291464 | tf_op jit(solution)/shard_map/ppermute | solution.py:94
  109.8 27.1 %collective-permute-start.14 = (bf16[288,512]{1,0:T(8,128)(2,1)S(1)}, bf16[288,512]{1,0:T(8,128)(2,1)}, u32[]{:S(2)}, u32[]{:S(2)}) collective-permute-start(bf16[288,512]{1,0:T(8,128)(2,1)S(1)} %copy-done.27), channel_id=1, source_target_pairs={{0,16},{1,17},{2,18},{3,19},{4,20},{5,21},{6,22},{7,23},{8,24},{9,... | collective-permute-start | bytes 884744 | tf_op jit(solution)/shard_map/ppermute | solution.py:94
  132.8 172.5 %all-gather.8.cloned.1.call-start = ((), (), s32[]{:S(2)}) async-start(), calls=%async_computation.13 | async-start | bytes 3932160 | tf_op jit(solution)/shard_map/all_gather | solution.py:888
  139.1 60.1 %collective-permute-start.16 = (bf16[288,512]{1,0:T(8,128)(2,1)}, bf16[288,512]{1,0:T(8,128)(2,1)}, u32[]{:S(2)}, u32[]{:S(2)}) collective-permute-start(bf16[288,512]{1,0:T(8,128)(2,1)} %collective-permute-done.14.refs_1_), channel_id=1, source_target_pairs={{0,4},{1,5},{2,6},{3,7},{4,0},{5,1},{6,2},{7,3},{8,12},{9,13},{10,... | collective-permute-start | bytes 884744 | tf_op jit(solution)/shard_map/ppermute | solution.py:94
  140.4 58.9 %collective-permute-start.15 = (bf16[288,512]{1,0:T(8,128)(2,1)S(1)}, bf16[288,512]{1,0:T(8,128)(2,1)}, u32[]{:S(2)}, u32[]{:S(2)}) collective-permute-start(bf16[288,512]{1,0:T(8,128)(2,1)S(1)} %copy-done.27), channel_id=1, source_target_pairs={{0,4},{1,5},{2,6},{3,7},{4,0},{5,1},{6,2},{7,3},{8,12},{9,13},{10,... | collective-permute-start | bytes 884744 | tf_op jit(solution)/shard_map/ppermute | solution.py:94
  141.2 46.7 %collective-permute-start.17 = (bf16[128,2048]{1,0:T(8,128)(2,1)S(1)}, bf16[128,2048]{1,0:T(8,128)(2,1)}, u32[]{:S(2)}, u32[]{:S(2)}) collective-permute-start(bf16[128,2048]{1,0:T(8,128)(2,1)S(1)} %copy-done.6), channel_id=1, source_target_pairs={{0,8},{1,9},{2,10},{3,11},{4,12},{5,13},{6,14},{7,15},{8,0},{9,1},... | collective-permute-start | bytes 1572872 | tf_op jit(solution)/shard_map/ppermute | solution.py:94
  141.2 46.7 %collective-permute-start.18 = (bf16[128,2048]{1,0:T(8,128)(2,1)S(1)}, bf16[128,2048]{1,0:T(8,128)(2,1)}, u32[]{:S(2)}, u32[]{:S(2)}) collective-permute-start(bf16[128,2048]{1,0:T(8,128)(2,1)S(1)} %copy-done.6), channel_id=1, source_target_pairs={{0,2},{1,3},{2,0},{3,1},{4,6},{5,7},{6,4},{7,5},{8,10},{9,11},{10,... | collective-permute-start | bytes 1572872 | tf_op jit(solution)/shard_map/ppermute | solution.py:94
  186.5 15.9 %collective-permute-start.13 = (f32[16,640]{1,0:T(8,128)S(1)}, f32[16,640]{1,0:T(8,128)S(1)}, u32[]{:S(2)}, u32[]{:S(2)}) collective-permute-start(f32[16,640]{1,0:T(8,128)S(1)} %get-tuple-element.232.refs_0_), channel_id=1, source_target_pairs={{0,4},{1,5},{2,6},{3,7},{4,0},{5,1},{6,2},{7,3},{8,12},{9,13},{10,... | collective-permute-start | bytes 122888 | tf_op jit(solution)/shard_map/ppermute | solution.py:94
  187.8 156.2 %all-gather.6.cloned.1.call-start = ((), (), s32[]{:S(2)}) async-start(), calls=%async_computation.12 | async-start | bytes 3932160 | tf_op jit(solution)/shard_map/all_gather | solution.py:888
  221.7 55.9 %collective-permute-start.28 = (bf16[512,2048]{1,0:T(8,128)(2,1)}, bf16[512,2048]{1,0:T(8,128)(2,1)}, u32[]{:S(2)}, u32[]{:S(2)}) collective-permute-start(bf16[512,2048]{1,0:T(8,128)(2,1)} %constant_dynamic-update-slice_fusion.6), channel_id=1, source_target_pairs={{0,1},{1,0},{2,3},{3,2},{4,5},{5,4},{6,7},{7,6},{8,9},{9,8},{10,11... | collective-permute-start | bytes 6291464 | tf_op jit(solution)/shard_map/ppermute | solution.py:94
  222.2 21.2 %collective-permute-start.22 = (bf16[256,1024]{1,0:T(8,128)(2,1)}, bf16[256,1024]{1,0:T(8,128)(2,1)S(1)}, u32[]{:S(2)}, u32[]{:S(2)}) collective-permute-start(bf16[256,1024]{1,0:T(8,128)(2,1)} %get-tuple-element.240), channel_id=1, source_target_pairs={{0,8},{1,9},{2,10},{3,11},{4,12},{5,13},{6,14},{7,15},{8,0},{9,1},... | collective-permute-start | bytes 1572872 | tf_op jit(solution)/shard_map/ppermute | solution.py:94
  222.2 21.2 %collective-permute-start.23 = (bf16[256,1024]{1,0:T(8,128)(2,1)S(1)}, bf16[256,1024]{1,0:T(8,128)(2,1)}, u32[]{:S(2)}, u32[]{:S(2)}) collective-permute-start(bf16[256,1024]{1,0:T(8,128)(2,1)S(1)} %get-tuple-element.242), channel_id=1, source_target_pairs={{0,2},{1,3},{2,0},{3,1},{4,6},{5,7},{6,4},{7,5},{8,10},{9,11},{10,... | collective-permute-start | bytes 1572872 | tf_op jit(solution)/shard_map/ppermute | solution.py:94
  223.7 249.0 %reduce-scatter.4.cloned.1.call-start = ((), (), s32[]{:S(2)}) async-start(), calls=%async_computation.14 | async-start | bytes 3932160 | tf_op jit(solution)/shard_map/reduce_scatter | solution.py:1080
  250.2 23.6 %collective-permute-start.25 = (bf16[128,1024]{1,0:T(8,128)(2,1)S(1)}, bf16[128,1024]{1,0:T(8,128)(2,1)}, u32[]{:S(2)}, u32[]{:S(2)}) collective-permute-start(bf16[128,1024]{1,0:T(8,128)(2,1)S(1)} %get-tuple-element.245), channel_id=1, source_target_pairs={{0,8},{1,9},{2,10},{3,11},{4,12},{5,13},{6,14},{7,15},{8,0},{9,1},... | collective-permute-start | bytes 786440 | tf_op jit(solution)/shard_map/ppermute | solution.py:94
  276.3 17.4 %collective-permute-start.26 = (bf16[128,2048]{1,0:T(8,128)(2,1)S(1)}, bf16[128,2048]{1,0:T(8,128)(2,1)S(1)}, u32[]{:S(2)}, u32[]{:S(2)}) collective-permute-start(bf16[128,2048]{1,0:T(8,128)(2,1)S(1)} %get-tuple-element.251), channel_id=1, source_target_pairs={{0,8},{1,9},{2,10},{3,11},{4,12},{5,13},{6,14},{7,15},{8,0},{9,1},... | collective-permute-start | bytes 1572872 | tf_op jit(solution)/shard_map/ppermute | solution.py:94
  276.3 17.4 %collective-permute-start.27 = (bf16[128,2048]{1,0:T(8,128)(2,1)S(1)}, bf16[128,2048]{1,0:T(8,128)(2,1)S(1)}, u32[]{:S(2)}, u32[]{:S(2)}) collective-permute-start(bf16[128,2048]{1,0:T(8,128)(2,1)S(1)} %get-tuple-element.251), channel_id=1, source_target_pairs={{0,2},{1,3},{2,0},{3,1},{4,6},{5,7},{6,4},{7,5},{8,10},{9,11},{10,... | collective-permute-start | bytes 1572872 | tf_op jit(solution)/shard_map/ppermute | solution.py:94
  388.8 156.6 %reduce-scatter.6.cloned.1.call-start = ((), (), s32[]{:S(2)}) async-start(), calls=%async_computation.15 | async-start | bytes 3932160 | tf_op jit(solution)/shard_map/reduce_scatter | solution.py:1080
  408.3 215.1 %reduce-scatter.8.cloned.1.call-start = ((), (), s32[]{:S(2)}) async-start(), calls=%async_computation.16 | async-start | bytes 3932160 | tf_op jit(solution)/shard_map/reduce_scatter | solution.py:1080
  408.6 25.6 %collective-permute-start.37 = (bf16[128,2048]{1,0:T(8,128)(2,1)S(1)}, bf16[128,2048]{1,0:T(8,128)(2,1)S(1)}, u32[]{:S(2)}, u32[]{:S(2)}) collective-permute-start(bf16[128,2048]{1,0:T(8,128)(2,1)S(1)} %get-tuple-element.270), channel_id=1, source_target_pairs={{0,8},{1,9},{2,10},{3,11},{4,12},{5,13},{6,14},{7,15},{8,0},{9,1},... | collective-permute-start | bytes 1572872 | tf_op jit(solution)/shard_map/ppermute | solution.py:94
  411.0 23.2 %collective-permute-start.38 = (bf16[128,2048]{1,0:T(8,128)(2,1)S(1)}, bf16[128,2048]{1,0:T(8,128)(2,1)}, u32[]{:S(2)}, u32[]{:S(2)}) collective-permute-start(bf16[128,2048]{1,0:T(8,128)(2,1)S(1)} %get-tuple-element.270), channel_id=1, source_target_pairs={{0,2},{1,3},{2,0},{3,1},{4,6},{5,7},{6,4},{7,5},{8,10},{9,11},{10,... | collective-permute-start | bytes 1572872 | tf_op jit(solution)/shard_map/ppermute | solution.py:94
  450.4 39.7 %collective-permute-start.44 = (bf16[512,2048]{1,0:T(8,128)(2,1)}, bf16[512,2048]{1,0:T(8,128)(2,1)}, u32[]{:S(2)}, u32[]{:S(2)}) collective-permute-start(bf16[512,2048]{1,0:T(8,128)(2,1)} %convolution_convert_fusion.1), channel_id=1, source_target_pairs={{0,1},{1,0},{2,3},{3,2},{4,5},{5,4},{6,7},{7,6},{8,9},{9,8},{10,11... | collective-permute-start | bytes 6291464 | tf_op jit(solution)/shard_map/ppermute | solution.py:94
  471.2 27.4 %collective-permute-start.42 = (f32[16,640]{1,0:T(8,128)S(1)}, f32[16,640]{1,0:T(8,128)}, u32[]{:S(2)}, u32[]{:S(2)}) collective-permute-start(f32[16,640]{1,0:T(8,128)S(1)} %get-tuple-element.289.refs_0_), channel_id=1, source_target_pairs={{0,4},{1,5},{2,6},{3,7},{4,0},{5,1},{6,2},{7,3},{8,12},{9,13},{10,... | collective-permute-start | bytes 122888 | tf_op jit(solution)/shard_map/ppermute | solution.py:94
  472.7 25.9 %all-to-all-start.3 = ((bf16[8,64,768]{2,1,0:T(8,128)(2,1)}), bf16[8,64,768]{2,1,0:T(8,128)(2,1)}, u32[]{:S(2)}, u32[]{:S(2)}) async-start(bf16[8,64,768]{2,1,0:T(8,128)(2,1)} %bitcast.121), calls=%async_computation.4 | async-start | bytes 1572864 | tf_op jit(solution)/shard_map/all_to_all | solution.py:794
  495.0 37.3 %collective-permute-start.45 = (bf16[256,1024]{1,0:T(8,128)(2,1)}, bf16[256,1024]{1,0:T(8,128)(2,1)}, u32[]{:S(2)}, u32[]{:S(2)}) collective-permute-start(bf16[256,1024]{1,0:T(8,128)(2,1)} %get-tuple-element.304), channel_id=1, source_target_pairs={{0,8},{1,9},{2,10},{3,11},{4,12},{5,13},{6,14},{7,15},{8,0},{9,1},... | collective-permute-start | bytes 1572872 | tf_op jit(solution)/shard_map/ppermute | solution.py:94
  497.1 35.2 %collective-permute-start.46 = (bf16[256,1024]{1,0:T(8,128)(2,1)}, bf16[256,1024]{1,0:T(8,128)(2,1)}, u32[]{:S(2)}, u32[]{:S(2)}) collective-permute-start(bf16[256,1024]{1,0:T(8,128)(2,1)} %get-tuple-element.306), channel_id=1, source_target_pairs={{0,2},{1,3},{2,0},{3,1},{4,6},{5,7},{6,4},{7,5},{8,10},{9,11},{10,... | collective-permute-start | bytes 1572872 | tf_op jit(solution)/shard_map/ppermute | solution.py:94
  527.0 53.0 %collective-permute-start.50 = (bf16[288,1024]{1,0:T(8,128)(2,1)}, bf16[288,1024]{1,0:T(8,128)(2,1)}, u32[]{:S(2)}, u32[]{:S(2)}) collective-permute-start(bf16[288,1024]{1,0:T(8,128)(2,1)} %get-tuple-element.374), channel_id=1, source_target_pairs={{0,4},{1,5},{2,6},{3,7},{4,0},{5,1},{6,2},{7,3},{8,12},{9,13},{10,... | collective-permute-start | bytes 1769480 | tf_op jit(solution)/shard_map/ppermute | solution.py:94
  528.4 51.6 %collective-permute-start.51 = (bf16[288,1024]{1,0:T(8,128)(2,1)}, bf16[288,1024]{1,0:T(8,128)(2,1)}, u32[]{:S(2)}, u32[]{:S(2)}) collective-permute-start(bf16[288,1024]{1,0:T(8,128)(2,1)} %get-tuple-element.373), channel_id=1, source_target_pairs={{0,4},{4,0},{10,14},{14,10},{16,20},{20,16},{26,30},{30,26}} | collective-permute-start | bytes 1769480 | tf_op jit(solution)/shard_map/ppermute | solution.py:94
  537.1 37.9 %collective-permute-start.53 = (bf16[304,768]{1,0:T(8,128)(2,1)}, bf16[304,768]{1,0:T(8,128)(2,1)}, u32[]{:S(2)}, u32[]{:S(2)}) collective-permute-start(bf16[304,768]{1,0:T(8,128)(2,1)} %fusion.17), channel_id=1, source_target_pairs={{0,4},{4,0},{10,14},{14,10},{16,20},{20,16},{26,30},{30,26}} | collective-permute-start | bytes 1400840 | tf_op jit(solution)/shard_map/ppermute | solution.py:94
  545.4 78.1 %all-to-all-start.6 = ((bf16[8,64,768]{2,1,0:T(8,128)(2,1)}), bf16[8,64,768]{2,1,0:T(8,128)(2,1)S(1)}, u32[]{:S(2)}, u32[]{:S(2)}) async-start(bf16[8,64,768]{2,1,0:T(8,128)(2,1)} %bitcast.120), calls=%async_computation.8 | async-start | bytes 1572864 | tf_op jit(solution)/shard_map/all_to_all | solution.py:794
  549.7 30.2 %collective-permute-start.52 = (bf16[304,768]{1,0:T(8,128)(2,1)}, bf16[304,768]{1,0:T(8,128)(2,1)S(1)}, u32[]{:S(2)}, u32[]{:S(2)}) collective-permute-start(bf16[304,768]{1,0:T(8,128)(2,1)} %fusion.16), channel_id=1, source_target_pairs={{0,4},{1,5},{2,6},{3,7},{4,0},{5,1},{6,2},{7,3},{8,12},{9,13},{10,... | collective-permute-start | bytes 1400840 | tf_op jit(solution)/shard_map/ppermute | solution.py:94
  556.0 26.3 %collective-permute-start.49 = (bf16[512,2048]{1,0:T(8,128)(2,1)S(1)}, bf16[512,2048]{1,0:T(8,128)(2,1)S(1)}, u32[]{:S(2)}, u32[]{:S(2)}) collective-permute-start(bf16[512,2048]{1,0:T(8,128)(2,1)S(1)} %convolution_convert_fusion), channel_id=1, source_target_pairs={{0,1},{1,0},{2,3},{3,2},{4,5},{5,4},{6,7},{7,6},{8,9},{9,8},{10,11... | collective-permute-start | bytes 6291464 | tf_op jit(solution)/shard_map/ppermute | solution.py:94
  582.7 15.6 %collective-permute-start.54 = (bf16[256,1024]{1,0:T(8,128)(2,1)S(1)}, bf16[256,1024]{1,0:T(8,128)(2,1)S(1)}, u32[]{:S(2)}, u32[]{:S(2)}) collective-permute-start(bf16[256,1024]{1,0:T(8,128)(2,1)S(1)} %get-tuple-element.323), channel_id=1, source_target_pairs={{0,8},{1,9},{2,10},{3,11},{4,12},{5,13},{6,14},{7,15},{8,0},{9,1},... | collective-permute-start | bytes 1572872 | tf_op jit(solution)/shard_map/ppermute | solution.py:94
  598.5 18.2 %collective-permute-start.56 = (bf16[128,1024]{1,0:T(8,128)(2,1)S(1)}, bf16[128,1024]{1,0:T(8,128)(2,1)S(1)}, u32[]{:S(2)}, u32[]{:S(2)}) collective-permute-start(bf16[128,1024]{1,0:T(8,128)(2,1)S(1)} %get-tuple-element.327), channel_id=1, source_target_pairs={{0,2},{1,3},{2,0},{3,1},{4,6},{5,7},{6,4},{7,5},{8,10},{9,11},{10,... | collective-permute-start | bytes 786440 | tf_op jit(solution)/shard_map/ppermute | solution.py:94
  600.9 18.1 %collective-permute-start.57 = (bf16[128,1024]{1,0:T(8,128)(2,1)S(1)}, bf16[128,1024]{1,0:T(8,128)(2,1)S(1)}, u32[]{:S(2)}, u32[]{:S(2)}) collective-permute-start(bf16[128,1024]{1,0:T(8,128)(2,1)S(1)} %get-tuple-element.328), channel_id=1, source_target_pairs={{0,8},{1,9},{2,10},{3,11},{4,12},{5,13},{6,14},{7,15},{8,0},{9,1},... | collective-permute-start | bytes 786440 | tf_op jit(solution)/shard_map/ppermute | solution.py:94
  606.2 22.8 %collective-permute-start.80 = (bf16[288,512]{1,0:T(8,128)(2,1)}, bf16[288,512]{1,0:T(8,128)(2,1)}, u32[]{:S(2)}, u32[]{:S(2)}) collective-permute-start(bf16[288,512]{1,0:T(8,128)(2,1)} %slice.300), channel_id=1, source_target_pairs={{0,16},{4,20},{10,26},{14,30},{16,0},{20,4},{26,10},{30,14}} | collective-permute-start | bytes 884744 | tf_op jit(solution)/shard_map/ppermute | solution.py:94
  609.6 23.4 %collective-permute-start.79 = (bf16[288,512]{1,0:T(8,128)(2,1)}, bf16[288,512]{1,0:T(8,128)(2,1)}, u32[]{:S(2)}, u32[]{:S(2)}) collective-permute-start(bf16[288,512]{1,0:T(8,128)(2,1)} %slice.298), channel_id=1, source_target_pairs={{0,16},{1,17},{2,18},{3,19},{4,20},{5,21},{6,22},{7,23},{8,24},{9,... | collective-permute-start | bytes 884744 | tf_op jit(solution)/shard_map/ppermute | solution.py:94
  611.8 26.1 %collective-permute-start.70 = (bf16[304,768]{1,0:T(8,128)(2,1)S(1)}, bf16[304,768]{1,0:T(8,128)(2,1)S(1)}, u32[]{:S(2)}, u32[]{:S(2)}) collective-permute-start(bf16[304,768]{1,0:T(8,128)(2,1)S(1)} %add_convert_fusion.14), channel_id=1, source_target_pairs={{0,16},{4,20},{10,26},{14,30},{16,0},{20,4},{26,10},{30,14}} | collective-permute-start | bytes 1400840 | tf_op jit(solution)/shard_map/ppermute | solution.py:94
  616.8 26.3 %collective-permute-start.69 = (bf16[304,768]{1,0:T(8,128)(2,1)S(1)}, bf16[304,768]{1,0:T(8,128)(2,1)}, u32[]{:S(2)}, u32[]{:S(2)}) collective-permute-start(bf16[304,768]{1,0:T(8,128)(2,1)S(1)} %add_convert_fusion.15), channel_id=1, source_target_pairs={{0,16},{1,17},{2,18},{3,19},{4,20},{5,21},{6,22},{7,23},{8,24},{9,... | collective-permute-start | bytes 1400840 | tf_op jit(solution)/shard_map/ppermute | solution.py:94
  623.4 52.3 %collective-permute-start.67 = (bf16[576,1024]{1,0:T(8,128)(2,1)}, bf16[576,1024]{1,0:T(8,128)(2,1)}, u32[]{:S(2)}, u32[]{:S(2)}) collective-permute-start(bf16[576,1024]{1,0:T(8,128)(2,1)} %slice.285), channel_id=1, source_target_pairs={{0,4},{4,0},{10,14},{14,10},{16,20},{20,16},{26,30},{30,26}} | collective-permute-start | bytes 3538952 | tf_op jit(solution)/shard_map/ppermute | solution.py:94
  629.0 16.1 %collective-permute-start.59 = (f32[16,256]{1,0:T(8,128)S(1)}, f32[16,256]{1,0:T(8,128)S(1)}, u32[]{:S(2)}, u32[]{:S(2)}) collective-permute-start(f32[16,256]{1,0:T(8,128)S(1)} %add.176), channel_id=1, source_target_pairs={{0,2},{1,3},{2,0},{3,1},{4,6},{5,7},{6,4},{7,5},{8,10},{9,11},{10,... | collective-permute-start | bytes 49160 | tf_op jit(solution)/shard_map/ppermute | solution.py:94
  633.0 17.1 %collective-permute-start.60 = (f32[16,256]{1,0:T(8,128)S(1)}, f32[16,256]{1,0:T(8,128)S(1)}, u32[]{:S(2)}, u32[]{:S(2)}) collective-permute-start(f32[16,256]{1,0:T(8,128)S(1)} %add.176), channel_id=1, source_target_pairs={{0,8},{1,9},{2,10},{3,11},{4,12},{5,13},{6,14},{7,15},{8,0},{9,1},... | collective-permute-start | bytes 49160 | tf_op jit(solution)/shard_map/ppermute | solution.py:94
  646.2 32.2 %all-to-all-start.5 = ((bf16[8,64,640]{2,1,0:T(8,128)(2,1)}), bf16[8,64,640]{2,1,0:T(8,128)(2,1)S(1)}, u32[]{:S(2)}, u32[]{:S(2)}) async-start(bf16[8,64,640]{2,1,0:T(8,128)(2,1)} %shard_map.338), calls=%async_computation.6 | async-start | bytes 1310720 | tf_op jit(solution)/shard_map/all_to_all | solution.py:794
  650.1 31.9 %collective-permute-start.65 = (bf16[576,1024]{1,0:T(8,128)(2,1)}, bf16[576,1024]{1,0:T(8,128)(2,1)}, u32[]{:S(2)}, u32[]{:S(2)}) collective-permute-start(bf16[576,1024]{1,0:T(8,128)(2,1)} %slice.281), channel_id=1, source_target_pairs={{0,4},{1,5},{2,6},{3,7},{4,0},{5,1},{6,2},{7,3},{8,12},{9,13},{10,... | collective-permute-start | bytes 3538952 | tf_op jit(solution)/shard_map/ppermute | solution.py:94
  656.1 72.8 %collective-permute-start.62 = (f32[16,256]{1,0:T(8,128)S(1)}, f32[16,256]{1,0:T(8,128)S(1)}, u32[]{:S(2)}, u32[]{:S(2)}) collective-permute-start(f32[16,256]{1,0:T(8,128)S(1)} %add_add_fusion.1), channel_id=1, source_target_pairs={{0,16},{1,17},{2,18},{3,19},{4,20},{5,21},{6,22},{7,23},{8,24},{9,... | collective-permute-start | bytes 49160 | tf_op jit(solution)/shard_map/ppermute | solution.py:94
  658.5 70.4 %collective-permute-start.63 = (f32[16,256]{1,0:T(8,128)S(1)}, f32[16,256]{1,0:T(8,128)S(1)}, u32[]{:S(2)}, u32[]{:S(2)}) collective-permute-start(f32[16,256]{1,0:T(8,128)S(1)} %add_add_fusion.1), channel_id=1, source_target_pairs={{0,4},{1,5},{2,6},{3,7},{4,0},{5,1},{6,2},{7,3},{8,12},{9,13},{10,... | collective-permute-start | bytes 49160 | tf_op jit(solution)/shard_map/ppermute | solution.py:94
  672.0 18.7 %collective-permute-start.77 = (bf16[304,768]{1,0:T(8,128)(2,1)}, bf16[304,768]{1,0:T(8,128)(2,1)}, u32[]{:S(2)}, u32[]{:S(2)}) collective-permute-start(bf16[304,768]{1,0:T(8,128)(2,1)} %select_select_fusion), channel_id=1, source_target_pairs={{0,8},{1,9},{2,10},{3,11},{4,12},{5,13},{6,14},{7,15},{8,0},{9,1},... | collective-permute-start | bytes 1400840 | tf_op jit(solution)/shard_map/ppermute | solution.py:94
  678.4 43.9 %all-to-all-start.7 = ((bf16[8,64,768]{2,1,0:T(8,128)(2,1)}), bf16[8,64,768]{2,1,0:T(8,128)(2,1)S(1)}, u32[]{:S(2)}, u32[]{:S(2)}) async-start(bf16[8,64,768]{2,1,0:T(8,128)(2,1)} %bitcast.119), calls=%async_computation.10 | async-start | bytes 1572864 | tf_op jit(solution)/shard_map/all_to_all | solution.py:794
  682.0 31.9 %collective-permute-start.68 = (bf16[576,512]{1,0:T(8,128)(2,1)}, bf16[576,512]{1,0:T(8,128)(2,1)S(1)}, u32[]{:S(2)}, u32[]{:S(2)}) collective-permute-start(bf16[576,512]{1,0:T(8,128)(2,1)} %slice.326), channel_id=1, source_target_pairs={{0,16},{4,20},{10,26},{14,30},{16,0},{20,4},{26,10},{30,14}} | collective-permute-start | bytes 1769480 | tf_op jit(solution)/shard_map/ppermute | solution.py:94
  688.8 31.9 %collective-permute-start.66 = (bf16[576,512]{1,0:T(8,128)(2,1)S(1)}, bf16[576,512]{1,0:T(8,128)(2,1)S(1)}, u32[]{:S(2)}, u32[]{:S(2)}) collective-permute-start(bf16[576,512]{1,0:T(8,128)(2,1)S(1)} %slice.324), channel_id=1, source_target_pairs={{0,16},{1,17},{2,18},{3,19},{4,20},{5,21},{6,22},{7,23},{8,24},{9,... | collective-permute-start | bytes 1769480 | tf_op jit(solution)/shard_map/ppermute | solution.py:94
  690.7 38.3 %collective-permute-start.64 = (f32[16,256]{1,0:T(8,128)S(1)}, f32[16,256]{1,0:T(8,128)S(1)}, u32[]{:S(2)}, u32[]{:S(2)}) collective-permute-start(f32[16,256]{1,0:T(8,128)S(1)} %add_add_fusion.1), channel_id=1, source_target_pairs={{0,20},{1,21},{2,22},{3,23},{4,16},{5,17},{6,18},{7,19},{8,28},{9,... | collective-permute-start | bytes 49160 | tf_op jit(solution)/shard_map/ppermute | solution.py:94
  713.9 19.1 %collective-permute-start.75 = (bf16[1216,768]{1,0:T(8,128)(2,1)}, bf16[1216,768]{1,0:T(8,128)(2,1)}, u32[]{:S(2)}, u32[]{:S(2)}) collective-permute-start(bf16[1216,768]{1,0:T(8,128)(2,1)} %constant_dynamic-update-slice_fusion.21), channel_id=1, source_target_pairs={{0,1},{1,0},{2,3},{3,2},{4,5},{5,4},{6,7},{7,6},{8,9},{9,8},{10,11... | collective-permute-start | bytes 5603336 | tf_op jit(solution)/shard_map/ppermute | solution.py:94
  722.3 19.4 %all-to-all-start.4 = ((bf16[8,64,1152]{2,1,0:T(8,128)(2,1)}), bf16[8,64,1152]{2,1,0:T(8,128)(2,1)S(1)}, u32[]{:S(2)}, u32[]{:S(2)}) async-start(bf16[8,64,1152]{2,1,0:T(8,128)(2,1)} %shard_map.335), calls=%async_computation.5 | async-start | bytes 2359296 | tf_op jit(solution)/shard_map/all_to_all | solution.py:794
  (161 other events, 1218.7 us)
Sparse Core Ops, SparseCore 0:
  133.0 68.1 all-gather.3
  203.6 69.2 all-gather.7
  274.7 69.2 all-gather.5
  388.9 69.3 reduce-scatter.3
  461.7 69.0 reduce-scatter.5
  533.6 69.0 reduce-scatter.7

commit v4 on v3

--- a/solution.py
+++ b/solution.py
@@ -671,16 +671,17 @@
 
 def feed_parts_kernel(*refs):
     *weights, out = refs
-    rows, size = weights[0].shape[0], out.shape[2]
+    size = out.shape[2] // len(weights)
     for k, w in enumerate(weights):
         for s in range(SIDE):
-            out[s, k * rows : (k + 1) * rows, :] = w[:, s * size : (s + 1) * size]
-
-
-def feed_join_kernel(parts, out):
-    size = parts.shape[2]
-    for s in range(SIDE):
-        out[:, s * size : (s + 1) * size] = parts[s, :, :].astype(F32)
+            out[s, :, k * size : (k + 1) * size] = w[:, s * size : (s + 1) * size]
+
+
+def feed_join_kernel(parts, *outs):
+    size = parts.shape[2] // len(outs)
+    for k, out in enumerate(outs):
+        for s in range(SIDE):
+            out[:, s * size : (s + 1) * size] = parts[s, :, k * size : (k + 1) * size].astype(F32)
 
 
 def turn_kernel(parts, *outs):
@@ -824,8 +825,8 @@
     )[0]
     f_parts = kernel_call(
         feed_parts_kernel,
-        (after(feed_gate_weight, packet), feed_value_weight, feed_down_weight),
-        [((SIDE, 3 * rows_w, fs), BF16)],
+        (after(feed_value_weight, packet), feed_gate_weight, feed_down_weight),
+        [((SIDE, rows_w, 3 * fs), BF16)],
         smem=0,
     )[0]
     top = kernel_call(
@@ -869,11 +870,10 @@
     f_parts = after(f_parts, c_extra)
     c_extra = gather_later(c_extra, only)
     c_out = gather_start(p_out, 1)
-    f_parts = f_parts.reshape(SIDE, 3, rows_w, fs)
+    f_parts = f_parts.reshape(cols_w, 3 * fs)
     norm_mine = jnp.concatenate([packet[:tok], by_x[:tok], by_l[:tok], low, high[:half]])
     halo_mine = jnp.concatenate([packet[tok:], by_x[tok:], by_l[tok:], high[half:]])
     norm_theirs, halo_theirs = swap(norm_mine, CBIT), swap(halo_mine, CBIT)
-    f_parts = [f_parts[:, k].reshape(cols_w, fs) for k in range(3)]
     w_mix = kernel_call(
         functools.partial(assemble_kernel, places, (0, 1)),
         (*c_mix, *c_extra),
@@ -887,7 +887,8 @@
     def feed_full(part):
         return lax.all_gather(part, AXIS, axis_index_groups=far, tiled=True)
 
-    w_down, w_gate, w_value = (feed_full(f_parts[k]) for k in (2, 0, 1))
+    w_first, w_value = feed_full(f_parts[:, fs:]), feed_full(f_parts[:, :fs])
+    w_gate, w_down = w_first[:, :fs], w_first[:, fs:]
 
     def pick(p):
         one = lax.dynamic_index_in_dim(p, here, 0, False)
@@ -997,19 +998,20 @@
     gh_theirs = dot(after(top_theirs, normed_two), w_down)
     two_mine, two_theirs = gather_side(normed_two, marks=(gh_theirs, None))
 
-    def feed_half(two, grad_hidden):
-        inner_gate, inner_value = dot(two, w_gate), dot(two, w_value)
+    def feed_half(two, inner_gate, grad_hidden):
+        inner_value = dot(two, w_value)
         act, slope = gelu_pair(inner_gate)
         hidden = (act * inner_value).astype(BF16)
         grad_ig = (grad_hidden * inner_value * slope).astype(BF16)
         grad_iv = (grad_hidden * act).astype(BF16)
-        return hidden, grad_ig, grad_iv
-
-    hid_t, gig_t, giv_t = feed_half(two_theirs, gh_theirs)
-    back_t = (dot_last(gig_t, w_gate) + dot_last(giv_t, w_value)).astype(BF16)
+        return hidden, jnp.concatenate([grad_ig, grad_iv], axis=1)
+
+    ig_mine, ig_theirs = dot(two_mine, w_gate), dot(two_theirs, w_gate)
+    hid_t, gi_t = feed_half(after(two_theirs, ig_mine), ig_theirs, gh_theirs)
+    back_t = (dot_last(gi_t[:, :fs], w_gate) + dot_last(gi_t[:, fs:], w_value)).astype(BF16)
     two_mine = after(two_mine, back_t)
-    hid_m, gig_m, giv_m = feed_half(two_mine, gh_mine)
-    back_m = dot_last(gig_m, w_gate) + dot_last(giv_m, w_value)
+    hid_m, gi_m = feed_half(two_mine, ig_mine, gh_mine)
+    back_m = dot_last(gi_m[:, :fs], w_gate) + dot_last(gi_m[:, fs:], w_value)
 
     def feed_grad(a_m, b_m, a_t, b_t, mark):
         a_m, a_t = after((a_m, a_t), mark)
@@ -1034,19 +1036,18 @@
     parts, mark_one, mark_two = scatter_side(back_m, back_t)
     feed_mark = mark_two
     fg_down = feed_grad(top_mine, hid_m, top_theirs, hid_t, mark_one)
-    fg_gate = feed_grad(two_mine, gig_m, two_theirs, gig_t, (mark_two, fg_down))
-    parts = after(parts, fg_gate)
+    hid_t, hid_m = after((hid_t, hid_m), mark_two, fg_down)
+    out_t = dot_last(hid_t, w_down).astype(BF16)
+    out_m = dot_last(after(hid_m, out_t), w_down)
+    parts = after(parts, out_m)
     grad_middle, branch, gain_grad_two = kernel_call(
         functools.partial(middle_back_kernel, n),
         (me1, middle, output_grad, gain_two, *parts),
         [((tok, width), F32), ((tok, width), BF16), ((1, width), F32)],
         [held],
     )
-    fg_value = feed_grad(two_mine, giv_m, two_theirs, giv_t, branch)
-    hid_t, hid_m = after((hid_t, hid_m), fg_value)
-    out_t = dot_last(hid_t, w_down).astype(BF16)
-    out_m = dot_last(after(hid_m, out_t), w_down)
-    branch_mine, branch_theirs = gather_side(branch, marks=(fg_value, out_m))
+    fg_pair = feed_grad(two_mine, gi_m, two_theirs, gi_t, branch)
+    branch_mine, branch_theirs = gather_side(branch, marks=(fg_pair, None))
 
     gm_theirs = dot_last(branch_theirs, w_out)
     gm_mine = dot_last(branch_mine, w_out)
@@ -1067,12 +1068,13 @@
         return (dot_first(grad[:four], mine) + dot_first(grad[four:], theirs)).astype(BF16)
 
     def feed_send(shard):
-        return exchange(shard.reshape(SIDE, rows_w, fs))
+        return exchange(shard.reshape(SIDE, rows_w, shard.shape[1]))
 
     def feed_rows(v, mark):
+        kinds = v.shape[2] // fs
         return kernel_call(
-            feed_join_kernel, (after(v, mark),), [((rows_w, feed), F32)], smem=0, us=2
-        )[0]
+            feed_join_kernel, (after(v, mark),), [((rows_w, feed), F32)] * kinds, smem=0, us=2
+        )
 
     mixed_late = after(mixed, grad_gate)
     go = mixer_grad(mixed_late, branch_mine, branch_theirs)
@@ -1080,8 +1082,7 @@
         return lax.psum_scatter(g, AXIS, axis_index_groups=far, tiled=True)
 
     down_sum = feed_sum(after(fg_down, feed_mark))
-    gate_sum = feed_sum(after(fg_gate, branch))
-    value_sum = feed_sum(fg_value)
+    pair_sum = feed_sum(fg_pair)
     sent_down = feed_send(after(down_sum, scan_done))
     from_later = chain(totals, True, (go, sent_down))
     go = after(go, from_later)
@@ -1109,7 +1110,7 @@
                     if ((i ^ j) & ~side) != low_far:
                         pairs.append((j, i))
         head_parts.append(lax.ppermute(heads, AXIS, pairs))
-    low_late = after(low, heads)
+    low_late = after(low, heads, go0, go1)
     sq_r, sq_i = dot_first(low_late, g_reset), dot_first(low_late, g_input)
 
     rows = SLOT + HALO
@@ -1125,9 +1126,7 @@
     def total_far(v, m, sel=None):
         return (v.astype(F32) + swap(v, m, sel).astype(F32)).astype(BF16)
 
-    packed_one, packed_two = after((pack(0), pack(1)), heads_y)
-    packed_one = total_far(packed_one, masks[-1])
-    packed_two = total_far(packed_two, masks[-1], only)
+    packed_one, packed_two = pack(0), pack(1)
 
     out_parts, out_one, out_two = scatter_side(after(out_m, scan_done), out_t, heads)
     head_parts = after(tuple(head_parts), sq_i, out_two)
@@ -1142,15 +1141,17 @@
         ],
         us=8,
     )[0]
-    sent_gate = feed_send(after(gate_sum, grad_lin))
     grad_lin = after(grad_lin, out_parts)
     grad_pre = jnp.concatenate([grad_gate, grad_lin], axis=1)
     back_t = dot(grad_pre[four:], w_mix).astype(BF16)
     back_m = dot(after(grad_pre[:four], back_t), w_mix)
     parts, mark_one, mark_two = scatter_side(
-        back_m, back_t, (go0, go1, packed_one, packed_two)
+        back_m, back_t
     )
     go0, go1 = far_rest(after(go0, mark_two), 1), far_rest(after(go1, mark_two), 1, None, only)
+    packed_one, packed_two = after((packed_one, packed_two), mark_one)
+    packed_one = total_far(packed_one, masks[-1])
+    packed_two = total_far(packed_two, masks[-1], only)
     packed_one, packed_two = after((packed_one, packed_two), mark_two)
     for m in masks[:-1]:
         packed_one, packed_two = total_far(packed_one, m), total_far(packed_two, m, only)
@@ -1164,8 +1165,8 @@
     gp = mixer_grad(after(grad_pre, mark_one), norm_mine, norm_theirs)
     gp0 = jnp.concatenate([gp[:SLOT], gp[CW : CW + SLOT]])
     gp1 = jnp.concatenate([gp[SLOT : 2 * SLOT], gp[CW + SLOT : CW + 2 * SLOT]])
-    gp0, gp1 = after((gp0, gp1), mark_two)
-    gp0, gp1 = far_first(gp0, 1), far_first(gp1, 1, None, only)
+    gp0 = far_first(gp0, 1)
+    gp1 = far_first(after(gp1, mark_two), 1, None, only)
     input_grad, gain_grad_one = kernel_call(
         functools.partial(input_back_kernel, n),
         (me1, block_input, grad_middle, gain_one, *after(parts, block_output)),
@@ -1173,10 +1174,9 @@
         [held],
     )
     done = input_grad
-    sent_value = feed_send(after(value_sum, done))
-    grad_w_down = feed_rows(sent_down, done)
-    grad_w_gate = feed_rows(sent_gate, done)
-    grad_w_value = feed_rows(sent_value, done)
+    sent_pair = feed_send(after(pair_sum, done))
+    grad_w_down = feed_rows(sent_down, done)[0]
+    grad_w_gate, grad_w_value = feed_rows(sent_pair, done)
 
     def to_rows(parts, kinds):
         size = (2 * kinds * SLOT + 127) // 128 * 128
@@ -1189,7 +1189,7 @@
         )
 
     gp0, gp1 = far_rest(gp0, 1), far_rest(gp1, 1, None, only)
-    go0, go1 = after((go0, go1), done)
+    go0, go1, gp0, gp1 = after((go0, go1, gp0, gp1), done, sent_pair)
     grad_w_out = to_rows((go0, go1), 1)[0]
     grad_w_g, grad_w_l = to_rows((gp0, gp1), 2)
 

time: 758 us -> 742 us (0.979)
  local copies, waits for them, and re-layouts: 124 us -> 104 us
  waiting for transfers between devices: 212 us -> 230 us
  starting transfers between devices: 149 us -> 138 us
    ppermute x80, waiting for transfers between devices: 161 us -> 182 us  [swap(): return lax.ppermute(v, AXIS, pairs)]
    unnamed x283 -> x287, local copies, waits for them, and re-layouts: 92.4 us -> 73.4 us
    all_to_all x8 -> x7, waiting for transfers between devices: 22.5 us -> 6.87 us  [exchange(): return lax.all_to_all(v, AXIS, 0, 0, axis_index_groups=groups, tiled=True)]
    all_gather x3 -> x2, waiting for transfers between devices: 28.7 us -> 41.1 us  [feed_full(): return lax.all_gather(part, AXIS, axis_index_groups=far, tiled=True)]
    all_to_all x8 -> x7, starting transfers between devices: 34.7 us -> 30.2 us  [exchange(): return lax.all_to_all(v, AXIS, 0, 0, axis_index_groups=groups, tiled=True)]
    pallas_call x38 -> x37, Pallas kernels: 96.4 us -> 92.9 us  [kernel_call(): pl.pallas_call(kernel, in_specs=specs, out_specs=[pl.BlockSpec(memory_spa...]
    dot_general x12 -> x10, matrix products: 49.3 us -> 47.9 us  [dot_first(): lax.dot_general(a, b, (((0,), (0,)), ((), ())), preferred_element_type=F32)]
  transfers between devices with their start and end apart: 95 -> 92, of which waited for: 30 -> 32; matrix products, arithmetic and copies ran while one was open for 26% -> 26% of each run, Pallas kernels for 12% -> 12%
where the time goes in v4:
time: 742 us; the launch traced here: 732 us
  waiting for transfers between devices  230 us (31%)
  starting transfers between devices  138 us (19%)
  matrix products  132 us (18%)
  local copies, waits for them, and re-layouts  104 us (14%)
  Pallas kernels  92.9 us (13%)
  other arithmetic  18.2 us (2%)
  between operations  16.3 us (2%)
    ppermute x80, waiting for transfers between devices, swap(): return lax.ppermute(v, AXIS, pairs)  182 us
    ppermute x80, starting transfers between devices, swap(): return lax.ppermute(v, AXIS, pairs)  105 us
    pallas_call x37, Pallas kernels, kernel_call(): pl.pallas_call(kernel, in_specs=specs, out_specs=[pl.BlockSpec(memory_spa...  92.9 us
    unnamed x287, local copies, waits for them, and re-layouts  73.4 us
    dot_general x10, matrix products, dot_first(): lax.dot_general(a, b, (((0,), (0,)), ((), ())), preferred_element_type=F32)  47.9 us
    dot_general x11, matrix products, dot_last(): lax.dot_general(a, b, (((1,), (1,)), ((), ())), preferred_element_type=F32)  44.5 us
    all_gather x2, waiting for transfers between devices, feed_full(): return lax.all_gather(part, AXIS, axis_index_groups=far, tiled=True)  41.1 us
    dot_general x10, matrix products, dot(): lax.dot_general(a, b, (((1,), (0,)), ((), ())), preferred_element_type=F32)  39.8 us
  transfers between devices with their start and end apart: 92, of which 32 were waited for; matrix products, arithmetic and copies ran while one was open for 26% of the time, Pallas kernels for 12%

profile of v4, /device:TPU:0, one launch (start us, length us, event | category | flops | bytes accessed | tf_op | source)
XLA Modules:
  0.0 732.0 jit_solution(7299871688411673050)
XLA Ops:
  12.0 5.2 all-to-all-start
  24.8 6.0 all-to-all-done.parts
  30.8 5.1 all-to-all-start.1
  55.4 6.2 collective-permute-done.4
  61.6 12.4 %collective-permute-done.3 = bf16[144,2048]{1,0:T(8,128)(2,1)} collective-permute-done((bf16[144,2048]{1,0:T(8,128)(2,1)}, bf16[144,2048]{1,0:T(8,128)(2,1)}, u32[]{:S(2)}, u32[]{:S(2)}) %collective-permute-start.3) | collective-permute-done | bytes 589856 | tf_op jit(solution)/shard_map/ppermute | solution.py:94
  90.0 4.5 all-to-all-start.2
  96.4 3.9 collective-permute-done.6.refs_5_
  101.3 3.3 collective-permute-start.14
  115.0 4.9 collective-permute-done.9.refs_6_
  119.9 9.5 %collective-permute-done.10.refs_7_ = bf16[864,512]{1,0:T(8,128)(2,1)} collective-permute-done((bf16[864,512]{1,0:T(8,128)(2,1)S(1)}, bf16[864,512]{1,0:T(8,128)(2,1)}, u32[]{:S(2)}, u32[]{:S(2)}) %collective-permute-start.10) | collective-permute-done | bytes 884768 | tf_op jit(solution)/shard_map/ppermute | solution.py:94
  130.4 5.0 shard_map.310
  137.6 7.5 %fusion.56.lin_mine.gate_mine = f32[512,1280]{1,0:T(8,128)} fusion(bf16[512,2048]{1,0:T(8,128)(2,1)} %slice_dynamic-update-slice_fusion.3, bf16[1280,2048]{1,0:T(8,128)(2,1)} %shard_map.310), kind=kOutput, calls=%fused_computation.165 | convolution fusion | flops 2684354560 | bytes 9961472 | tf_op jit(solution)/shard_map/dot_general | solution.py:102
  150.9 6.2 fusion.57.lin_theirs.gate_theirs
  157.4 18.2 %shard_map.311 = (f32[5,1024,128]{2,1,0:T(8,128)S(1)}, bf16[1024,640]{1,0:T(8,128)(2,1)S(1)}, f32[5,1024,128]{2,1,0:T(8,128)S(1)}, f32[5,1024,128]{2,1,0:T(8,128...) custom-call(f32[512,1280]{1,0:T(8,128)S(1)} %copy-done.49, ...), custom_call_target="tpu_custom_call" | custom-call | flops 28999999488 | bytes 87000000 | tf_op jit(solution)/shard_map/pallas_call | solution.py:116
  189.9 9.7 %collective-permute-done.20 = bf16[64,2048]{1,0:T(8,128)(2,1)S(1)} collective-permute-done((bf16[64,2048]{1,0:T(8,128)(2,1)S(1)}, bf16[64,2048]{1,0:T(8,128)(2,1)S(1)}, u32[]{:S(2)}, u32[]{:S(2)}) %collective-permute-start.20) | collective-permute-done | bytes 262176 | tf_op jit(solution)/shard_map/ppermute | solution.py:94
  219.1 21.4 %collective-permute-done.22.recv_a = bf16[256,1024]{1,0:T(8,128)(2,1)S(1)} collective-permute-done((bf16[256,1024]{1,0:T(8,128)(2,1)}, bf16[256,1024]{1,0:T(8,128)(2,1)S(1)}, u32[]{:S(2)}, u32[]{:S(2)}) %collective-permute-start.22) | collective-permute-done | bytes 524320 | tf_op jit(solution)/shard_map/ppermute | solution.py:94
  248.3 21.3 %all-gather.3.cloned.1.call-done = bf16[2048,1536]{1,0:T(8,128)(2,1)} async-done(((bf16[512,1536]{1,0:T(8,128)(2,1)}), bf16[2048,1536]{1,0:T(8,128)(2,1)}) %all-gather.3.cloned.1.call-update) | async-done | bytes 6291472 | tf_op jit(solution)/shard_map/all_gather | solution.py:888
  269.6 5.6 fusion.15
  279.3 4.5 fusion.13
  283.8 7.5 %collective-permute-done.27 = bf16[128,2048]{1,0:T(8,128)(2,1)S(1)} collective-permute-done((bf16[128,2048]{1,0:T(8,128)(2,1)S(1)}, bf16[128,2048]{1,0:T(8,128)(2,1)S(1)}, u32[]{:S(2)}, u32[]{:S(2)}) %collective-permute-start.27) | collective-permute-done | bytes 524320 | tf_op jit(solution)/shard_map/ppermute | solution.py:94
  291.3 9.6 %collective-permute-done.26 = bf16[128,2048]{1,0:T(8,128)(2,1)S(1)} collective-permute-done((bf16[128,2048]{1,0:T(8,128)(2,1)S(1)}, bf16[128,2048]{1,0:T(8,128)(2,1)S(1)}, u32[]{:S(2)}, u32[]{:S(2)}) %collective-permute-start.26) | collective-permute-done | bytes 524320 | tf_op jit(solution)/shard_map/ppermute | solution.py:94
  302.1 6.4 collective-permute-done.29
  308.5 3.8 collective-permute-done.30
  320.7 19.8 %all-gather.5.cloned.1.call-done = bf16[2048,768]{1,0:T(8,128)(2,1)} async-done(((bf16[512,768]{1,0:T(8,128)(2,1)}), bf16[2048,768]{1,0:T(8,128)(2,1)}) %all-gather.5.cloned.1.call-update) | async-done | bytes 3145744 | tf_op jit(solution)/shard_map/all_gather | solution.py:888
  340.6 6.0 multiply_convert_fusion.1
  346.6 4.6 fusion.4
  365.2 3.5 fusion.59
  368.6 5.3 add_convert_fusion.2
  373.9 3.7 collective-permute-done.33.recv_a
  385.8 5.8 convolution_convert_fusion.1
  391.6 3.8 fusion.10.mine
  398.2 6.7 fusion.20
  404.9 8.7 %add_convert_fusion = bf16[2048,1536]{1,0:T(8,128)(2,1)} fusion(f32[2048,1536]{1,0:T(8,128)} %fusion.20, bf16[512,2048]{1,0:T(8,128)(2,1)S(1)} %copy-done.101, bf16[512,768]{1,0:T(8,128)(2,1)S(1)} %copy-done.117, bf16[512,768]{1,0:T(8,128)(2,1)S(1)} %copy-done.123), kind=kOutput, calls=%fused_computation | convolution fusion | flops 3230662656 | bytes 22544384 | tf_op jit(solution)/shard_map/dot_general | solution.py:106
  414.4 11.2 %collective-permute-done.37 = bf16[128,2048]{1,0:T(8,128)(2,1)S(1)} collective-permute-done((bf16[128,2048]{1,0:T(8,128)(2,1)S(1)}, bf16[128,2048]{1,0:T(8,128)(2,1)S(1)}, u32[]{:S(2)}, u32[]{:S(2)}) %collective-permute-start.37) | collective-permute-done | bytes 524320 | tf_op jit(solution)/shard_map/ppermute | solution.py:94
  432.7 6.9 collective-permute-done.40
  441.0 4.3 fusion.60.gm_mine
  445.4 3.9 fusion.61.gm_theirs
  449.3 8.9 %shard_map.324 = (f32[5,1024,128]{2,1,0:T(8,128)S(1)}, f32[5,1024,128]{2,1,0:T(8,128)S(1)}, f32[16,640]{1,0:T(8,128)S(1)}) custom-call(f32[512,640]{1,0:T(8,128)S(1)} %fusion.60.gm_mine, f32[512,640]{1,0:T(8,128)S(1)} %fusion.61.gm_theirs, f32[5,1024,128]{2,1,0:T(8,128)S(1)} %copy-done.62, f32[5,1024,128]{2,1,0:T(8,128)S(1)} %copy-done.66), custom_call_target="tpu_custom_call" | custom-call | flops 16000000000 | bytes 48000000 | tf_op jit(solution)/shard_map/pallas_call | solution.py:116
  462.9 4.6 all-to-all-start.3
  486.1 4.6 add_convert_fusion.3
  507.0 11.2 %shard_map.327 = (bf16[1024,640]{1,0:T(8,128)(2,1)S(1)}, bf16[1024,640]{1,0:T(8,128)(2,1)S(1)}, f32[5,1024,128]{2,1,0:T(8,128)S(1)}, f32[8,640]{1,0:T(8,128)S(1)}, f32[24,640]{1,0:T(8,128)S(1)}) custom-call(f32[5,1024,128]{2,1,0:T(8,128)S(1)} %copy-done.69, f32[5,1024,128]{2,1,0:T(8,128)S(1)} %copy-done.71, f32[8,8,640]{2,1,0:T(8,128)S(1)} %shard_map.326.from_later, ...), custom_call_target="tpu_custom_call" | custom-call | flops 20999999488 | bytes 63000000 | tf_op jit(solution)/shard_map/pallas_call | solution.py:116
  521.4 3.3 collective-permute-done.44
  527.7 4.9 shard_map.330
  532.7 3.6 collective-permute-done.50.rb
  536.3 6.3 convolution_convert_fusion
  544.7 4.9 fusion.63.mine
  554.8 7.1 fusion.30
  561.9 6.4 add_convert_fusion.1
  572.8 9.8 %collective-permute-done.52.recv_a = bf16[256,1024]{1,0:T(8,128)(2,1)S(1)} collective-permute-done((bf16[256,1024]{1,0:T(8,128)(2,1)S(1)}, bf16[256,1024]{1,0:T(8,128)(2,1)S(1)}, u32[]{:S(2)}, u32[]{:S(2)}) %collective-permute-start.52) | collective-permute-done | bytes 524320 | tf_op jit(solution)/shard_map/ppermute | solution.py:94
  588.0 4.2 collective-permute-start.64
  595.1 3.6 all-to-all-start.4
  608.9 3.5 collective-permute-done.63
  613.5 13.3 %collective-permute-done.71 = bf16[304,768]{1,0:T(8,128)(2,1)S(1)} collective-permute-done((bf16[304,768]{1,0:T(8,128)(2,1)}, bf16[304,768]{1,0:T(8,128)(2,1)S(1)}, u32[]{:S(2)}, u32[]{:S(2)}) %collective-permute-start.71) | collective-permute-done | bytes 466976 | tf_op jit(solution)/shard_map/ppermute | solution.py:94
  627.9 6.2 collective-permute-done.72
  634.3 5.5 collective-permute-start.73
  644.3 4.8 collective-permute-start.68
  649.9 5.7 collective-permute-done.74
  659.9 4.4 collective-permute-done.66
  664.2 7.1 collective-permute-start.75
  672.9 3.5 all-to-all-start.6
  693.3 3.6 all-to-all-start.5
  697.8 3.7 collective-permute-start.60
  703.8 7.3 collective-permute-done.62
  714.0 5.8 shard_map.337
  (580 shorter events, 276.0 us)
Async XLA Ops:
  12.0 18.8 %all-to-all-start = ((bf16[8,64,896]{2,1,0:T(8,128)(2,1)}), bf16[8,64,896]{2,1,0:T(8,128)(2,1)S(1)}, u32[]{:S(2)}, u32[]{:S(2)}) async-start(bf16[8,64,896]{2,1,0:T(8,128)(2,1)} %get-tuple-element.182), calls=%async_computation | async-start | bytes 1835008 | tf_op jit(solution)/shard_map/all_to_all | solution.py:795
  30.8 23.5 %all-to-all-start.1 = ((bf16[8,64,896]{2,1,0:T(8,128)(2,1)}), bf16[8,64,896]{2,1,0:T(8,128)(2,1)S(1)}, u32[]{:S(2)}, u32[]{:S(2)}) async-start(bf16[8,64,896]{2,1,0:T(8,128)(2,1)} %get-tuple-element.187), calls=%async_computation.1 | async-start | bytes 1835008 | tf_op jit(solution)/shard_map/all_to_all | solution.py:795
  43.5 18.2 %collective-permute-start.4 = (bf16[144,2048]{1,0:T(8,128)(2,1)}, bf16[144,2048]{1,0:T(8,128)(2,1)}, u32[]{:S(2)}, u32[]{:S(2)}) collective-permute-start(bf16[144,2048]{1,0:T(8,128)(2,1)} %shard_map.307), channel_id=1, source_target_pairs={{0,2},{1,3},{2,0},{3,1},{4,6},{5,7},{6,4},{7,5},{8,10},{9,11},{10,... | collective-permute-start | bytes 1769480 | tf_op jit(solution)/shard_map/ppermute | solution.py:94
  45.5 28.5 %collective-permute-start.3 = (bf16[144,2048]{1,0:T(8,128)(2,1)}, bf16[144,2048]{1,0:T(8,128)(2,1)}, u32[]{:S(2)}, u32[]{:S(2)}) collective-permute-start(bf16[144,2048]{1,0:T(8,128)(2,1)} %shard_map.307), channel_id=1, source_target_pairs={{0,8},{1,9},{2,10},{3,11},{4,12},{5,13},{6,14},{7,15},{8,0},{9,1},... | collective-permute-start | bytes 1769480 | tf_op jit(solution)/shard_map/ppermute | solution.py:94
  47.0 27.0 %collective-permute-start.2 = (bf16[576,512]{1,0:T(8,128)(2,1)}, bf16[576,512]{1,0:T(8,128)(2,1)S(1)}, u32[]{:S(2)}, u32[]{:S(2)}) collective-permute-start(bf16[576,512]{1,0:T(8,128)(2,1)} %get-tuple-element.197.refs_0_), channel_id=1, source_target_pairs={{0,4},{1,5},{2,6},{3,7},{4,0},{5,1},{6,2},{7,3},{8,12},{9,13},{10,... | collective-permute-start | bytes 1769480 | tf_op jit(solution)/shard_map/ppermute | solution.py:94
  48.2 28.5 %collective-permute-start.1 = (bf16[576,512]{1,0:T(8,128)(2,1)}, bf16[576,512]{1,0:T(8,128)(2,1)}, u32[]{:S(2)}, u32[]{:S(2)}) collective-permute-start(bf16[576,512]{1,0:T(8,128)(2,1)} %get-tuple-element.197.refs_0_), channel_id=1, source_target_pairs={{0,16},{1,17},{2,18},{3,19},{4,20},{5,21},{6,22},{7,23},{8,24},{9,... | collective-permute-start | bytes 1769480 | tf_op jit(solution)/shard_map/ppermute | solution.py:94
  78.4 18.0 %collective-permute-start.7 = (bf16[64,2048]{1,0:T(8,128)(2,1)}, bf16[64,2048]{1,0:T(8,128)(2,1)}, u32[]{:S(2)}, u32[]{:S(2)}) collective-permute-start(bf16[64,2048]{1,0:T(8,128)(2,1)} %slice.237), channel_id=1, source_target_pairs={{0,2},{1,3},{2,0},{3,1},{4,6},{5,7},{6,4},{7,5},{8,10},{9,11},{10,... | collective-permute-start | bytes 786440 | tf_op jit(solution)/shard_map/ppermute | solution.py:94
  80.1 16.3 %collective-permute-start.8 = (bf16[80,2048]{1,0:T(8,128)(2,1)}, bf16[80,2048]{1,0:T(8,128)(2,1)}, u32[]{:S(2)}, u32[]{:S(2)}) collective-permute-start(bf16[80,2048]{1,0:T(8,128)(2,1)} %slice.238), channel_id=1, source_target_pairs={{0,8},{1,9},{2,10},{3,11},{4,12},{5,13},{6,14},{7,15},{8,0},{9,1},... | collective-permute-start | bytes 983048 | tf_op jit(solution)/shard_map/ppermute | solution.py:94
  83.0 17.3 %collective-permute-start.6 = (bf16[864,512]{1,0:T(8,128)(2,1)}, bf16[864,512]{1,0:T(8,128)(2,1)S(1)}, u32[]{:S(2)}, u32[]{:S(2)}) collective-permute-start(bf16[864,512]{1,0:T(8,128)(2,1)} %shard_map.309.refs_4_), channel_id=1, source_target_pairs={{0,16},{4,20},{10,26},{14,30},{16,0},{20,4},{26,10},{30,14}} | collective-permute-start | bytes 2654216 | tf_op jit(solution)/shard_map/ppermute | solution.py:94
  90.0 55.1 %all-to-all-start.2 = ((bf16[8,64,2304]{2,1,0:T(8,128)(2,1)}), bf16[8,64,2304]{2,1,0:T(8,128)(2,1)}, u32[]{:S(2)}, u32[]{:S(2)}) async-start(bf16[8,64,2304]{2,1,0:T(8,128)(2,1)} %shard_map.312), calls=%async_computation.2 | async-start | bytes 4718592 | tf_op jit(solution)/shard_map/all_to_all | solution.py:795
  94.6 175.0 %all-gather.3.cloned.1.call-start = ((), (), s32[]{:S(2)}) async-start(), calls=%async_computation.9 | async-start | bytes 7864320 | tf_op jit(solution)/shard_map/all_gather | solution.py:888
  101.3 34.2 %collective-permute-start.14 = (bf16[288,512]{1,0:T(8,128)(2,1)S(1)}, bf16[288,512]{1,0:T(8,128)(2,1)}, u32[]{:S(2)}, u32[]{:S(2)}) collective-permute-start(bf16[288,512]{1,0:T(8,128)(2,1)S(1)} %copy-done.25), channel_id=1, source_target_pairs={{0,16},{1,17},{2,18},{3,19},{4,20},{5,21},{6,22},{7,23},{8,24},{9,... | collective-permute-start | bytes 884744 | tf_op jit(solution)/shard_map/ppermute | solution.py:94
  104.6 15.2 %collective-permute-start.9 = (bf16[864,512]{1,0:T(8,128)(2,1)}, bf16[864,512]{1,0:T(8,128)(2,1)}, u32[]{:S(2)}, u32[]{:S(2)}) collective-permute-start(bf16[864,512]{1,0:T(8,128)(2,1)} %shard_map.309.refs_4_), channel_id=1, source_target_pairs={{0,4},{4,0},{10,14},{14,10},{16,20},{20,16},{26,30},{30,26}} | collective-permute-start | bytes 2654216 | tf_op jit(solution)/shard_map/ppermute | solution.py:94
  107.8 21.6 %collective-permute-start.10 = (bf16[864,512]{1,0:T(8,128)(2,1)S(1)}, bf16[864,512]{1,0:T(8,128)(2,1)}, u32[]{:S(2)}, u32[]{:S(2)}) collective-permute-start(bf16[864,512]{1,0:T(8,128)(2,1)S(1)} %collective-permute-done.6.refs_5_), channel_id=1, source_target_pairs={{0,4},{4,0},{10,14},{14,10},{16,20},{20,16},{26,30},{30,26}} | collective-permute-start | bytes 2654216 | tf_op jit(solution)/shard_map/ppermute | solution.py:94
  113.8 37.1 %collective-permute-start.11 = (bf16[512,2048]{1,0:T(8,128)(2,1)}, bf16[512,2048]{1,0:T(8,128)(2,1)}, u32[]{:S(2)}, u32[]{:S(2)}) collective-permute-start(bf16[512,2048]{1,0:T(8,128)(2,1)} %slice_dynamic-update-slice_fusion.3), channel_id=1, source_target_pairs={{0,1},{1,0},{2,3},{3,2},{4,5},{5,4},{6,7},{7,6},{8,9},{9,8},{10,11... | collective-permute-start | bytes 6291464 | tf_op jit(solution)/shard_map/ppermute | solution.py:94
  135.4 43.2 %collective-permute-start.18 = (bf16[128,2048]{1,0:T(8,128)(2,1)S(1)}, bf16[128,2048]{1,0:T(8,128)(2,1)}, u32[]{:S(2)}, u32[]{:S(2)}) collective-permute-start(bf16[128,2048]{1,0:T(8,128)(2,1)S(1)} %copy-done.5), channel_id=1, source_target_pairs={{0,2},{1,3},{2,0},{3,1},{4,6},{5,7},{6,4},{7,5},{8,10},{9,11},{10,... | collective-permute-start | bytes 1572872 | tf_op jit(solution)/shard_map/ppermute | solution.py:94
  135.4 43.2 %collective-permute-start.17 = (bf16[128,2048]{1,0:T(8,128)(2,1)S(1)}, bf16[128,2048]{1,0:T(8,128)(2,1)}, u32[]{:S(2)}, u32[]{:S(2)}) collective-permute-start(bf16[128,2048]{1,0:T(8,128)(2,1)S(1)} %copy-done.5), channel_id=1, source_target_pairs={{0,8},{1,9},{2,10},{3,11},{4,12},{5,13},{6,14},{7,15},{8,0},{9,1},... | collective-permute-start | bytes 1572872 | tf_op jit(solution)/shard_map/ppermute | solution.py:94
  135.5 47.8 %collective-permute-start.15 = (bf16[288,512]{1,0:T(8,128)(2,1)S(1)}, bf16[288,512]{1,0:T(8,128)(2,1)}, u32[]{:S(2)}, u32[]{:S(2)}) collective-permute-start(bf16[288,512]{1,0:T(8,128)(2,1)S(1)} %copy-done.25), channel_id=1, source_target_pairs={{0,4},{1,5},{2,6},{3,7},{4,0},{5,1},{6,2},{7,3},{8,12},{9,13},{10,... | collective-permute-start | bytes 884744 | tf_op jit(solution)/shard_map/ppermute | solution.py:94
  136.8 46.5 %collective-permute-start.16 = (bf16[288,512]{1,0:T(8,128)(2,1)}, bf16[288,512]{1,0:T(8,128)(2,1)}, u32[]{:S(2)}, u32[]{:S(2)}) collective-permute-start(bf16[288,512]{1,0:T(8,128)(2,1)} %collective-permute-done.14.refs_1_), channel_id=1, source_target_pairs={{0,4},{1,5},{2,6},{3,7},{4,0},{5,1},{6,2},{7,3},{8,12},{9,13},{10,... | collective-permute-start | bytes 884744 | tf_op jit(solution)/shard_map/ppermute | solution.py:94
  147.8 192.8 %all-gather.5.cloned.1.call-start = ((), (), s32[]{:S(2)}) async-start(), calls=%async_computation.10 | async-start | bytes 3932160 | tf_op jit(solution)/shard_map/all_gather | solution.py:888
  215.0 64.3 %collective-permute-start.28 = (bf16[512,2048]{1,0:T(8,128)(2,1)}, bf16[512,2048]{1,0:T(8,128)(2,1)}, u32[]{:S(2)}, u32[]{:S(2)}) collective-permute-start(bf16[512,2048]{1,0:T(8,128)(2,1)} %constant_dynamic-update-slice_fusion.6), channel_id=1, source_target_pairs={{0,1},{1,0},{2,3},{3,2},{4,5},{5,4},{6,7},{7,6},{8,9},{9,8},{10,11... | collective-permute-start | bytes 6291464 | tf_op jit(solution)/shard_map/ppermute | solution.py:94
  215.4 25.1 %collective-permute-start.22 = (bf16[256,1024]{1,0:T(8,128)(2,1)}, bf16[256,1024]{1,0:T(8,128)(2,1)S(1)}, u32[]{:S(2)}, u32[]{:S(2)}) collective-permute-start(bf16[256,1024]{1,0:T(8,128)(2,1)} %get-tuple-element.232), channel_id=1, source_target_pairs={{0,8},{1,9},{2,10},{3,11},{4,12},{5,13},{6,14},{7,15},{8,0},{9,1},... | collective-permute-start | bytes 1572872 | tf_op jit(solution)/shard_map/ppermute | solution.py:94
  215.5 25.1 %collective-permute-start.23 = (bf16[256,1024]{1,0:T(8,128)(2,1)S(1)}, bf16[256,1024]{1,0:T(8,128)(2,1)}, u32[]{:S(2)}, u32[]{:S(2)}) collective-permute-start(bf16[256,1024]{1,0:T(8,128)(2,1)S(1)} %get-tuple-element.234), channel_id=1, source_target_pairs={{0,2},{1,3},{2,0},{3,1},{4,6},{5,7},{6,4},{7,5},{8,10},{9,11},{10,... | collective-permute-start | bytes 1572872 | tf_op jit(solution)/shard_map/ppermute | solution.py:94
  219.1 243.9 %reduce-scatter.3.cloned.1.call-start = ((), (), s32[]{:S(2)}) async-start(), calls=%async_computation.11 | async-start | bytes 3932160 | tf_op jit(solution)/shard_map/reduce_scatter | solution.py:1082
  245.9 29.3 %collective-permute-start.24 = (bf16[128,1024]{1,0:T(8,128)(2,1)}, bf16[128,1024]{1,0:T(8,128)(2,1)}, u32[]{:S(2)}, u32[]{:S(2)}) collective-permute-start(bf16[128,1024]{1,0:T(8,128)(2,1)} %get-tuple-element.236), channel_id=1, source_target_pairs={{0,2},{1,3},{2,0},{3,1},{4,6},{5,7},{6,4},{7,5},{8,10},{9,11},{10,... | collective-permute-start | bytes 786440 | tf_op jit(solution)/shard_map/ppermute | solution.py:94
  247.3 27.8 %collective-permute-start.25 = (bf16[128,1024]{1,0:T(8,128)(2,1)S(1)}, bf16[128,1024]{1,0:T(8,128)(2,1)}, u32[]{:S(2)}, u32[]{:S(2)}) collective-permute-start(bf16[128,1024]{1,0:T(8,128)(2,1)S(1)} %get-tuple-element.237), channel_id=1, source_target_pairs={{0,8},{1,9},{2,10},{3,11},{4,12},{5,13},{6,14},{7,15},{8,0},{9,1},... | collective-permute-start | bytes 786440 | tf_op jit(solution)/shard_map/ppermute | solution.py:94
  279.2 21.7 %collective-permute-start.26 = (bf16[128,2048]{1,0:T(8,128)(2,1)S(1)}, bf16[128,2048]{1,0:T(8,128)(2,1)S(1)}, u32[]{:S(2)}, u32[]{:S(2)}) collective-permute-start(bf16[128,2048]{1,0:T(8,128)(2,1)S(1)} %get-tuple-element.245), channel_id=1, source_target_pairs={{0,8},{1,9},{2,10},{3,11},{4,12},{5,13},{6,14},{7,15},{8,0},{9,1},... | collective-permute-start | bytes 1572872 | tf_op jit(solution)/shard_map/ppermute | solution.py:94
  382.4 212.7 %reduce-scatter.5.cloned.1.call-start = ((), (), s32[]{:S(2)}) async-start(), calls=%async_computation.12 | async-start | bytes 7864320 | tf_op jit(solution)/shard_map/reduce_scatter | solution.py:1082
  397.4 16.9 %collective-permute-start.38 = (bf16[128,2048]{1,0:T(8,128)(2,1)S(1)}, bf16[128,2048]{1,0:T(8,128)(2,1)}, u32[]{:S(2)}, u32[]{:S(2)}) collective-permute-start(bf16[128,2048]{1,0:T(8,128)(2,1)S(1)} %get-tuple-element.266), channel_id=1, source_target_pairs={{0,2},{1,3},{2,0},{3,1},{4,6},{5,7},{6,4},{7,5},{8,10},{9,11},{10,... | collective-permute-start | bytes 1572872 | tf_op jit(solution)/shard_map/ppermute | solution.py:94
  397.9 27.6 %collective-permute-start.37 = (bf16[128,2048]{1,0:T(8,128)(2,1)S(1)}, bf16[128,2048]{1,0:T(8,128)(2,1)S(1)}, u32[]{:S(2)}, u32[]{:S(2)}) collective-permute-start(bf16[128,2048]{1,0:T(8,128)(2,1)S(1)} %get-tuple-element.266), channel_id=1, source_target_pairs={{0,8},{1,9},{2,10},{3,11},{4,12},{5,13},{6,14},{7,15},{8,0},{9,1},... | collective-permute-start | bytes 1572872 | tf_op jit(solution)/shard_map/ppermute | solution.py:94
  440.4 31.9 %collective-permute-start.46 = (bf16[512,2048]{1,0:T(8,128)(2,1)}, bf16[512,2048]{1,0:T(8,128)(2,1)}, u32[]{:S(2)}, u32[]{:S(2)}) collective-permute-start(bf16[512,2048]{1,0:T(8,128)(2,1)} %convolution_convert_fusion.1), channel_id=1, source_target_pairs={{0,1},{1,0},{2,3},{3,2},{4,5},{5,4},{6,7},{7,6},{8,9},{9,8},{10,11... | collective-permute-start | bytes 6291464 | tf_op jit(solution)/shard_map/ppermute | solution.py:94
  461.3 29.4 %collective-permute-start.42 = (f32[16,640]{1,0:T(8,128)S(1)}, f32[16,640]{1,0:T(8,128)}, u32[]{:S(2)}, u32[]{:S(2)}) collective-permute-start(f32[16,640]{1,0:T(8,128)S(1)} %get-tuple-element.280.refs_0_), channel_id=1, source_target_pairs={{0,4},{1,5},{2,6},{3,7},{4,0},{5,1},{6,2},{7,3},{8,12},{9,13},{10,... | collective-permute-start | bytes 122888 | tf_op jit(solution)/shard_map/ppermute | solution.py:94
  462.9 27.8 %all-to-all-start.3 = ((bf16[8,64,768]{2,1,0:T(8,128)(2,1)}), bf16[8,64,768]{2,1,0:T(8,128)(2,1)}, u32[]{:S(2)}, u32[]{:S(2)}) async-start(bf16[8,64,768]{2,1,0:T(8,128)(2,1)} %bitcast.98), calls=%async_computation.4 | async-start | bytes 1572864 | tf_op jit(solution)/shard_map/all_to_all | solution.py:795
  479.0 39.7 %collective-permute-start.47 = (bf16[256,1024]{1,0:T(8,128)(2,1)}, bf16[256,1024]{1,0:T(8,128)(2,1)}, u32[]{:S(2)}, u32[]{:S(2)}) collective-permute-start(bf16[256,1024]{1,0:T(8,128)(2,1)} %get-tuple-element.296), channel_id=1, source_target_pairs={{0,8},{1,9},{2,10},{3,11},{4,12},{5,13},{6,14},{7,15},{8,0},{9,1},... | collective-permute-start | bytes 1572872 | tf_op jit(solution)/shard_map/ppermute | solution.py:94
  481.9 36.8 %collective-permute-start.48 = (bf16[256,1024]{1,0:T(8,128)(2,1)}, bf16[256,1024]{1,0:T(8,128)(2,1)}, u32[]{:S(2)}, u32[]{:S(2)}) collective-permute-start(bf16[256,1024]{1,0:T(8,128)(2,1)} %get-tuple-element.298), channel_id=1, source_target_pairs={{0,2},{1,3},{2,0},{3,1},{4,6},{5,7},{6,4},{7,5},{8,10},{9,11},{10,... | collective-permute-start | bytes 1572872 | tf_op jit(solution)/shard_map/ppermute | solution.py:94
  493.8 27.7 %collective-permute-start.45 = (bf16[288,1024]{1,0:T(8,128)(2,1)S(1)}, bf16[288,1024]{1,0:T(8,128)(2,1)S(1)}, u32[]{:S(2)}, u32[]{:S(2)}) collective-permute-start(bf16[288,1024]{1,0:T(8,128)(2,1)S(1)} %get-tuple-element.363), channel_id=1, source_target_pairs={{0,4},{4,0},{10,14},{14,10},{16,20},{20,16},{26,30},{30,26}} | collective-permute-start | bytes 1769480 | tf_op jit(solution)/shard_map/ppermute | solution.py:94
  496.1 28.6 %collective-permute-start.44 = (bf16[288,1024]{1,0:T(8,128)(2,1)S(1)}, bf16[288,1024]{1,0:T(8,128)(2,1)S(1)}, u32[]{:S(2)}, u32[]{:S(2)}) collective-permute-start(bf16[288,1024]{1,0:T(8,128)(2,1)S(1)} %get-tuple-element.364), channel_id=1, source_target_pairs={{0,4},{1,5},{2,6},{3,7},{4,0},{5,1},{6,2},{7,3},{8,12},{9,13},{10,... | collective-permute-start | bytes 1769480 | tf_op jit(solution)/shard_map/ppermute | solution.py:94
  520.3 16.0 %collective-permute-start.50 = (bf16[128,1024]{1,0:T(8,128)(2,1)S(1)}, bf16[128,1024]{1,0:T(8,128)(2,1)S(1)}, u32[]{:S(2)}, u32[]{:S(2)}) collective-permute-start(bf16[128,1024]{1,0:T(8,128)(2,1)S(1)} %get-tuple-element.303), channel_id=1, source_target_pairs={{0,8},{1,9},{2,10},{3,11},{4,12},{5,13},{6,14},{7,15},{8,0},{9,1},... | collective-permute-start | bytes 786440 | tf_op jit(solution)/shard_map/ppermute | solution.py:94
  550.0 35.6 %collective-permute-start.69 = (bf16[304,768]{1,0:T(8,128)(2,1)S(1)}, bf16[304,768]{1,0:T(8,128)(2,1)S(1)}, u32[]{:S(2)}, u32[]{:S(2)}) collective-permute-start(bf16[304,768]{1,0:T(8,128)(2,1)S(1)} %fusion.39), channel_id=1, source_target_pairs={{0,4},{1,5},{2,6},{3,7},{4,0},{5,1},{6,2},{7,3},{8,12},{9,13},{10,... | collective-permute-start | bytes 1400840 | tf_op jit(solution)/shard_map/ppermute | solution.py:94
  551.6 47.1 %collective-permute-start.70 = (bf16[304,768]{1,0:T(8,128)(2,1)S(1)}, bf16[304,768]{1,0:T(8,128)(2,1)}, u32[]{:S(2)}, u32[]{:S(2)}) collective-permute-start(bf16[304,768]{1,0:T(8,128)(2,1)S(1)} %fusion.40), channel_id=1, source_target_pairs={{0,4},{4,0},{10,14},{14,10},{16,20},{20,16},{26,30},{30,26}} | collective-permute-start | bytes 1400840 | tf_op jit(solution)/shard_map/ppermute | solution.py:94
  554.2 28.4 %collective-permute-start.52 = (bf16[256,1024]{1,0:T(8,128)(2,1)S(1)}, bf16[256,1024]{1,0:T(8,128)(2,1)S(1)}, u32[]{:S(2)}, u32[]{:S(2)}) collective-permute-start(bf16[256,1024]{1,0:T(8,128)(2,1)S(1)} %get-tuple-element.309), channel_id=1, source_target_pairs={{0,8},{1,9},{2,10},{3,11},{4,12},{5,13},{6,14},{7,15},{8,0},{9,1},... | collective-permute-start | bytes 1572872 | tf_op jit(solution)/shard_map/ppermute | solution.py:94
  554.3 28.4 %collective-permute-start.53 = (bf16[256,1024]{1,0:T(8,128)(2,1)S(1)}, bf16[256,1024]{1,0:T(8,128)(2,1)S(1)}, u32[]{:S(2)}, u32[]{:S(2)}) collective-permute-start(bf16[256,1024]{1,0:T(8,128)(2,1)S(1)} %get-tuple-element.311), channel_id=1, source_target_pairs={{0,2},{1,3},{2,0},{3,1},{4,6},{5,7},{6,4},{7,5},{8,10},{9,11},{10,... | collective-permute-start | bytes 1572872 | tf_op jit(solution)/shard_map/ppermute | solution.py:94
  570.0 71.7 %collective-permute-start.65 = (bf16[576,1024]{1,0:T(8,128)(2,1)}, bf16[576,1024]{1,0:T(8,128)(2,1)}, u32[]{:S(2)}, u32[]{:S(2)}) collective-permute-start(bf16[576,1024]{1,0:T(8,128)(2,1)} %pad_maximum_fusion.2), channel_id=1, source_target_pairs={{0,4},{1,5},{2,6},{3,7},{4,0},{5,1},{6,2},{7,3},{8,12},{9,13},{10,... | collective-permute-start | bytes 3538952 | tf_op jit(solution)/shard_map/ppermute | solution.py:94
  588.0 18.2 %collective-permute-start.64 = (bf16[288,512]{1,0:T(8,128)(2,1)}, bf16[288,512]{1,0:T(8,128)(2,1)S(1)}, u32[]{:S(2)}, u32[]{:S(2)}) collective-permute-start(bf16[288,512]{1,0:T(8,128)(2,1)} %slice.275), channel_id=1, source_target_pairs={{0,16},{4,20},{10,26},{14,30},{16,0},{20,4},{26,10},{30,14}} | collective-permute-start | bytes 884744 | tf_op jit(solution)/shard_map/ppermute | solution.py:94
  592.2 20.2 %collective-permute-start.63 = (bf16[288,512]{1,0:T(8,128)(2,1)}, bf16[288,512]{1,0:T(8,128)(2,1)}, u32[]{:S(2)}, u32[]{:S(2)}) collective-permute-start(bf16[288,512]{1,0:T(8,128)(2,1)} %slice.273), channel_id=1, source_target_pairs={{0,16},{1,17},{2,18},{3,19},{4,20},{5,21},{6,22},{7,23},{8,24},{9,... | collective-permute-start | bytes 884744 | tf_op jit(solution)/shard_map/ppermute | solution.py:94
  595.1 76.8 %all-to-all-start.4 = ((bf16[8,64,1536]{2,1,0:T(8,128)(2,1)}), bf16[8,64,1536]{2,1,0:T(8,128)(2,1)S(1)}, u32[]{:S(2)}, u32[]{:S(2)}) async-start(bf16[8,64,1536]{2,1,0:T(8,128)(2,1)} %bitcast.97), calls=%async_computation.6 | async-start | bytes 3145728 | tf_op jit(solution)/shard_map/all_to_all | solution.py:795
  599.9 26.9 %collective-permute-start.71 = (bf16[304,768]{1,0:T(8,128)(2,1)}, bf16[304,768]{1,0:T(8,128)(2,1)S(1)}, u32[]{:S(2)}, u32[]{:S(2)}) collective-permute-start(bf16[304,768]{1,0:T(8,128)(2,1)} %add_convert_fusion.14), channel_id=1, source_target_pairs={{0,16},{1,17},{2,18},{3,19},{4,20},{5,21},{6,22},{7,23},{8,24},{9,... | collective-permute-start | bytes 1400840 | tf_op jit(solution)/shard_map/ppermute | solution.py:94
  603.7 30.5 %collective-permute-start.72 = (bf16[304,768]{1,0:T(8,128)(2,1)S(1)}, bf16[304,768]{1,0:T(8,128)(2,1)S(1)}, u32[]{:S(2)}, u32[]{:S(2)}) collective-permute-start(bf16[304,768]{1,0:T(8,128)(2,1)S(1)} %add_convert_fusion.13), channel_id=1, source_target_pairs={{0,16},{4,20},{10,26},{14,30},{16,0},{20,4},{26,10},{30,14}} | collective-permute-start | bytes 1400840 | tf_op jit(solution)/shard_map/ppermute | solution.py:94
  606.2 37.5 %collective-permute-start.67 = (bf16[576,1024]{1,0:T(8,128)(2,1)S(1)}, bf16[576,1024]{1,0:T(8,128)(2,1)S(1)}, u32[]{:S(2)}, u32[]{:S(2)}) collective-permute-start(bf16[576,1024]{1,0:T(8,128)(2,1)S(1)} %slice.287), channel_id=1, source_target_pairs={{0,4},{4,0},{10,14},{14,10},{16,20},{20,16},{26,30},{30,26}} | collective-permute-start | bytes 3538952 | tf_op jit(solution)/shard_map/ppermute | solution.py:94
  634.3 21.3 %collective-permute-start.74 = (bf16[304,768]{1,0:T(8,128)(2,1)S(1)}, bf16[304,768]{1,0:T(8,128)(2,1)S(1)}, u32[]{:S(2)}, u32[]{:S(2)}) collective-permute-start(bf16[304,768]{1,0:T(8,128)(2,1)S(1)} %add_convert_fusion.12), channel_id=1, source_target_pairs={{0,8},{1,9},{2,10},{3,11},{4,12},{5,13},{6,14},{7,15},{8,0},{9,1},... | collective-permute-start | bytes 1400840 | tf_op jit(solution)/shard_map/ppermute | solution.py:94
  634.3 22.8 %collective-permute-start.73 = (bf16[304,768]{1,0:T(8,128)(2,1)S(1)}, bf16[304,768]{1,0:T(8,128)(2,1)S(1)}, u32[]{:S(2)}, u32[]{:S(2)}) collective-permute-start(bf16[304,768]{1,0:T(8,128)(2,1)S(1)} %add_convert_fusion.12), channel_id=1, source_target_pairs={{0,2},{1,3},{2,0},{3,1},{4,6},{5,7},{6,4},{7,5},{8,10},{9,11},{10,... | collective-permute-start | bytes 1400840 | tf_op jit(solution)/shard_map/ppermute | solution.py:94
  639.8 16.5 %collective-permute-start.78 = (bf16[304,768]{1,0:T(8,128)(2,1)S(1)}, bf16[304,768]{1,0:T(8,128)(2,1)S(1)}, u32[]{:S(2)}, u32[]{:S(2)}) collective-permute-start(bf16[304,768]{1,0:T(8,128)(2,1)S(1)} %add_convert_fusion.11), channel_id=1, source_target_pairs={{0,2},{4,6},{10,8},{14,12},{16,18},{20,22},{26,24},{30,28}} | collective-permute-start | bytes 1400840 | tf_op jit(solution)/shard_map/ppermute | solution.py:94
  643.6 20.6 %collective-permute-start.66 = (bf16[576,512]{1,0:T(8,128)(2,1)S(1)}, bf16[576,512]{1,0:T(8,128)(2,1)S(1)}, u32[]{:S(2)}, u32[]{:S(2)}) collective-permute-start(bf16[576,512]{1,0:T(8,128)(2,1)S(1)} %slice.324), channel_id=1, source_target_pairs={{0,16},{1,17},{2,18},{3,19},{4,20},{5,21},{6,22},{7,23},{8,24},{9,... | collective-permute-start | bytes 1769480 | tf_op jit(solution)/shard_map/ppermute | solution.py:94
  644.3 27.3 %collective-permute-start.68 = (bf16[576,512]{1,0:T(8,128)(2,1)S(1)}, bf16[576,512]{1,0:T(8,128)(2,1)S(1)}, u32[]{:S(2)}, u32[]{:S(2)}) collective-permute-start(bf16[576,512]{1,0:T(8,128)(2,1)S(1)} %slice.328), channel_id=1, source_target_pairs={{0,16},{4,20},{10,26},{14,30},{16,0},{20,4},{26,10},{30,14}} | collective-permute-start | bytes 1769480 | tf_op jit(solution)/shard_map/ppermute | solution.py:94
  655.5 41.3 %collective-permute-start.59 = (f32[16,256]{1,0:T(8,128)S(1)}, f32[16,256]{1,0:T(8,128)S(1)}, u32[]{:S(2)}, u32[]{:S(2)}) collective-permute-start(f32[16,256]{1,0:T(8,128)S(1)} %add.168), channel_id=1, source_target_pairs={{0,10},{1,11},{2,8},{3,9},{4,14},{5,15},{6,12},{7,13},{8,2},{9,3},... | collective-permute-start | bytes 49160 | tf_op jit(solution)/shard_map/ppermute | solution.py:94
  656.3 40.6 %collective-permute-start.58 = (f32[16,256]{1,0:T(8,128)S(1)}, f32[16,256]{1,0:T(8,128)S(1)}, u32[]{:S(2)}, u32[]{:S(2)}) collective-permute-start(f32[16,256]{1,0:T(8,128)S(1)} %add.168), channel_id=1, source_target_pairs={{0,8},{1,9},{2,10},{3,11},{4,12},{5,13},{6,14},{7,15},{8,0},{9,1},... | collective-permute-start | bytes 49160 | tf_op jit(solution)/shard_map/ppermute | solution.py:94
  657.1 31.0 %collective-permute-start.79 = (bf16[304,768]{1,0:T(8,128)(2,1)}, bf16[304,768]{1,0:T(8,128)(2,1)}, u32[]{:S(2)}, u32[]{:S(2)}) collective-permute-start(bf16[304,768]{1,0:T(8,128)(2,1)} %select_select_fusion), channel_id=1, source_target_pairs={{0,8},{1,9},{2,10},{3,11},{4,12},{5,13},{6,14},{7,15},{8,0},{9,1},... | collective-permute-start | bytes 1400840 | tf_op jit(solution)/shard_map/ppermute | solution.py:94
  664.2 15.9 %collective-permute-start.75 = (bf16[144,768]{1,0:T(8,128)(2,1)}, bf16[144,768]{1,0:T(8,128)(2,1)}, u32[]{:S(2)}, u32[]{:S(2)}) collective-permute-start(bf16[144,768]{1,0:T(8,128)(2,1)} %slice.335), channel_id=1, source_target_pairs={{0,2},{1,3},{2,0},{3,1},{4,6},{5,7},{6,4},{7,5},{8,10},{9,11},{10,... | collective-permute-start | bytes 663560 | tf_op jit(solution)/shard_map/ppermute | solution.py:94
  671.5 14.9 %collective-permute-start.76 = (bf16[160,768]{1,0:T(8,128)(2,1)}, bf16[160,768]{1,0:T(8,128)(2,1)}, u32[]{:S(2)}, u32[]{:S(2)}) collective-permute-start(bf16[160,768]{1,0:T(8,128)(2,1)} %slice.336), channel_id=1, source_target_pairs={{0,8},{1,9},{2,10},{3,11},{4,12},{5,13},{6,14},{7,15},{8,0},{9,1},... | collective-permute-start | bytes 737288 | tf_op jit(solution)/shard_map/ppermute | solution.py:94
  672.9 20.4 %all-to-all-start.6 = ((bf16[8,64,640]{2,1,0:T(8,128)(2,1)}), bf16[8,64,640]{2,1,0:T(8,128)(2,1)S(1)}, u32[]{:S(2)}, u32[]{:S(2)}) async-start(bf16[8,64,640]{2,1,0:T(8,128)(2,1)} %shard_map.338), calls=%async_computation.8 | async-start | bytes 1310720 | tf_op jit(solution)/shard_map/all_to_all | solution.py:795
  680.1 16.8 %collective-permute-start.57 = (f32[16,256]{1,0:T(8,128)S(1)}, f32[16,256]{1,0:T(8,128)S(1)}, u32[]{:S(2)}, u32[]{:S(2)}) collective-permute-start(f32[16,256]{1,0:T(8,128)S(1)} %add.168), channel_id=1, source_target_pairs={{0,2},{1,3},{2,0},{3,1},{4,6},{5,7},{6,4},{7,5},{8,10},{9,11},{10,... | collective-permute-start | bytes 49160 | tf_op jit(solution)/shard_map/ppermute | solution.py:94
  688.1 24.6 %collective-permute-start.77 = (bf16[1216,768]{1,0:T(8,128)(2,1)}, bf16[1216,768]{1,0:T(8,128)(2,1)}, u32[]{:S(2)}, u32[]{:S(2)}) collective-permute-start(bf16[1216,768]{1,0:T(8,128)(2,1)} %constant_dynamic-update-slice_fusion.21), channel_id=1, source_target_pairs={{0,1},{1,0},{2,3},{3,2},{4,5},{5,4},{6,7},{7,6},{8,9},{9,8},{10,11... | collective-permute-start | bytes 5603336 | tf_op jit(solution)/shard_map/ppermute | solution.py:94
  690.5 22.0 %collective-permute-start.80 = (bf16[2,304,768]{2,1,0:T(8,128)(2,1)}, bf16[2,304,768]{2,1,0:T(8,128)(2,1)}, u32[]{:S(2)}, u32[]{:S(2)}) collective-permute-start(bf16[2,304,768]{2,1,0:T(8,128)(2,1)} %pad_maximum_fusion.3), channel_id=1, source_target_pairs={{0,1},{1,0},{2,3},{3,2},{4,5},{5,4},{6,7},{7,6},{8,9},{9,8},{10,11... | collective-permute-start | bytes 2801672 | tf_op jit(solution)/shard_map/ppermute | solution.py:94
  693.3 30.7 %all-to-all-start.5 = ((bf16[8,64,1152]{2,1,0:T(8,128)(2,1)}), bf16[8,64,1152]{2,1,0:T(8,128)(2,1)S(1)}, u32[]{:S(2)}, u32[]{:S(2)}) async-start(bf16[8,64,1152]{2,1,0:T(8,128)(2,1)} %shard_map.335), calls=%async_computation.7 | async-start | bytes 2359296 | tf_op jit(solution)/shard_map/all_to_all | solution.py:795
  (160 other events, 1288.5 us)
Sparse Core Ops, SparseCore 0:
  147.9 121.5 all-gather.2
  271.4 69.1 all-gather.4
  382.5 69.3 reduce-scatter.2
  454.7 120.5 reduce-scatter.4

commit v5 on v4

--- a/solution.py
+++ b/solution.py
@@ -1174,7 +1174,7 @@
         [held],
     )
     done = input_grad
-    sent_pair = feed_send(after(pair_sum, done))
+    sent_pair = feed_send(after(pair_sum, mark_two))
     grad_w_down = feed_rows(sent_down, done)[0]
     grad_w_gate, grad_w_value = feed_rows(sent_pair, done)
 

time: 742 us -> 742 us (level)
  no operation moved by 1% of the time
where the time goes in v5:
time: 742 us; the launch traced here: 732 us
  waiting for transfers between devices  230 us (31%)
  starting transfers between devices  138 us (19%)
  matrix products  132 us (18%)
  local copies, waits for them, and re-layouts  104 us (14%)
  Pallas kernels  92.9 us (13%)
  other arithmetic  18.2 us (2%)
  between operations  16.3 us (2%)
    ppermute x80, waiting for transfers between devices, swap(): return lax.ppermute(v, AXIS, pairs)  182 us
    ppermute x80, starting transfers between devices, swap(): return lax.ppermute(v, AXIS, pairs)  105 us
    pallas_call x37, Pallas kernels, kernel_call(): pl.pallas_call(kernel, in_specs=specs, out_specs=[pl.BlockSpec(memory_spa...  92.9 us
    unnamed x287, local copies, waits for them, and re-layouts  73.4 us
    dot_general x10, matrix products, dot_first(): lax.dot_general(a, b, (((0,), (0,)), ((), ())), preferred_element_type=F32)  47.9 us
    dot_general x11, matrix products, dot_last(): lax.dot_general(a, b, (((1,), (1,)), ((), ())), preferred_element_type=F32)  44.5 us
    all_gather x2, waiting for transfers between devices, feed_full(): return lax.all_gather(part, AXIS, axis_index_groups=far, tiled=True)  41.1 us
    dot_general x10, matrix products, dot(): lax.dot_general(a, b, (((1,), (0,)), ((), ())), preferred_element_type=F32)  39.8 us
  transfers between devices with their start and end apart: 92, of which 32 were waited for; matrix products, arithmetic and copies ran while one was open for 26% of the time, Pallas kernels for 12%

profile of v5, /device:TPU:0, one launch (start us, length us, event | category | flops | bytes accessed | tf_op | source)
XLA Modules:
  0.0 732.0 jit_solution(9026745647950908697)
XLA Ops:
  12.0 5.2 all-to-all-start
  24.8 6.0 all-to-all-done.parts
  30.8 5.1 all-to-all-start.1
  55.4 6.2 collective-permute-done.4
  61.6 12.4 %collective-permute-done.3 = bf16[144,2048]{1,0:T(8,128)(2,1)} collective-permute-done((bf16[144,2048]{1,0:T(8,128)(2,1)}, bf16[144,2048]{1,0:T(8,128)(2,1)}, u32[]{:S(2)}, u32[]{:S(2)}) %collective-permute-start.3) | collective-permute-done | bytes 589856 | tf_op jit(solution)/shard_map/ppermute | solution.py:94
  90.0 4.5 all-to-all-start.2
  96.4 3.9 collective-permute-done.6.refs_5_
  101.3 3.3 collective-permute-start.14
  115.0 4.9 collective-permute-done.9.refs_6_
  119.9 9.5 %collective-permute-done.10.refs_7_ = bf16[864,512]{1,0:T(8,128)(2,1)} collective-permute-done((bf16[864,512]{1,0:T(8,128)(2,1)S(1)}, bf16[864,512]{1,0:T(8,128)(2,1)}, u32[]{:S(2)}, u32[]{:S(2)}) %collective-permute-start.10) | collective-permute-done | bytes 884768 | tf_op jit(solution)/shard_map/ppermute | solution.py:94
  130.4 5.0 shard_map.310
  137.6 7.5 %fusion.56.lin_mine.gate_mine = f32[512,1280]{1,0:T(8,128)} fusion(bf16[512,2048]{1,0:T(8,128)(2,1)} %slice_dynamic-update-slice_fusion.3, bf16[1280,2048]{1,0:T(8,128)(2,1)} %shard_map.310), kind=kOutput, calls=%fused_computation.165 | convolution fusion | flops 2684354560 | bytes 9961472 | tf_op jit(solution)/shard_map/dot_general | solution.py:102
  150.9 6.2 fusion.57.lin_theirs.gate_theirs
  157.4 18.2 %shard_map.311 = (f32[5,1024,128]{2,1,0:T(8,128)S(1)}, bf16[1024,640]{1,0:T(8,128)(2,1)S(1)}, f32[5,1024,128]{2,1,0:T(8,128)S(1)}, f32[5,1024,128]{2,1,0:T(8,128...) custom-call(f32[512,1280]{1,0:T(8,128)S(1)} %copy-done.49, ...), custom_call_target="tpu_custom_call" | custom-call | flops 28999999488 | bytes 87000000 | tf_op jit(solution)/shard_map/pallas_call | solution.py:116
  189.9 9.7 %collective-permute-done.20 = bf16[64,2048]{1,0:T(8,128)(2,1)S(1)} collective-permute-done((bf16[64,2048]{1,0:T(8,128)(2,1)S(1)}, bf16[64,2048]{1,0:T(8,128)(2,1)S(1)}, u32[]{:S(2)}, u32[]{:S(2)}) %collective-permute-start.20) | collective-permute-done | bytes 262176 | tf_op jit(solution)/shard_map/ppermute | solution.py:94
  219.1 21.4 %collective-permute-done.22.recv_a = bf16[256,1024]{1,0:T(8,128)(2,1)S(1)} collective-permute-done((bf16[256,1024]{1,0:T(8,128)(2,1)}, bf16[256,1024]{1,0:T(8,128)(2,1)S(1)}, u32[]{:S(2)}, u32[]{:S(2)}) %collective-permute-start.22) | collective-permute-done | bytes 524320 | tf_op jit(solution)/shard_map/ppermute | solution.py:94
  248.3 21.3 %all-gather.3.cloned.1.call-done = bf16[2048,1536]{1,0:T(8,128)(2,1)} async-done(((bf16[512,1536]{1,0:T(8,128)(2,1)}), bf16[2048,1536]{1,0:T(8,128)(2,1)}) %all-gather.3.cloned.1.call-update) | async-done | bytes 6291472 | tf_op jit(solution)/shard_map/all_gather | solution.py:888
  269.6 5.6 fusion.15
  279.3 4.5 fusion.13
  283.8 7.5 %collective-permute-done.27 = bf16[128,2048]{1,0:T(8,128)(2,1)S(1)} collective-permute-done((bf16[128,2048]{1,0:T(8,128)(2,1)S(1)}, bf16[128,2048]{1,0:T(8,128)(2,1)S(1)}, u32[]{:S(2)}, u32[]{:S(2)}) %collective-permute-start.27) | collective-permute-done | bytes 524320 | tf_op jit(solution)/shard_map/ppermute | solution.py:94
  291.3 9.6 %collective-permute-done.26 = bf16[128,2048]{1,0:T(8,128)(2,1)S(1)} collective-permute-done((bf16[128,2048]{1,0:T(8,128)(2,1)S(1)}, bf16[128,2048]{1,0:T(8,128)(2,1)S(1)}, u32[]{:S(2)}, u32[]{:S(2)}) %collective-permute-start.26) | collective-permute-done | bytes 524320 | tf_op jit(solution)/shard_map/ppermute | solution.py:94
  302.1 6.4 collective-permute-done.29
  308.5 3.8 collective-permute-done.30
  320.7 19.8 %all-gather.5.cloned.1.call-done = bf16[2048,768]{1,0:T(8,128)(2,1)} async-done(((bf16[512,768]{1,0:T(8,128)(2,1)}), bf16[2048,768]{1,0:T(8,128)(2,1)}) %all-gather.5.cloned.1.call-update) | async-done | bytes 3145744 | tf_op jit(solution)/shard_map/all_gather | solution.py:888
  340.6 6.0 multiply_convert_fusion.1
  346.6 4.6 fusion.4
  365.2 3.5 fusion.59
  368.6 5.3 add_convert_fusion.2
  373.9 3.7 collective-permute-done.33.recv_a
  385.8 5.8 convolution_convert_fusion.1
  391.6 3.8 fusion.10.mine
  398.2 6.7 fusion.20
  404.9 8.7 %add_convert_fusion = bf16[2048,1536]{1,0:T(8,128)(2,1)} fusion(f32[2048,1536]{1,0:T(8,128)} %fusion.20, bf16[512,2048]{1,0:T(8,128)(2,1)S(1)} %copy-done.101, bf16[512,768]{1,0:T(8,128)(2,1)S(1)} %copy-done.117, bf16[512,768]{1,0:T(8,128)(2,1)S(1)} %copy-done.123), kind=kOutput, calls=%fused_computation | convolution fusion | flops 3230662656 | bytes 22544384 | tf_op jit(solution)/shard_map/dot_general | solution.py:106
  414.4 11.2 %collective-permute-done.37 = bf16[128,2048]{1,0:T(8,128)(2,1)S(1)} collective-permute-done((bf16[128,2048]{1,0:T(8,128)(2,1)S(1)}, bf16[128,2048]{1,0:T(8,128)(2,1)S(1)}, u32[]{:S(2)}, u32[]{:S(2)}) %collective-permute-start.37) | collective-permute-done | bytes 524320 | tf_op jit(solution)/shard_map/ppermute | solution.py:94
  432.7 6.9 collective-permute-done.40
  441.0 4.3 fusion.60.gm_mine
  445.4 3.9 fusion.61.gm_theirs
  449.3 8.9 %shard_map.324 = (f32[5,1024,128]{2,1,0:T(8,128)S(1)}, f32[5,1024,128]{2,1,0:T(8,128)S(1)}, f32[16,640]{1,0:T(8,128)S(1)}) custom-call(f32[512,640]{1,0:T(8,128)S(1)} %fusion.60.gm_mine, f32[512,640]{1,0:T(8,128)S(1)} %fusion.61.gm_theirs, f32[5,1024,128]{2,1,0:T(8,128)S(1)} %copy-done.62, f32[5,1024,128]{2,1,0:T(8,128)S(1)} %copy-done.66), custom_call_target="tpu_custom_call" | custom-call | flops 16000000000 | bytes 48000000 | tf_op jit(solution)/shard_map/pallas_call | solution.py:116
  462.9 4.6 all-to-all-start.3
  486.1 4.6 add_convert_fusion.3
  507.0 11.2 %shard_map.327 = (bf16[1024,640]{1,0:T(8,128)(2,1)S(1)}, bf16[1024,640]{1,0:T(8,128)(2,1)S(1)}, f32[5,1024,128]{2,1,0:T(8,128)S(1)}, f32[8,640]{1,0:T(8,128)S(1)}, f32[24,640]{1,0:T(8,128)S(1)}) custom-call(f32[5,1024,128]{2,1,0:T(8,128)S(1)} %copy-done.69, f32[5,1024,128]{2,1,0:T(8,128)S(1)} %copy-done.71, f32[8,8,640]{2,1,0:T(8,128)S(1)} %shard_map.326.from_later, ...), custom_call_target="tpu_custom_call" | custom-call | flops 20999999488 | bytes 63000000 | tf_op jit(solution)/shard_map/pallas_call | solution.py:116
  521.4 3.3 collective-permute-done.44
  527.7 4.9 shard_map.330
  532.7 3.6 collective-permute-done.50.rb
  536.3 6.3 convolution_convert_fusion
  544.7 4.9 fusion.63.mine
  554.8 7.1 fusion.30
  561.9 6.4 add_convert_fusion.1
  572.8 9.8 %collective-permute-done.52.recv_a = bf16[256,1024]{1,0:T(8,128)(2,1)S(1)} collective-permute-done((bf16[256,1024]{1,0:T(8,128)(2,1)S(1)}, bf16[256,1024]{1,0:T(8,128)(2,1)S(1)}, u32[]{:S(2)}, u32[]{:S(2)}) %collective-permute-start.52) | collective-permute-done | bytes 524320 | tf_op jit(solution)/shard_map/ppermute | solution.py:94
  588.0 4.2 collective-permute-start.64
  595.1 3.6 all-to-all-start.4
  608.9 3.5 collective-permute-done.63
  613.5 13.3 %collective-permute-done.71 = bf16[304,768]{1,0:T(8,128)(2,1)S(1)} collective-permute-done((bf16[304,768]{1,0:T(8,128)(2,1)}, bf16[304,768]{1,0:T(8,128)(2,1)S(1)}, u32[]{:S(2)}, u32[]{:S(2)}) %collective-permute-start.71) | collective-permute-done | bytes 466976 | tf_op jit(solution)/shard_map/ppermute | solution.py:94
  627.9 6.2 collective-permute-done.72
  634.3 5.5 collective-permute-start.73
  644.3 4.8 collective-permute-start.68
  649.9 5.7 collective-permute-done.74
  659.9 4.4 collective-permute-done.66
  664.2 7.1 collective-permute-start.75
  672.9 3.5 all-to-all-start.6
  693.3 3.6 all-to-all-start.5
  697.8 3.7 collective-permute-start.60
  703.8 7.3 collective-permute-done.62
  714.0 5.8 shard_map.337
  (580 shorter events, 276.0 us)
Async XLA Ops:
  12.0 18.8 %all-to-all-start = ((bf16[8,64,896]{2,1,0:T(8,128)(2,1)}), bf16[8,64,896]{2,1,0:T(8,128)(2,1)S(1)}, u32[]{:S(2)}, u32[]{:S(2)}) async-start(bf16[8,64,896]{2,1,0:T(8,128)(2,1)} %get-tuple-element.182), calls=%async_computation | async-start | bytes 1835008 | tf_op jit(solution)/shard_map/all_to_all | solution.py:795
  30.8 23.5 %all-to-all-start.1 = ((bf16[8,64,896]{2,1,0:T(8,128)(2,1)}), bf16[8,64,896]{2,1,0:T(8,128)(2,1)S(1)}, u32[]{:S(2)}, u32[]{:S(2)}) async-start(bf16[8,64,896]{2,1,0:T(8,128)(2,1)} %get-tuple-element.187), calls=%async_computation.1 | async-start | bytes 1835008 | tf_op jit(solution)/shard_map/all_to_all | solution.py:795
  43.5 18.2 %collective-permute-start.4 = (bf16[144,2048]{1,0:T(8,128)(2,1)}, bf16[144,2048]{1,0:T(8,128)(2,1)}, u32[]{:S(2)}, u32[]{:S(2)}) collective-permute-start(bf16[144,2048]{1,0:T(8,128)(2,1)} %shard_map.307), channel_id=1, source_target_pairs={{0,2},{1,3},{2,0},{3,1},{4,6},{5,7},{6,4},{7,5},{8,10},{9,11},{10,... | collective-permute-start | bytes 1769480 | tf_op jit(solution)/shard_map/ppermute | solution.py:94
  45.5 28.5 %collective-permute-start.3 = (bf16[144,2048]{1,0:T(8,128)(2,1)}, bf16[144,2048]{1,0:T(8,128)(2,1)}, u32[]{:S(2)}, u32[]{:S(2)}) collective-permute-start(bf16[144,2048]{1,0:T(8,128)(2,1)} %shard_map.307), channel_id=1, source_target_pairs={{0,8},{1,9},{2,10},{3,11},{4,12},{5,13},{6,14},{7,15},{8,0},{9,1},... | collective-permute-start | bytes 1769480 | tf_op jit(solution)/shard_map/ppermute | solution.py:94
  47.0 27.0 %collective-permute-start.2 = (bf16[576,512]{1,0:T(8,128)(2,1)}, bf16[576,512]{1,0:T(8,128)(2,1)S(1)}, u32[]{:S(2)}, u32[]{:S(2)}) collective-permute-start(bf16[576,512]{1,0:T(8,128)(2,1)} %get-tuple-element.197.refs_0_), channel_id=1, source_target_pairs={{0,4},{1,5},{2,6},{3,7},{4,0},{5,1},{6,2},{7,3},{8,12},{9,13},{10,... | collective-permute-start | bytes 1769480 | tf_op jit(solution)/shard_map/ppermute | solution.py:94
  48.2 28.5 %collective-permute-start.1 = (bf16[576,512]{1,0:T(8,128)(2,1)}, bf16[576,512]{1,0:T(8,128)(2,1)}, u32[]{:S(2)}, u32[]{:S(2)}) collective-permute-start(bf16[576,512]{1,0:T(8,128)(2,1)} %get-tuple-element.197.refs_0_), channel_id=1, source_target_pairs={{0,16},{1,17},{2,18},{3,19},{4,20},{5,21},{6,22},{7,23},{8,24},{9,... | collective-permute-start | bytes 1769480 | tf_op jit(solution)/shard_map/ppermute | solution.py:94
  78.4 18.0 %collective-permute-start.7 = (bf16[64,2048]{1,0:T(8,128)(2,1)}, bf16[64,2048]{1,0:T(8,128)(2,1)}, u32[]{:S(2)}, u32[]{:S(2)}) collective-permute-start(bf16[64,2048]{1,0:T(8,128)(2,1)} %slice.237), channel_id=1, source_target_pairs={{0,2},{1,3},{2,0},{3,1},{4,6},{5,7},{6,4},{7,5},{8,10},{9,11},{10,... | collective-permute-start | bytes 786440 | tf_op jit(solution)/shard_map/ppermute | solution.py:94
  80.1 16.3 %collective-permute-start.8 = (bf16[80,2048]{1,0:T(8,128)(2,1)}, bf16[80,2048]{1,0:T(8,128)(2,1)}, u32[]{:S(2)}, u32[]{:S(2)}) collective-permute-start(bf16[80,2048]{1,0:T(8,128)(2,1)} %slice.238), channel_id=1, source_target_pairs={{0,8},{1,9},{2,10},{3,11},{4,12},{5,13},{6,14},{7,15},{8,0},{9,1},... | collective-permute-start | bytes 983048 | tf_op jit(solution)/shard_map/ppermute | solution.py:94
  83.0 17.3 %collective-permute-start.6 = (bf16[864,512]{1,0:T(8,128)(2,1)}, bf16[864,512]{1,0:T(8,128)(2,1)S(1)}, u32[]{:S(2)}, u32[]{:S(2)}) collective-permute-start(bf16[864,512]{1,0:T(8,128)(2,1)} %shard_map.309.refs_4_), channel_id=1, source_target_pairs={{0,16},{4,20},{10,26},{14,30},{16,0},{20,4},{26,10},{30,14}} | collective-permute-start | bytes 2654216 | tf_op jit(solution)/shard_map/ppermute | solution.py:94
  90.0 55.1 %all-to-all-start.2 = ((bf16[8,64,2304]{2,1,0:T(8,128)(2,1)}), bf16[8,64,2304]{2,1,0:T(8,128)(2,1)}, u32[]{:S(2)}, u32[]{:S(2)}) async-start(bf16[8,64,2304]{2,1,0:T(8,128)(2,1)} %shard_map.312), calls=%async_computation.2 | async-start | bytes 4718592 | tf_op jit(solution)/shard_map/all_to_all | solution.py:795
  94.6 175.0 %all-gather.3.cloned.1.call-start = ((), (), s32[]{:S(2)}) async-start(), calls=%async_computation.9 | async-start | bytes 7864320 | tf_op jit(solution)/shard_map/all_gather | solution.py:888
  101.3 34.2 %collective-permute-start.14 = (bf16[288,512]{1,0:T(8,128)(2,1)S(1)}, bf16[288,512]{1,0:T(8,128)(2,1)}, u32[]{:S(2)}, u32[]{:S(2)}) collective-permute-start(bf16[288,512]{1,0:T(8,128)(2,1)S(1)} %copy-done.25), channel_id=1, source_target_pairs={{0,16},{1,17},{2,18},{3,19},{4,20},{5,21},{6,22},{7,23},{8,24},{9,... | collective-permute-start | bytes 884744 | tf_op jit(solution)/shard_map/ppermute | solution.py:94
  104.6 15.2 %collective-permute-start.9 = (bf16[864,512]{1,0:T(8,128)(2,1)}, bf16[864,512]{1,0:T(8,128)(2,1)}, u32[]{:S(2)}, u32[]{:S(2)}) collective-permute-start(bf16[864,512]{1,0:T(8,128)(2,1)} %shard_map.309.refs_4_), channel_id=1, source_target_pairs={{0,4},{4,0},{10,14},{14,10},{16,20},{20,16},{26,30},{30,26}} | collective-permute-start | bytes 2654216 | tf_op jit(solution)/shard_map/ppermute | solution.py:94
  107.8 21.6 %collective-permute-start.10 = (bf16[864,512]{1,0:T(8,128)(2,1)S(1)}, bf16[864,512]{1,0:T(8,128)(2,1)}, u32[]{:S(2)}, u32[]{:S(2)}) collective-permute-start(bf16[864,512]{1,0:T(8,128)(2,1)S(1)} %collective-permute-done.6.refs_5_), channel_id=1, source_target_pairs={{0,4},{4,0},{10,14},{14,10},{16,20},{20,16},{26,30},{30,26}} | collective-permute-start | bytes 2654216 | tf_op jit(solution)/shard_map/ppermute | solution.py:94
  113.8 37.1 %collective-permute-start.11 = (bf16[512,2048]{1,0:T(8,128)(2,1)}, bf16[512,2048]{1,0:T(8,128)(2,1)}, u32[]{:S(2)}, u32[]{:S(2)}) collective-permute-start(bf16[512,2048]{1,0:T(8,128)(2,1)} %slice_dynamic-update-slice_fusion.3), channel_id=1, source_target_pairs={{0,1},{1,0},{2,3},{3,2},{4,5},{5,4},{6,7},{7,6},{8,9},{9,8},{10,11... | collective-permute-start | bytes 6291464 | tf_op jit(solution)/shard_map/ppermute | solution.py:94
  135.4 43.2 %collective-permute-start.18 = (bf16[128,2048]{1,0:T(8,128)(2,1)S(1)}, bf16[128,2048]{1,0:T(8,128)(2,1)}, u32[]{:S(2)}, u32[]{:S(2)}) collective-permute-start(bf16[128,2048]{1,0:T(8,128)(2,1)S(1)} %copy-done.5), channel_id=1, source_target_pairs={{0,2},{1,3},{2,0},{3,1},{4,6},{5,7},{6,4},{7,5},{8,10},{9,11},{10,... | collective-permute-start | bytes 1572872 | tf_op jit(solution)/shard_map/ppermute | solution.py:94
  135.4 43.2 %collective-permute-start.17 = (bf16[128,2048]{1,0:T(8,128)(2,1)S(1)}, bf16[128,2048]{1,0:T(8,128)(2,1)}, u32[]{:S(2)}, u32[]{:S(2)}) collective-permute-start(bf16[128,2048]{1,0:T(8,128)(2,1)S(1)} %copy-done.5), channel_id=1, source_target_pairs={{0,8},{1,9},{2,10},{3,11},{4,12},{5,13},{6,14},{7,15},{8,0},{9,1},... | collective-permute-start | bytes 1572872 | tf_op jit(solution)/shard_map/ppermute | solution.py:94
  135.5 47.8 %collective-permute-start.15 = (bf16[288,512]{1,0:T(8,128)(2,1)S(1)}, bf16[288,512]{1,0:T(8,128)(2,1)}, u32[]{:S(2)}, u32[]{:S(2)}) collective-permute-start(bf16[288,512]{1,0:T(8,128)(2,1)S(1)} %copy-done.25), channel_id=1, source_target_pairs={{0,4},{1,5},{2,6},{3,7},{4,0},{5,1},{6,2},{7,3},{8,12},{9,13},{10,... | collective-permute-start | bytes 884744 | tf_op jit(solution)/shard_map/ppermute | solution.py:94
  136.8 46.5 %collective-permute-start.16 = (bf16[288,512]{1,0:T(8,128)(2,1)}, bf16[288,512]{1,0:T(8,128)(2,1)}, u32[]{:S(2)}, u32[]{:S(2)}) collective-permute-start(bf16[288,512]{1,0:T(8,128)(2,1)} %collective-permute-done.14.refs_1_), channel_id=1, source_target_pairs={{0,4},{1,5},{2,6},{3,7},{4,0},{5,1},{6,2},{7,3},{8,12},{9,13},{10,... | collective-permute-start | bytes 884744 | tf_op jit(solution)/shard_map/ppermute | solution.py:94
  147.8 192.8 %all-gather.5.cloned.1.call-start = ((), (), s32[]{:S(2)}) async-start(), calls=%async_computation.10 | async-start | bytes 3932160 | tf_op jit(solution)/shard_map/all_gather | solution.py:888
  215.0 64.3 %collective-permute-start.28 = (bf16[512,2048]{1,0:T(8,128)(2,1)}, bf16[512,2048]{1,0:T(8,128)(2,1)}, u32[]{:S(2)}, u32[]{:S(2)}) collective-permute-start(bf16[512,2048]{1,0:T(8,128)(2,1)} %constant_dynamic-update-slice_fusion.6), channel_id=1, source_target_pairs={{0,1},{1,0},{2,3},{3,2},{4,5},{5,4},{6,7},{7,6},{8,9},{9,8},{10,11... | collective-permute-start | bytes 6291464 | tf_op jit(solution)/shard_map/ppermute | solution.py:94
  215.4 25.1 %collective-permute-start.22 = (bf16[256,1024]{1,0:T(8,128)(2,1)}, bf16[256,1024]{1,0:T(8,128)(2,1)S(1)}, u32[]{:S(2)}, u32[]{:S(2)}) collective-permute-start(bf16[256,1024]{1,0:T(8,128)(2,1)} %get-tuple-element.232), channel_id=1, source_target_pairs={{0,8},{1,9},{2,10},{3,11},{4,12},{5,13},{6,14},{7,15},{8,0},{9,1},... | collective-permute-start | bytes 1572872 | tf_op jit(solution)/shard_map/ppermute | solution.py:94
  215.5 25.1 %collective-permute-start.23 = (bf16[256,1024]{1,0:T(8,128)(2,1)S(1)}, bf16[256,1024]{1,0:T(8,128)(2,1)}, u32[]{:S(2)}, u32[]{:S(2)}) collective-permute-start(bf16[256,1024]{1,0:T(8,128)(2,1)S(1)} %get-tuple-element.234), channel_id=1, source_target_pairs={{0,2},{1,3},{2,0},{3,1},{4,6},{5,7},{6,4},{7,5},{8,10},{9,11},{10,... | collective-permute-start | bytes 1572872 | tf_op jit(solution)/shard_map/ppermute | solution.py:94
  219.1 243.9 %reduce-scatter.3.cloned.1.call-start = ((), (), s32[]{:S(2)}) async-start(), calls=%async_computation.11 | async-start | bytes 3932160 | tf_op jit(solution)/shard_map/reduce_scatter | solution.py:1082
  245.9 29.3 %collective-permute-start.24 = (bf16[128,1024]{1,0:T(8,128)(2,1)}, bf16[128,1024]{1,0:T(8,128)(2,1)}, u32[]{:S(2)}, u32[]{:S(2)}) collective-permute-start(bf16[128,1024]{1,0:T(8,128)(2,1)} %get-tuple-element.236), channel_id=1, source_target_pairs={{0,2},{1,3},{2,0},{3,1},{4,6},{5,7},{6,4},{7,5},{8,10},{9,11},{10,... | collective-permute-start | bytes 786440 | tf_op jit(solution)/shard_map/ppermute | solution.py:94
  247.3 27.8 %collective-permute-start.25 = (bf16[128,1024]{1,0:T(8,128)(2,1)S(1)}, bf16[128,1024]{1,0:T(8,128)(2,1)}, u32[]{:S(2)}, u32[]{:S(2)}) collective-permute-start(bf16[128,1024]{1,0:T(8,128)(2,1)S(1)} %get-tuple-element.237), channel_id=1, source_target_pairs={{0,8},{1,9},{2,10},{3,11},{4,12},{5,13},{6,14},{7,15},{8,0},{9,1},... | collective-permute-start | bytes 786440 | tf_op jit(solution)/shard_map/ppermute | solution.py:94
  279.2 21.7 %collective-permute-start.26 = (bf16[128,2048]{1,0:T(8,128)(2,1)S(1)}, bf16[128,2048]{1,0:T(8,128)(2,1)S(1)}, u32[]{:S(2)}, u32[]{:S(2)}) collective-permute-start(bf16[128,2048]{1,0:T(8,128)(2,1)S(1)} %get-tuple-element.245), channel_id=1, source_target_pairs={{0,8},{1,9},{2,10},{3,11},{4,12},{5,13},{6,14},{7,15},{8,0},{9,1},... | collective-permute-start | bytes 1572872 | tf_op jit(solution)/shard_map/ppermute | solution.py:94
  382.4 212.7 %reduce-scatter.5.cloned.1.call-start = ((), (), s32[]{:S(2)}) async-start(), calls=%async_computation.12 | async-start | bytes 7864320 | tf_op jit(solution)/shard_map/reduce_scatter | solution.py:1082
  397.4 16.9 %collective-permute-start.38 = (bf16[128,2048]{1,0:T(8,128)(2,1)S(1)}, bf16[128,2048]{1,0:T(8,128)(2,1)}, u32[]{:S(2)}, u32[]{:S(2)}) collective-permute-start(bf16[128,2048]{1,0:T(8,128)(2,1)S(1)} %get-tuple-element.266), channel_id=1, source_target_pairs={{0,2},{1,3},{2,0},{3,1},{4,6},{5,7},{6,4},{7,5},{8,10},{9,11},{10,... | collective-permute-start | bytes 1572872 | tf_op jit(solution)/shard_map/ppermute | solution.py:94
  397.9 27.6 %collective-permute-start.37 = (bf16[128,2048]{1,0:T(8,128)(2,1)S(1)}, bf16[128,2048]{1,0:T(8,128)(2,1)S(1)}, u32[]{:S(2)}, u32[]{:S(2)}) collective-permute-start(bf16[128,2048]{1,0:T(8,128)(2,1)S(1)} %get-tuple-element.266), channel_id=1, source_target_pairs={{0,8},{1,9},{2,10},{3,11},{4,12},{5,13},{6,14},{7,15},{8,0},{9,1},... | collective-permute-start | bytes 1572872 | tf_op jit(solution)/shard_map/ppermute | solution.py:94
  440.4 31.9 %collective-permute-start.46 = (bf16[512,2048]{1,0:T(8,128)(2,1)}, bf16[512,2048]{1,0:T(8,128)(2,1)}, u32[]{:S(2)}, u32[]{:S(2)}) collective-permute-start(bf16[512,2048]{1,0:T(8,128)(2,1)} %convolution_convert_fusion.1), channel_id=1, source_target_pairs={{0,1},{1,0},{2,3},{3,2},{4,5},{5,4},{6,7},{7,6},{8,9},{9,8},{10,11... | collective-permute-start | bytes 6291464 | tf_op jit(solution)/shard_map/ppermute | solution.py:94
  461.3 29.4 %collective-permute-start.42 = (f32[16,640]{1,0:T(8,128)S(1)}, f32[16,640]{1,0:T(8,128)}, u32[]{:S(2)}, u32[]{:S(2)}) collective-permute-start(f32[16,640]{1,0:T(8,128)S(1)} %get-tuple-element.280.refs_0_), channel_id=1, source_target_pairs={{0,4},{1,5},{2,6},{3,7},{4,0},{5,1},{6,2},{7,3},{8,12},{9,13},{10,... | collective-permute-start | bytes 122888 | tf_op jit(solution)/shard_map/ppermute | solution.py:94
  462.9 27.8 %all-to-all-start.3 = ((bf16[8,64,768]{2,1,0:T(8,128)(2,1)}), bf16[8,64,768]{2,1,0:T(8,128)(2,1)}, u32[]{:S(2)}, u32[]{:S(2)}) async-start(bf16[8,64,768]{2,1,0:T(8,128)(2,1)} %bitcast.98), calls=%async_computation.4 | async-start | bytes 1572864 | tf_op jit(solution)/shard_map/all_to_all | solution.py:795
  479.0 39.7 %collective-permute-start.47 = (bf16[256,1024]{1,0:T(8,128)(2,1)}, bf16[256,1024]{1,0:T(8,128)(2,1)}, u32[]{:S(2)}, u32[]{:S(2)}) collective-permute-start(bf16[256,1024]{1,0:T(8,128)(2,1)} %get-tuple-element.296), channel_id=1, source_target_pairs={{0,8},{1,9},{2,10},{3,11},{4,12},{5,13},{6,14},{7,15},{8,0},{9,1},... | collective-permute-start | bytes 1572872 | tf_op jit(solution)/shard_map/ppermute | solution.py:94
  481.9 36.8 %collective-permute-start.48 = (bf16[256,1024]{1,0:T(8,128)(2,1)}, bf16[256,1024]{1,0:T(8,128)(2,1)}, u32[]{:S(2)}, u32[]{:S(2)}) collective-permute-start(bf16[256,1024]{1,0:T(8,128)(2,1)} %get-tuple-element.298), channel_id=1, source_target_pairs={{0,2},{1,3},{2,0},{3,1},{4,6},{5,7},{6,4},{7,5},{8,10},{9,11},{10,... | collective-permute-start | bytes 1572872 | tf_op jit(solution)/shard_map/ppermute | solution.py:94
  493.8 27.7 %collective-permute-start.45 = (bf16[288,1024]{1,0:T(8,128)(2,1)S(1)}, bf16[288,1024]{1,0:T(8,128)(2,1)S(1)}, u32[]{:S(2)}, u32[]{:S(2)}) collective-permute-start(bf16[288,1024]{1,0:T(8,128)(2,1)S(1)} %get-tuple-element.363), channel_id=1, source_target_pairs={{0,4},{4,0},{10,14},{14,10},{16,20},{20,16},{26,30},{30,26}} | collective-permute-start | bytes 1769480 | tf_op jit(solution)/shard_map/ppermute | solution.py:94
  496.1 28.6 %collective-permute-start.44 = (bf16[288,1024]{1,0:T(8,128)(2,1)S(1)}, bf16[288,1024]{1,0:T(8,128)(2,1)S(1)}, u32[]{:S(2)}, u32[]{:S(2)}) collective-permute-start(bf16[288,1024]{1,0:T(8,128)(2,1)S(1)} %get-tuple-element.364), channel_id=1, source_target_pairs={{0,4},{1,5},{2,6},{3,7},{4,0},{5,1},{6,2},{7,3},{8,12},{9,13},{10,... | collective-permute-start | bytes 1769480 | tf_op jit(solution)/shard_map/ppermute | solution.py:94
  520.3 16.0 %collective-permute-start.50 = (bf16[128,1024]{1,0:T(8,128)(2,1)S(1)}, bf16[128,1024]{1,0:T(8,128)(2,1)S(1)}, u32[]{:S(2)}, u32[]{:S(2)}) collective-permute-start(bf16[128,1024]{1,0:T(8,128)(2,1)S(1)} %get-tuple-element.303), channel_id=1, source_target_pairs={{0,8},{1,9},{2,10},{3,11},{4,12},{5,13},{6,14},{7,15},{8,0},{9,1},... | collective-permute-start | bytes 786440 | tf_op jit(solution)/shard_map/ppermute | solution.py:94
  550.0 35.6 %collective-permute-start.69 = (bf16[304,768]{1,0:T(8,128)(2,1)S(1)}, bf16[304,768]{1,0:T(8,128)(2,1)S(1)}, u32[]{:S(2)}, u32[]{:S(2)}) collective-permute-start(bf16[304,768]{1,0:T(8,128)(2,1)S(1)} %fusion.39), channel_id=1, source_target_pairs={{0,4},{1,5},{2,6},{3,7},{4,0},{5,1},{6,2},{7,3},{8,12},{9,13},{10,... | collective-permute-start | bytes 1400840 | tf_op jit(solution)/shard_map/ppermute | solution.py:94
  551.6 47.1 %collective-permute-start.70 = (bf16[304,768]{1,0:T(8,128)(2,1)S(1)}, bf16[304,768]{1,0:T(8,128)(2,1)}, u32[]{:S(2)}, u32[]{:S(2)}) collective-permute-start(bf16[304,768]{1,0:T(8,128)(2,1)S(1)} %fusion.40), channel_id=1, source_target_pairs={{0,4},{4,0},{10,14},{14,10},{16,20},{20,16},{26,30},{30,26}} | collective-permute-start | bytes 1400840 | tf_op jit(solution)/shard_map/ppermute | solution.py:94
  554.2 28.4 %collective-permute-start.52 = (bf16[256,1024]{1,0:T(8,128)(2,1)S(1)}, bf16[256,1024]{1,0:T(8,128)(2,1)S(1)}, u32[]{:S(2)}, u32[]{:S(2)}) collective-permute-start(bf16[256,1024]{1,0:T(8,128)(2,1)S(1)} %get-tuple-element.309), channel_id=1, source_target_pairs={{0,8},{1,9},{2,10},{3,11},{4,12},{5,13},{6,14},{7,15},{8,0},{9,1},... | collective-permute-start | bytes 1572872 | tf_op jit(solution)/shard_map/ppermute | solution.py:94
  554.3 28.4 %collective-permute-start.53 = (bf16[256,1024]{1,0:T(8,128)(2,1)S(1)}, bf16[256,1024]{1,0:T(8,128)(2,1)S(1)}, u32[]{:S(2)}, u32[]{:S(2)}) collective-permute-start(bf16[256,1024]{1,0:T(8,128)(2,1)S(1)} %get-tuple-element.311), channel_id=1, source_target_pairs={{0,2},{1,3},{2,0},{3,1},{4,6},{5,7},{6,4},{7,5},{8,10},{9,11},{10,... | collective-permute-start | bytes 1572872 | tf_op jit(solution)/shard_map/ppermute | solution.py:94
  570.0 71.7 %collective-permute-start.65 = (bf16[576,1024]{1,0:T(8,128)(2,1)}, bf16[576,1024]{1,0:T(8,128)(2,1)}, u32[]{:S(2)}, u32[]{:S(2)}) collective-permute-start(bf16[576,1024]{1,0:T(8,128)(2,1)} %pad_maximum_fusion.2), channel_id=1, source_target_pairs={{0,4},{1,5},{2,6},{3,7},{4,0},{5,1},{6,2},{7,3},{8,12},{9,13},{10,... | collective-permute-start | bytes 3538952 | tf_op jit(solution)/shard_map/ppermute | solution.py:94
  588.0 18.2 %collective-permute-start.64 = (bf16[288,512]{1,0:T(8,128)(2,1)}, bf16[288,512]{1,0:T(8,128)(2,1)S(1)}, u32[]{:S(2)}, u32[]{:S(2)}) collective-permute-start(bf16[288,512]{1,0:T(8,128)(2,1)} %slice.275), channel_id=1, source_target_pairs={{0,16},{4,20},{10,26},{14,30},{16,0},{20,4},{26,10},{30,14}} | collective-permute-start | bytes 884744 | tf_op jit(solution)/shard_map/ppermute | solution.py:94
  592.2 20.2 %collective-permute-start.63 = (bf16[288,512]{1,0:T(8,128)(2,1)}, bf16[288,512]{1,0:T(8,128)(2,1)}, u32[]{:S(2)}, u32[]{:S(2)}) collective-permute-start(bf16[288,512]{1,0:T(8,128)(2,1)} %slice.273), channel_id=1, source_target_pairs={{0,16},{1,17},{2,18},{3,19},{4,20},{5,21},{6,22},{7,23},{8,24},{9,... | collective-permute-start | bytes 884744 | tf_op jit(solution)/shard_map/ppermute | solution.py:94
  595.1 76.8 %all-to-all-start.4 = ((bf16[8,64,1536]{2,1,0:T(8,128)(2,1)}), bf16[8,64,1536]{2,1,0:T(8,128)(2,1)S(1)}, u32[]{:S(2)}, u32[]{:S(2)}) async-start(bf16[8,64,1536]{2,1,0:T(8,128)(2,1)} %bitcast.97), calls=%async_computation.6 | async-start | bytes 3145728 | tf_op jit(solution)/shard_map/all_to_all | solution.py:795
  599.9 26.9 %collective-permute-start.71 = (bf16[304,768]{1,0:T(8,128)(2,1)}, bf16[304,768]{1,0:T(8,128)(2,1)S(1)}, u32[]{:S(2)}, u32[]{:S(2)}) collective-permute-start(bf16[304,768]{1,0:T(8,128)(2,1)} %add_convert_fusion.14), channel_id=1, source_target_pairs={{0,16},{1,17},{2,18},{3,19},{4,20},{5,21},{6,22},{7,23},{8,24},{9,... | collective-permute-start | bytes 1400840 | tf_op jit(solution)/shard_map/ppermute | solution.py:94
  603.7 30.5 %collective-permute-start.72 = (bf16[304,768]{1,0:T(8,128)(2,1)S(1)}, bf16[304,768]{1,0:T(8,128)(2,1)S(1)}, u32[]{:S(2)}, u32[]{:S(2)}) collective-permute-start(bf16[304,768]{1,0:T(8,128)(2,1)S(1)} %add_convert_fusion.13), channel_id=1, source_target_pairs={{0,16},{4,20},{10,26},{14,30},{16,0},{20,4},{26,10},{30,14}} | collective-permute-start | bytes 1400840 | tf_op jit(solution)/shard_map/ppermute | solution.py:94
  606.2 37.5 %collective-permute-start.67 = (bf16[576,1024]{1,0:T(8,128)(2,1)S(1)}, bf16[576,1024]{1,0:T(8,128)(2,1)S(1)}, u32[]{:S(2)}, u32[]{:S(2)}) collective-permute-start(bf16[576,1024]{1,0:T(8,128)(2,1)S(1)} %slice.287), channel_id=1, source_target_pairs={{0,4},{4,0},{10,14},{14,10},{16,20},{20,16},{26,30},{30,26}} | collective-permute-start | bytes 3538952 | tf_op jit(solution)/shard_map/ppermute | solution.py:94
  634.3 21.3 %collective-permute-start.74 = (bf16[304,768]{1,0:T(8,128)(2,1)S(1)}, bf16[304,768]{1,0:T(8,128)(2,1)S(1)}, u32[]{:S(2)}, u32[]{:S(2)}) collective-permute-start(bf16[304,768]{1,0:T(8,128)(2,1)S(1)} %add_convert_fusion.12), channel_id=1, source_target_pairs={{0,8},{1,9},{2,10},{3,11},{4,12},{5,13},{6,14},{7,15},{8,0},{9,1},... | collective-permute-start | bytes 1400840 | tf_op jit(solution)/shard_map/ppermute | solution.py:94
  634.3 22.8 %collective-permute-start.73 = (bf16[304,768]{1,0:T(8,128)(2,1)S(1)}, bf16[304,768]{1,0:T(8,128)(2,1)S(1)}, u32[]{:S(2)}, u32[]{:S(2)}) collective-permute-start(bf16[304,768]{1,0:T(8,128)(2,1)S(1)} %add_convert_fusion.12), channel_id=1, source_target_pairs={{0,2},{1,3},{2,0},{3,1},{4,6},{5,7},{6,4},{7,5},{8,10},{9,11},{10,... | collective-permute-start | bytes 1400840 | tf_op jit(solution)/shard_map/ppermute | solution.py:94
  639.8 16.5 %collective-permute-start.78 = (bf16[304,768]{1,0:T(8,128)(2,1)S(1)}, bf16[304,768]{1,0:T(8,128)(2,1)S(1)}, u32[]{:S(2)}, u32[]{:S(2)}) collective-permute-start(bf16[304,768]{1,0:T(8,128)(2,1)S(1)} %add_convert_fusion.11), channel_id=1, source_target_pairs={{0,2},{4,6},{10,8},{14,12},{16,18},{20,22},{26,24},{30,28}} | collective-permute-start | bytes 1400840 | tf_op jit(solution)/shard_map/ppermute | solution.py:94
  643.6 20.6 %collective-permute-start.66 = (bf16[576,512]{1,0:T(8,128)(2,1)S(1)}, bf16[576,512]{1,0:T(8,128)(2,1)S(1)}, u32[]{:S(2)}, u32[]{:S(2)}) collective-permute-start(bf16[576,512]{1,0:T(8,128)(2,1)S(1)} %slice.324), channel_id=1, source_target_pairs={{0,16},{1,17},{2,18},{3,19},{4,20},{5,21},{6,22},{7,23},{8,24},{9,... | collective-permute-start | bytes 1769480 | tf_op jit(solution)/shard_map/ppermute | solution.py:94
  644.3 27.3 %collective-permute-start.68 = (bf16[576,512]{1,0:T(8,128)(2,1)S(1)}, bf16[576,512]{1,0:T(8,128)(2,1)S(1)}, u32[]{:S(2)}, u32[]{:S(2)}) collective-permute-start(bf16[576,512]{1,0:T(8,128)(2,1)S(1)} %slice.328), channel_id=1, source_target_pairs={{0,16},{4,20},{10,26},{14,30},{16,0},{20,4},{26,10},{30,14}} | collective-permute-start | bytes 1769480 | tf_op jit(solution)/shard_map/ppermute | solution.py:94
  655.5 41.3 %collective-permute-start.59 = (f32[16,256]{1,0:T(8,128)S(1)}, f32[16,256]{1,0:T(8,128)S(1)}, u32[]{:S(2)}, u32[]{:S(2)}) collective-permute-start(f32[16,256]{1,0:T(8,128)S(1)} %add.168), channel_id=1, source_target_pairs={{0,10},{1,11},{2,8},{3,9},{4,14},{5,15},{6,12},{7,13},{8,2},{9,3},... | collective-permute-start | bytes 49160 | tf_op jit(solution)/shard_map/ppermute | solution.py:94
  656.3 40.6 %collective-permute-start.58 = (f32[16,256]{1,0:T(8,128)S(1)}, f32[16,256]{1,0:T(8,128)S(1)}, u32[]{:S(2)}, u32[]{:S(2)}) collective-permute-start(f32[16,256]{1,0:T(8,128)S(1)} %add.168), channel_id=1, source_target_pairs={{0,8},{1,9},{2,10},{3,11},{4,12},{5,13},{6,14},{7,15},{8,0},{9,1},... | collective-permute-start | bytes 49160 | tf_op jit(solution)/shard_map/ppermute | solution.py:94
  657.1 31.0 %collective-permute-start.79 = (bf16[304,768]{1,0:T(8,128)(2,1)}, bf16[304,768]{1,0:T(8,128)(2,1)}, u32[]{:S(2)}, u32[]{:S(2)}) collective-permute-start(bf16[304,768]{1,0:T(8,128)(2,1)} %select_select_fusion), channel_id=1, source_target_pairs={{0,8},{1,9},{2,10},{3,11},{4,12},{5,13},{6,14},{7,15},{8,0},{9,1},... | collective-permute-start | bytes 1400840 | tf_op jit(solution)/shard_map/ppermute | solution.py:94
  664.2 15.9 %collective-permute-start.75 = (bf16[144,768]{1,0:T(8,128)(2,1)}, bf16[144,768]{1,0:T(8,128)(2,1)}, u32[]{:S(2)}, u32[]{:S(2)}) collective-permute-start(bf16[144,768]{1,0:T(8,128)(2,1)} %slice.335), channel_id=1, source_target_pairs={{0,2},{1,3},{2,0},{3,1},{4,6},{5,7},{6,4},{7,5},{8,10},{9,11},{10,... | collective-permute-start | bytes 663560 | tf_op jit(solution)/shard_map/ppermute | solution.py:94
  671.5 14.9 %collective-permute-start.76 = (bf16[160,768]{1,0:T(8,128)(2,1)}, bf16[160,768]{1,0:T(8,128)(2,1)}, u32[]{:S(2)}, u32[]{:S(2)}) collective-permute-start(bf16[160,768]{1,0:T(8,128)(2,1)} %slice.336), channel_id=1, source_target_pairs={{0,8},{1,9},{2,10},{3,11},{4,12},{5,13},{6,14},{7,15},{8,0},{9,1},... | collective-permute-start | bytes 737288 | tf_op jit(solution)/shard_map/ppermute | solution.py:94
  672.9 20.4 %all-to-all-start.6 = ((bf16[8,64,640]{2,1,0:T(8,128)(2,1)}), bf16[8,64,640]{2,1,0:T(8,128)(2,1)S(1)}, u32[]{:S(2)}, u32[]{:S(2)}) async-start(bf16[8,64,640]{2,1,0:T(8,128)(2,1)} %shard_map.338), calls=%async_computation.8 | async-start | bytes 1310720 | tf_op jit(solution)/shard_map/all_to_all | solution.py:795
  680.1 16.8 %collective-permute-start.57 = (f32[16,256]{1,0:T(8,128)S(1)}, f32[16,256]{1,0:T(8,128)S(1)}, u32[]{:S(2)}, u32[]{:S(2)}) collective-permute-start(f32[16,256]{1,0:T(8,128)S(1)} %add.168), channel_id=1, source_target_pairs={{0,2},{1,3},{2,0},{3,1},{4,6},{5,7},{6,4},{7,5},{8,10},{9,11},{10,... | collective-permute-start | bytes 49160 | tf_op jit(solution)/shard_map/ppermute | solution.py:94
  688.1 24.6 %collective-permute-start.77 = (bf16[1216,768]{1,0:T(8,128)(2,1)}, bf16[1216,768]{1,0:T(8,128)(2,1)}, u32[]{:S(2)}, u32[]{:S(2)}) collective-permute-start(bf16[1216,768]{1,0:T(8,128)(2,1)} %constant_dynamic-update-slice_fusion.21), channel_id=1, source_target_pairs={{0,1},{1,0},{2,3},{3,2},{4,5},{5,4},{6,7},{7,6},{8,9},{9,8},{10,11... | collective-permute-start | bytes 5603336 | tf_op jit(solution)/shard_map/ppermute | solution.py:94
  690.5 22.0 %collective-permute-start.80 = (bf16[2,304,768]{2,1,0:T(8,128)(2,1)}, bf16[2,304,768]{2,1,0:T(8,128)(2,1)}, u32[]{:S(2)}, u32[]{:S(2)}) collective-permute-start(bf16[2,304,768]{2,1,0:T(8,128)(2,1)} %pad_maximum_fusion.3), channel_id=1, source_target_pairs={{0,1},{1,0},{2,3},{3,2},{4,5},{5,4},{6,7},{7,6},{8,9},{9,8},{10,11... | collective-permute-start | bytes 2801672 | tf_op jit(solution)/shard_map/ppermute | solution.py:94
  693.3 30.7 %all-to-all-start.5 = ((bf16[8,64,1152]{2,1,0:T(8,128)(2,1)}), bf16[8,64,1152]{2,1,0:T(8,128)(2,1)S(1)}, u32[]{:S(2)}, u32[]{:S(2)}) async-start(bf16[8,64,1152]{2,1,0:T(8,128)(2,1)} %shard_map.335), calls=%async_computation.7 | async-start | bytes 2359296 | tf_op jit(solution)/shard_map/all_to_all | solution.py:795
  (160 other events, 1288.5 us)
Sparse Core Ops, SparseCore 0:
  147.9 121.5 all-gather.2
  271.4 69.1 all-gather.4
  382.5 69.3 reduce-scatter.2
  454.7 120.5 reduce-scatter.4
